TPU v7x, 32 devices: a whole 2x2x4 slice. The times are simulated.
32 devices in a mesh: tile: 8 (over z, y), band: 4 (over x, core).
Axes of the slice: x: 2, y: 2, z: 4, core: 2. Of those that a mesh axis runs over, the one named last changes fastest.
Arguments:
- points: float32 [8192, 3, 128], P(('tile', 'band')), may hold values from -6 to 6
- normals: float32 [8192, 3, 128], P(('tile', 'band')), may hold values from -4 to 4
- poses: float32 [6, 256], P(None, ('tile', 'band')), may hold values from -4 to 4
- directions: float32 [2, 6, 256], P(None, None, ('tile', 'band')), may hold values from -6 to 6
- local_pairs: int32 [2, 8192], P(None, ('tile', 'band')), may hold values from 0 to 255
- local_maps: int32 [8192, 128], P(('tile', 'band')), may hold values from 0 to 127
- remote_src: int32 [32, 256], P(('tile', 'band')), may hold values from 0 to 255
- remote_maps: int32 [32, 256, 128], P(('tile', 'band')), may hold values from 0 to 127
- remote_dst: int32 [32, 256], P(('tile', 'band')), may hold values from 0 to 255
- counts: int32 [32, 32], P(('tile', 'band')), may hold values from 4 to 8, as said below
Outputs:
- gradient: float32 [6, 256], P(None, ('tile', 'band'))
- hess_products: float32 [2, 6, 256], P(None, None, ('tile', 'band'))
Inputs may be any that keep to these rules, and one draw needn't show every extreme that they name: `counts`: in every row some device pair uses all 8 slots.
All inputs are finite; a program needn't handle non-finite values.
Results may differ from a plain program's by a relative error of at most 0.0003.
Values sent between devices are 32-bit elements; how exact they have to be, the bound alone decides.
No kernel may reach another device: no remote copies, remote signals or barrier semaphores. Data moves between devices by JAX's collectives and lax.ppermute only.
A program may use at most 64 MiB of HBM per device.

v0:
```python
import math

import jax
import jax.numpy as jnp
from jax import lax
from jax.sharding import PartitionSpec as P

BF = 32


def rotations(poses):
    half_angle = poses[0:3] * 0.5
    inverse = 1.0 / jnp.sqrt(
        1.0
        + half_angle[0] * half_angle[0]
        + half_angle[1] * half_angle[1]
        + half_angle[2] * half_angle[2]
    )
    quat_x = half_angle[0] * inverse
    quat_y = half_angle[1] * inverse
    quat_z = half_angle[2] * inverse
    rotation = [
        [
            1.0 - 2.0 * (quat_y * quat_y + quat_z * quat_z),
            2.0 * (quat_x * quat_y - inverse * quat_z),
            2.0 * (quat_x * quat_z + inverse * quat_y),
        ],
        [
            2.0 * (quat_x * quat_y + inverse * quat_z),
            1.0 - 2.0 * (quat_x * quat_x + quat_z * quat_z),
            2.0 * (quat_y * quat_z - inverse * quat_x),
        ],
        [
            2.0 * (quat_x * quat_z - inverse * quat_y),
            2.0 * (quat_y * quat_z + inverse * quat_x),
            1.0 - 2.0 * (quat_x * quat_x + quat_y * quat_y),
        ],
    ]
    return (rotation, poses[3:6])


def to_world(points, normals, poses, per_pose):
    rotation, translation = rotations(poses)

    def spread(values):
        return jnp.repeat(values, per_pose)[:, None]

    world_rows = []
    normal_rows = []
    for i in range(3):
        coeffs = [spread(rotation[i][j]) for j in range(3)]
        world_rows.append(
            coeffs[0] * points[:, 0]
            + coeffs[1] * points[:, 1]
            + coeffs[2] * points[:, 2]
            + spread(translation[i])
        )
        normal_rows.append(
            coeffs[0] * normals[:, 0] + coeffs[1] * normals[:, 1] + coeffs[2] * normals[:, 2]
        )
    return (jnp.stack(world_rows, axis=1), jnp.stack(normal_rows, axis=1))


def cross_rows(left, right):
    return [
        left[:, 1] * right[:, 2] - left[:, 2] * right[:, 1],
        left[:, 2] * right[:, 0] - left[:, 0] * right[:, 2],
        left[:, 0] * right[:, 1] - left[:, 1] * right[:, 0],
    ]


def pick_points(world_pts, normal_pts, point_maps):
    stacked = jnp.concatenate([world_pts, normal_pts], axis=1)
    pair_count = stacked.shape[0]
    point_count = stacked.shape[2]
    per_step = math.gcd(pair_count, 64)
    positions = jnp.arange(point_count, dtype=jnp.int32)

    def select_block(operands):
        values, indices = operands
        selector = (indices[:, :, None] == positions[None, None, :]).astype(jnp.float32)
        return jnp.einsum("gcm,gkm->gck", values, selector, precision=lax.Precision.HIGHEST)

    picked = lax.map(
        select_block,
        (
            stacked.reshape(pair_count // per_step, per_step, 6, point_count),
            point_maps.reshape(pair_count // per_step, per_step, point_count),
        ),
    )
    picked = picked.reshape(pair_count, 6, point_count)
    return (picked[:, 0:3], picked[:, 3:6])


def pair_terms(world_a, world_b, normal_b, dirs_a, dirs_b, valid_mask, blocks_frag):
    count = world_a.shape[2]
    offset = world_a - world_b
    residual = (
        normal_b[:, 0] * offset[:, 0]
        + normal_b[:, 1] * offset[:, 1]
        + normal_b[:, 2] * offset[:, 2]
    ) * valid_mask[:, None]
    normal_list = [normal_b[:, 0], normal_b[:, 1], normal_b[:, 2]]
    jac_a = jnp.stack(cross_rows(world_a, normal_b) + normal_list, axis=1)
    jac_b = -jnp.stack(cross_rows(world_b, normal_b) + normal_list, axis=1)
    grad_scale = 1.0 / count
    hess_scale = 1.0 / (count * blocks_frag)
    parts_a = [jnp.sum(residual[:, None] * jac_a, axis=2) * grad_scale]
    parts_b = [jnp.sum(residual[:, None] * jac_b, axis=2) * grad_scale]
    for v in range(2):
        along_dir = (
            jnp.sum(jac_a * dirs_a[:, 6 * v : 6 * v + 6, None], axis=1)
            + jnp.sum(jac_b * dirs_b[:, 6 * v : 6 * v + 6, None], axis=1)
        ) * valid_mask[:, None]
        parts_a.append(jnp.sum(along_dir[:, None] * jac_a, axis=2) * hess_scale)
        parts_b.append(jnp.sum(along_dir[:, None] * jac_b, axis=2) * hess_scale)
    return (jnp.concatenate(parts_a, axis=1), jnp.concatenate(parts_b, axis=1))


def frag_sums(blocks, terms, frag_count):
    onehot = (blocks[:, None] // BF == jnp.arange(frag_count, dtype=jnp.int32)[None, :]).astype(
        jnp.float32
    )
    return jnp.dot(onehot.T, terms, precision=lax.Precision.HIGHEST)


def local(
    points,
    normals,
    poses,
    directions,
    local_pairs,
    local_maps,
    remote_src,
    remote_maps,
    remote_dst,
    counts,
):
    n_tile = lax.axis_size("tile")
    n_band = lax.axis_size("band")
    devices = n_tile * n_band
    frag_count = poses.shape[1]
    world_pts, normal_pts = to_world(points, normals, poses, BF)
    frag_dirs = directions.reshape(12, frag_count).T
    send_blocks = remote_dst[0]
    send_frags = send_blocks // BF
    cargo_rows = jnp.concatenate([world_pts[send_blocks], normal_pts[send_blocks]], axis=1)
    extras = frag_dirs[send_frags]
    slot_count = cargo_rows.shape[0]
    per_peer = slot_count // devices
    arrived_rows, arrived_extra = (
        lax.all_to_all(cargo_rows, ("tile", "band"), split_axis=0, concat_axis=0, tiled=True),
        lax.all_to_all(extras, ("tile", "band"), split_axis=0, concat_axis=0, tiled=True),
    )
    peer_world = arrived_rows[:, 0:3]
    peer_normal = arrived_rows[:, 3:6]
    world_b, normal_b = pick_points(
        world_pts[local_pairs[1]], normal_pts[local_pairs[1]], local_maps
    )
    local_ones = jnp.ones((local_pairs.shape[1],), jnp.float32)
    local_a, local_b = pair_terms(
        world_pts[local_pairs[0]],
        world_b,
        normal_b,
        frag_dirs[local_pairs[0] // BF],
        frag_dirs[local_pairs[1] // BF],
        local_ones,
        BF,
    )
    source_blocks = remote_src[0]
    used_slots = counts[0]
    valid_mask = (
        (jnp.arange(per_peer, dtype=jnp.int32)[None, :] < used_slots[:, None])
        .astype(jnp.float32)
        .reshape(-1)
    )
    world_b, normal_b = pick_points(peer_world, peer_normal, remote_maps[0])
    remote_a, remote_b = pair_terms(
        world_pts[source_blocks],
        world_b,
        normal_b,
        frag_dirs[source_blocks // BF],
        arrived_extra,
        valid_mask,
        BF,
    )
    returned = lax.all_to_all(remote_b, ("tile", "band"), split_axis=0, concat_axis=0, tiled=True)
    totals = frag_sums(local_pairs[0], local_a, frag_count) + frag_sums(
        local_pairs[1], local_b, frag_count
    )
    totals = (
        totals
        + frag_sums(source_blocks, remote_a, frag_count)
        + frag_sums(send_blocks, returned, frag_count)
    )
    gradient = totals[:, 0:6].T
    hess_products = totals[:, 6:18].T.reshape(2, 6, frag_count)
    return (gradient, hess_products)


def solution(mesh):
    placed = (
        P(("tile", "band"), None, None),
        P(("tile", "band"), None, None),
        P(None, ("tile", "band")),
        P(None, None, ("tile", "band")),
        P(None, ("tile", "band")),
        P(("tile", "band"), None),
        P(("tile", "band"), None),
        P(("tile", "band"), None, None),
        P(("tile", "band"), None),
        P(("tile", "band"), None),
    )
    return jax.shard_map(
        local,
        mesh=mesh,
        in_specs=placed,
        out_specs=(P(None, ("tile", "band")), P(None, None, ("tile", "band"))),
        check_vma=False,
    )
```

profile of v0, /device:TPU:0, one launch (start us, length us, event | category | flops | bytes accessed | tf_op | source)
XLA Modules:
  0.0 143.8 jit_solution(8584446051925342498)
XLA Ops:
  0.7 0.7 compare_select_fusion
  1.4 0.8 copy.122
  2.3 1.3 gather_fusion.9
  3.6 7.4 %all-to-all-start.1 = ((f32[32,8,12]{2,1,0:T(8,128)}), f32[32,8,12]{2,1,0:T(8,128)}, u32[]{:S(2)}, u32[]{:S(2)}) async-start(f32[32,8,12]{2,1,0:T(8,128)} %bitcast.31), calls=%async_computation.1 | async-start | bytes 262144 | tf_op jit(solution)/shard_map/all_to_all | solution.py:153
  15.9 1.0 gather_fusion.6
  16.9 1.8 %gather_fusion.5 = f32[256,3,128]{2,1,0:T(4,128)} fusion(f32[256,3,128]{2,1,0:T(4,128)S(1)} %copy.118, s32[1024]{0:T(1024)S(1)} %pad_clamp_fusion.3), kind=kCustom, calls=%fused_computation.5 | custom fusion | bytes 787456 | tf_op jit(solution)/shard_map/gather | solution.py:147
  18.7 1.0 gather_fusion.1
  19.7 1.0 gather_fusion
  21.0 22.0 %while.22 = (s32[]{:T(128)}, f32[4,64,6,128]{3,2,1,0:T(8,128)S(1)}, f32[4,64,6,128]{3,2,1,0:T(8,128)S(1)}, s32[4,64,128]{2,1,0:T(8,128)}, s32[]{:T(128)}) while((s32[]{:T(128)}, f32[4,64,6,128]{3,2,1,0:T(8,128)S(1)}, f32[4,64,6,128]{3,2,1,0:T(8,128)S(1)}, s32[4,64,128]{2,1,0:T(8,128)}, s32[]{:T(128)}) %tuple.107), condition=%wide.region_1.2_spmd.clone, body=%wide.region_0.1_spmd.clone.sunk | while | flops 76546048 | bytes 623689 | solution.py:84
  21.0 0.8 dynamic-slice_bitcast_fusion.4
  21.7 4.7 %fusion.75 = f32[4,64,6,128]{3,2,1,0:T(8,128)S(1)} fusion(f32[4,64,6,128]{3,2,1,0:T(8,128)S(1)} %get-tuple-element.257, s32[]{:T(128)S(6)} %copy.150, s32[64,128]{1,0:T(8,128)S(1)} %dynamic-slice_bitcast_fusion.4, f32[4,64,6,128]{3,2,1,0:T(8,128)S(1)} %get-tuple-element.263), kind=kOutput, calls=%fused_computation.16.clone.1 | convolution fusion | flops 76546048 | bytes 558080 | tf_op jit(solution)/shard_map/while/body/eval_jaxpr/gcm,gkm->gck/dot_general | solution.py:82
  26.5 0.8 dynamic-slice_bitcast_fusion.4
  27.3 4.7 %fusion.75 = f32[4,64,6,128]{3,2,1,0:T(8,128)S(1)} fusion(f32[4,64,6,128]{3,2,1,0:T(8,128)S(1)} %get-tuple-element.257, s32[]{:T(128)S(6)} %copy.150, s32[64,128]{1,0:T(8,128)S(1)} %dynamic-slice_bitcast_fusion.4, f32[4,64,6,128]{3,2,1,0:T(8,128)S(1)} %get-tuple-element.263), kind=kOutput, calls=%fused_computation.16.clone.1 | convolution fusion | flops 76546048 | bytes 558080 | tf_op jit(solution)/shard_map/while/body/eval_jaxpr/gcm,gkm->gck/dot_general | solution.py:82
  32.0 0.8 dynamic-slice_bitcast_fusion.4
  32.8 4.7 %fusion.75 = f32[4,64,6,128]{3,2,1,0:T(8,128)S(1)} fusion(f32[4,64,6,128]{3,2,1,0:T(8,128)S(1)} %get-tuple-element.257, s32[]{:T(128)S(6)} %copy.150, s32[64,128]{1,0:T(8,128)S(1)} %dynamic-slice_bitcast_fusion.4, f32[4,64,6,128]{3,2,1,0:T(8,128)S(1)} %get-tuple-element.263), kind=kOutput, calls=%fused_computation.16.clone.1 | convolution fusion | flops 76546048 | bytes 558080 | tf_op jit(solution)/shard_map/while/body/eval_jaxpr/gcm,gkm->gck/dot_general | solution.py:82
  37.5 0.8 dynamic-slice_bitcast_fusion.4
  38.3 4.7 %fusion.75 = f32[4,64,6,128]{3,2,1,0:T(8,128)S(1)} fusion(f32[4,64,6,128]{3,2,1,0:T(8,128)S(1)} %get-tuple-element.257, s32[]{:T(128)S(6)} %copy.150, s32[64,128]{1,0:T(8,128)S(1)} %dynamic-slice_bitcast_fusion.4, f32[4,64,6,128]{3,2,1,0:T(8,128)S(1)} %get-tuple-element.263), kind=kOutput, calls=%fused_computation.16.clone.1 | convolution fusion | flops 76546048 | bytes 558080 | tf_op jit(solution)/shard_map/while/body/eval_jaxpr/gcm,gkm->gck/dot_general | solution.py:82
  43.0 1.0 gather_fusion.2
  44.3 1.8 %multiply_subtract_fusion.11 = (f32[256,1,128]{2,1,0:T(1,128)}, f32[256,1,128]{2,1,0:T(1,128)}, f32[256,1,128]{2,1,0:T(1,128)}) fusion(f32[256,3,128]{2,1,0:T(4,128)S(1)} %gather_fusion.2, f32[256,6,128]{2,1,0:T(8,128)S(1)} %bitcast.201), kind=kLoop, calls=%fused_computation.94 | loop fusion | flops 294912 | bytes 1179648 | tf_op jit(solution)/shard_map/sub | solution.py:66
  47.4 1.0 multiply_subtract_fusion.8
  48.4 0.7 gather_fusion.4
  49.2 0.7 gather_fusion.3
  50.2 4.6 %multiply_reduce_fusion.19 = (f32[256,6]{1,0:T(8,128)S(1)}, f32[256,128]{1,0:T(8,128)S(1)}, f32[256,128]{1,0:T(8,128)S(1)}, f32[256,128]{1,0:T(8,128)S(1)}) fusion(f32[256,128]{1,0:T(8,128)S(1)} %bitcast.205, f32[256,3,128]{2,1,0:T(4,128)S(1)} %get-tuple-element.138, f32[256,1,128]{2,1,0:T(1,128)S(1)} %copy-done.3, f32[256,1,128]{2,1,0:T(1,128)S(1)} %copy-done.4, ...), kind=kLoop, calls=%fused_computation.60 | loop fusion | flops 2849280 | bytes 1728512 | tf_op jit(solution)/shard_map/reduce_sum | solution.py:108
  54.8 2.1 %multiply_reduce_fusion.12 = (f32[256,6]{1,0:T(8,128)}, f32[256,128]{1,0:T(8,128)S(1)}, f32[256,6]{1,0:T(8,128)}) fusion(f32[256,128]{1,0:T(8,128)S(1)} %bitcast.206, f32[256,3,128]{2,1,0:T(4,128)S(1)} %get-tuple-element.138, f32[256,1,128]{2,1,0:T(1,128)S(1)} %get-tuple-element.136, f32[256,1,128]{2,1,0:T(1,128)S(1)} %get-tuple-element.135, ...), kind=kLoop, calls=%fused_computation.53 | loop fusion | flops 1930240 | bytes 1198080 | tf_op jit(solution)/shard_map/reduce_sum | solution.py:109
  56.9 2.1 %multiply_reduce_fusion.16 = (f32[256,6]{1,0:T(8,128)S(1)}, f32[256,6]{1,0:T(8,128)S(1)}, f32[256,6]{1,0:T(8,128)}) fusion(f32[256,128]{1,0:T(8,128)S(1)} %add.337, f32[256,3,128]{2,1,0:T(4,128)S(1)} %get-tuple-element.138, f32[256,1,128]{2,1,0:T(1,128)S(1)} %copy-done.3, f32[256,1,128]{2,1,0:T(1,128)S(1)} %copy-done.4, f32[256,1,128]{2,1,0:T(1,128)S(1)} %copy-done.2, ...), kind=kLoop, calls=%fused_computation.57 | loop fusion | flops 2551296 | bytes 1460224 | tf_op jit(solution)/shard_map/reduce_sum | solution.py:115
  60.1 1.2 pad_maximum_fusion.5
  61.7 1.0 gather_fusion.7
  62.7 0.7 gather_fusion.8
  63.7 5.8 %all-to-all-start = ((f32[256,6,128]{2,1,0:T(8,128)}), f32[256,6,128]{2,1,0:T(8,128)S(1)}, u32[]{:S(2)}, u32[]{:S(2)}) async-start(f32[256,6,128]{2,1,0:T(8,128)} %pad_maximum_fusion.5), calls=%async_computation | async-start | bytes 2097152 | tf_op jit(solution)/shard_map/all_to_all | solution.py:152
  69.9 1.1 fusion.67
  71.0 24.7 %all-to-all-done = f32[256,6,128]{2,1,0:T(8,128)S(1)} async-done(((f32[256,6,128]{2,1,0:T(8,128)}), f32[256,6,128]{2,1,0:T(8,128)S(1)}, u32[]{:S(2)}, u32[]{:S(2)}) %all-to-all-start) | async-done | bytes 786464 | tf_op jit(solution)/shard_map/all_to_all | solution.py:152
  95.8 22.0 %while.23 = (s32[]{:T(128)}, f32[4,64,6,128]{3,2,1,0:T(8,128)S(1)}, f32[4,64,6,128]{3,2,1,0:T(8,128)S(1)}, s32[4,64,128]{2,1,0:T(8,128)}, s32[]{:T(128)}) while((s32[]{:T(128)}, f32[4,64,6,128]{3,2,1,0:T(8,128)S(1)}, f32[4,64,6,128]{3,2,1,0:T(8,128)S(1)}, s32[4,64,128]{2,1,0:T(8,128)}, s32[]{:T(128)}) %tuple.108), condition=%wide.region_13.14_spmd.clone, body=%wide.region_12.13_spmd.clone.sunk | while | flops 76546048 | bytes 623689 | solution.py:84
  95.8 0.8 dynamic-slice_bitcast_fusion.5
  96.5 4.7 %fusion.77 = f32[4,64,6,128]{3,2,1,0:T(8,128)S(1)} fusion(f32[4,64,6,128]{3,2,1,0:T(8,128)S(1)} %get-tuple-element.242, s32[]{:T(128)S(6)} %copy.144, s32[64,128]{1,0:T(8,128)S(1)} %dynamic-slice_bitcast_fusion.5, f32[4,64,6,128]{3,2,1,0:T(8,128)S(1)} %get-tuple-element.248), kind=kOutput, calls=%fused_computation.25.clone.1 | convolution fusion | flops 76546048 | bytes 558080 | tf_op jit(solution)/shard_map/while/body/eval_jaxpr/gcm,gkm->gck/dot_general | solution.py:82
  101.3 0.8 dynamic-slice_bitcast_fusion.5
  102.1 4.7 %fusion.77 = f32[4,64,6,128]{3,2,1,0:T(8,128)S(1)} fusion(f32[4,64,6,128]{3,2,1,0:T(8,128)S(1)} %get-tuple-element.242, s32[]{:T(128)S(6)} %copy.144, s32[64,128]{1,0:T(8,128)S(1)} %dynamic-slice_bitcast_fusion.5, f32[4,64,6,128]{3,2,1,0:T(8,128)S(1)} %get-tuple-element.248), kind=kOutput, calls=%fused_computation.25.clone.1 | convolution fusion | flops 76546048 | bytes 558080 | tf_op jit(solution)/shard_map/while/body/eval_jaxpr/gcm,gkm->gck/dot_general | solution.py:82
  106.8 0.8 dynamic-slice_bitcast_fusion.5
  107.6 4.7 %fusion.77 = f32[4,64,6,128]{3,2,1,0:T(8,128)S(1)} fusion(f32[4,64,6,128]{3,2,1,0:T(8,128)S(1)} %get-tuple-element.242, s32[]{:T(128)S(6)} %copy.144, s32[64,128]{1,0:T(8,128)S(1)} %dynamic-slice_bitcast_fusion.5, f32[4,64,6,128]{3,2,1,0:T(8,128)S(1)} %get-tuple-element.248), kind=kOutput, calls=%fused_computation.25.clone.1 | convolution fusion | flops 76546048 | bytes 558080 | tf_op jit(solution)/shard_map/while/body/eval_jaxpr/gcm,gkm->gck/dot_general | solution.py:82
  112.3 0.8 dynamic-slice_bitcast_fusion.5
  113.1 4.7 %fusion.77 = f32[4,64,6,128]{3,2,1,0:T(8,128)S(1)} fusion(f32[4,64,6,128]{3,2,1,0:T(8,128)S(1)} %get-tuple-element.242, s32[]{:T(128)S(6)} %copy.144, s32[64,128]{1,0:T(8,128)S(1)} %dynamic-slice_bitcast_fusion.5, f32[4,64,6,128]{3,2,1,0:T(8,128)S(1)} %get-tuple-element.248), kind=kOutput, calls=%fused_computation.25.clone.1 | convolution fusion | flops 76546048 | bytes 558080 | tf_op jit(solution)/shard_map/while/body/eval_jaxpr/gcm,gkm->gck/dot_general | solution.py:82
  118.7 1.4 %multiply_subtract_fusion.2 = (f32[256,1,128]{2,1,0:T(1,128)S(1)}, f32[256,1,128]{2,1,0:T(1,128)S(1)}, f32[256,1,128]{2,1,0:T(1,128)S(1)}, f32[256,1,128]{2,1,0:T(1,128)S(1)}) fusion(f32[256,6,128]{2,1,0:T(8,128)S(1)} %bitcast.199, f32[256]{0:T(256)S(1)} %reshape.853, f32[256,3,128]{2,1,0:T(4,128)S(1)} %get-tuple-element.145), kind=kLoop, calls=%fused_computation.83 | loop fusion | flops 491520 | bytes 1704960 | tf_op jit(solution)/shard_map/sub | solution.py:66
  120.2 4.4 %multiply_reduce_fusion.9 = (f32[256,6]{1,0:T(8,128)S(1)}, f32[256,128]{1,0:T(8,128)S(1)}, f32[256,128]{1,0:T(8,128)S(1)}, f32[256,128]{1,0:T(8,128)S(1)}) fusion(f32[256,128]{1,0:T(8,128)S(1)} %bitcast.203, f32[256,3,128]{2,1,0:T(4,128)S(1)} %get-tuple-element.144, f32[256,1,128]{2,1,0:T(1,128)S(1)} %get-tuple-element.132, ...), kind=kLoop, calls=%fused_computation.50 | loop fusion | flops 2849280 | bytes 1728512 | tf_op jit(solution)/shard_map/reduce_sum | solution.py:108
  124.7 1.4 %multiply_reduce_fusion.2 = (f32[256,6]{1,0:T(8,128)S(1)}, f32[256,128]{1,0:T(8,128)S(1)}, f32[256,6]{1,0:T(8,128)S(1)}) fusion(f32[256,128]{1,0:T(8,128)S(1)} %bitcast.204, f32[256,3,128]{2,1,0:T(4,128)S(1)} %get-tuple-element.144, f32[256,1,128]{2,1,0:T(1,128)S(1)} %get-tuple-element.142, f32[256,1,128]{2,1,0:T(1,128)S(1)} %get-tuple-element.141, ...), kind=kLoop, calls=%fused_computation.43 | loop fusion | flops 1930240 | bytes 1198080 | tf_op jit(solution)/shard_map/reduce_sum | solution.py:109
  126.3 1.5 %multiply_reduce_fusion.6 = (f32[256,6]{1,0:T(8,128)S(1)}, f32[256,6]{1,0:T(8,128)S(1)}, f32[256,6]{1,0:T(8,128)S(1)}) fusion(f32[256,128]{1,0:T(8,128)S(1)} %add_multiply_fusion.1, f32[256,3,128]{2,1,0:T(4,128)S(1)} %get-tuple-element.144, f32[256,1,128]{2,1,0:T(1,128)S(1)} %get-tuple-element.132, f32[256,1,128]{2,1,0:T(1,128)S(1)} %get-tuple-element.133, ...), kind=kLoop, calls=%fused_computation.47 | loop fusion | flops 2551296 | bytes 1460224 | tf_op jit(solution)/shard_map/reduce_sum | solution.py:115
  128.7 0.8 reshape.934
  129.4 3.6 %all-to-all-start.2 = ((f32[32,1,144]{2,1,0:T(1,128)}), f32[32,1,144]{2,1,0:T(1,128)S(1)}, u32[]{:S(2)}, u32[]{:S(2)}) async-start(f32[32,1,144]{2,1,0:T(1,128)} %reshape.934), calls=%async_computation.2 | async-start | bytes 65536 | tf_op jit(solution)/shard_map/all_to_all | solution.py:187
  133.3 7.0 %all-to-all-done.2 = f32[32,1,144]{2,1,0:T(1,128)S(1)} async-done(((f32[32,1,144]{2,1,0:T(1,128)}), f32[32,1,144]{2,1,0:T(1,128)S(1)}, u32[]{:S(2)}, u32[]{:S(2)}) %all-to-all-start.2) | async-done | bytes 18464 | tf_op jit(solution)/shard_map/all_to_all | solution.py:187
  140.8 0.7 reduce
  (144 shorter events, 14.0 us)
Async XLA Ops:
  0.6 10.4 %copy-start.16 = (f32[6,8]{1,0:T(8,128)S(1)}, f32[6,8]{1,0:T(8,128)}, u32[]{:S(2)}) copy-start(f32[6,8]{1,0:T(8,128)} %param.16) | copy-start | bytes 580
  0.6 10.5 %copy-start.10 = (s32[2,256]{1,0:T(2,128)S(1)}, s32[2,256]{1,0:T(2,128)}, u32[]{:S(2)}) copy-start(s32[2,256]{1,0:T(2,128)} %param.18) | copy-start | bytes 6148
  0.7 13.0 %copy-start.8 = (f32[256,3,128]{2,0,1:T(8,128)S(1)}, f32[256,3,128]{2,0,1:T(8,128)}, u32[]{:S(2)}) copy-start(f32[256,3,128]{2,0,1:T(8,128)} %param.15) | copy-start | bytes 1179652
  3.6 60.1 %all-to-all-start.1 = ((f32[32,8,12]{2,1,0:T(8,128)}), f32[32,8,12]{2,1,0:T(8,128)}, u32[]{:S(2)}, u32[]{:S(2)}) async-start(f32[32,8,12]{2,1,0:T(8,128)} %bitcast.31), calls=%async_computation.1 | async-start | bytes 262144 | tf_op jit(solution)/shard_map/all_to_all | solution.py:153
  14.0 1.0 copy-start.1
  44.3 1.8 %copy-start.18 = (s32[1,32]{1,0:T(1,128)S(1)}, s32[1,32]{1,0:T(1,128)}, u32[]{:S(2)}) copy-start(s32[1,32]{1,0:T(1,128)} %param.23) | copy-start | bytes 388
  44.3 2.5 %copy-start.12 = (s32[1,256]{1,0:T(1,128)S(1)}, s32[1,256]{1,0:T(1,128)}, u32[]{:S(2)}) copy-start(s32[1,256]{1,0:T(1,128)} %param.20) | copy-start | bytes 3076
  44.3 2.5 %copy-start.11 = (s32[1,256]{1,0:T(1,128)S(1)}, s32[1,256]{1,0:T(1,128)}, u32[]{:S(2)}) copy-start(s32[1,256]{1,0:T(1,128)} %param.22) | copy-start | bytes 3076
  46.1 2.3 %copy-start.15 = (s32[256,1]{0,1:T(1,128)S(1)}, s32[256,1]{0,1:T(1,128)}, u32[]{:S(2)}) copy-start(s32[256,1]{0,1:T(1,128)} %get-tuple-element.174) | copy-start | bytes 3076
  47.4 1.8 %copy-start.14 = (s32[256,1]{0,1:T(1,128)S(1)}, s32[256,1]{0,1:T(1,128)}, u32[]{:S(2)}) copy-start(s32[256,1]{0,1:T(1,128)} %get-tuple-element.175) | copy-start | bytes 3076
  49.2 0.9 copy-start.2
  49.2 1.0 copy-start.3
  49.2 1.0 copy-start.4
  56.9 3.1 %copy-start = (f32[256,3,128]{2,1,0:T(4,128)S(1)}, f32[256,3,128]{2,1,0:T(4,128)}, u32[]{:S(2)}) copy-start(f32[256,3,128]{2,1,0:T(4,128)} %gather_fusion.5) | copy-start | bytes 1179652
  60.0 1.2 copy-start.17
  60.0 1.5 %copy-start.9 = (f32[32,8]{1,0:T(8,128)S(1)}, f32[32,8]{1,0:T(8,128)}, u32[]{:S(2)}) copy-start(f32[32,8]{1,0:T(8,128)} %fusion.54) | copy-start | bytes 3076
  61.6 1.8 %copy-start.7 = (f32[256,6]{1,0:T(8,128)S(1)}, f32[256,6]{1,0:T(8,128)}, u32[]{:S(2)}) copy-start(f32[256,6]{1,0:T(8,128)} %get-tuple-element.108) | copy-start | bytes 18436
  61.7 1.8 %copy-start.6 = (f32[256,6]{1,0:T(8,128)S(1)}, f32[256,6]{1,0:T(8,128)}, u32[]{:S(2)}) copy-start(f32[256,6]{1,0:T(8,128)} %get-tuple-element.99) | copy-start | bytes 18436
  61.7 1.9 %copy-start.5 = (f32[256,6]{1,0:T(8,128)S(1)}, f32[256,6]{1,0:T(8,128)}, u32[]{:S(2)}) copy-start(f32[256,6]{1,0:T(8,128)} %get-tuple-element.97) | copy-start | bytes 18436
  63.7 5.8 %copy-start.13 = (s32[1,256]{1,0:T(1,128)S(1)}, s32[1,256]{1,0:T(1,128)}, u32[]{:S(2)}) copy-start(s32[1,256]{1,0:T(1,128)} %param.20) | copy-start | bytes 3076
  63.7 32.0 %all-to-all-start = ((f32[256,6,128]{2,1,0:T(8,128)}), f32[256,6,128]{2,1,0:T(8,128)S(1)}, u32[]{:S(2)}, u32[]{:S(2)}) async-start(f32[256,6,128]{2,1,0:T(8,128)} %pad_maximum_fusion.5), calls=%async_computation | async-start | bytes 2097152 | tf_op jit(solution)/shard_map/all_to_all | solution.py:152
  129.4 10.9 %all-to-all-start.2 = ((f32[32,1,144]{2,1,0:T(1,128)}), f32[32,1,144]{2,1,0:T(1,128)S(1)}, u32[]{:S(2)}, u32[]{:S(2)}) async-start(f32[32,1,144]{2,1,0:T(1,128)} %reshape.934), calls=%async_computation.2 | async-start | bytes 65536 | tf_op jit(solution)/shard_map/all_to_all | solution.py:187
where the time goes:
time: 145 us; the launch traced here: 144 us
  matrix products  39 us (27%)
  waiting for transfers between devices  31.7 us (22%)
  other arithmetic  28.3 us (20%)
  local copies, waits for them, and re-layouts  26.7 us (18%)
  starting transfers between devices  16.8 us (12%)
    dot_general x8, matrix products, select_block(): jnp.einsum('gcm,gkm->gck', values, selector, precision=lax.Precision.HIGH...  37.9 us
    all_to_all x1, waiting for transfers between devices, local(): lax.all_to_all(cargo_rows, ('tile', 'band'), split_axis=0, concat_axis=0,...  24.7 us
    reduce_sum x2, other arithmetic, pair_terms(): parts_a = [jnp.sum(residual[:, None] * jac_a, axis=2) * grad_scale]  9.05 us
    all_to_all x1, starting transfers between devices, local(): lax.all_to_all(extras, ('tile', 'band'), split_axis=0, concat_axis=0, til...  7.43 us
    all_to_all x1, waiting for transfers between devices, local(): lax.all_to_all(remote_b, ('tile', 'band'), split_axis=0, concat_axis=0, t...  6.99 us
    eq x8, local copies, waits for them, and re-layouts, select_block(): indices[:, :, None] == positions[None, None, :]  6.2 us
    all_to_all x1, starting transfers between devices, local(): lax.all_to_all(cargo_rows, ('tile', 'band'), split_axis=0, concat_axis=0,...  5.77 us
    sub x4, other arithmetic, cross_rows(): left[:, 1] * right[:, 2] - left[:, 2] * right[:, 1]  4.89 us
  transfers between devices with their start and end apart: 3, of which 2 were waited for; matrix products, arithmetic and copies ran while one was open for 37% of the time, Pallas kernels for 0%

commit v1 on v0

v1 whole, which is shorter than its diff:
```python
import functools

import jax
import jax.numpy as jnp
from jax import lax
from jax.experimental import pallas as pl
from jax.experimental.pallas import tpu as pltpu
from jax.sharding import PartitionSpec as P

AXES = ("tile", "band")
SUB = 8
LANE = 128
MSG = 4 * SUB + 1
STAGE = 6 * SUB
GROUP = 16
VMEM_LIMIT = 16 * 1024 * 1024


def iota(axis):
    return lax.broadcasted_iota(jnp.int32, (SUB, LANE), axis)


def pick(values, index):
    values = jnp.broadcast_to(values, (SUB, LANE))
    return jnp.take_along_axis(values, index, axis=1, mode="promise_in_bounds")


def shift_of(size):
    shift = size.bit_length() - 1
    assert 1 << shift == size
    return shift


def rotations(poses):
    half = [poses[i : i + 1, :] * 0.5 for i in range(3)]
    w = 1.0 / jnp.sqrt(1.0 + half[0] * half[0] + half[1] * half[1] + half[2] * half[2])
    x, y, z = half[0] * w, half[1] * w, half[2] * w
    rotation = [
        [1.0 - 2.0 * (y * y + z * z), 2.0 * (x * y - w * z), 2.0 * (x * z + w * y)],
        [2.0 * (x * y + w * z), 1.0 - 2.0 * (x * x + z * z), 2.0 * (y * z - w * x)],
        [2.0 * (x * z - w * y), 2.0 * (y * z + w * x), 1.0 - 2.0 * (x * x + y * y)],
    ]
    return rotation, [poses[i : i + 1, :] for i in range(3, 6)]


def write_world(points, normals, poses, world):
    blocks, frags = points.shape[1], poses.shape[1]
    per_frag = blocks // frags
    stride = world.shape[0] // (3 if normals is None else 6)
    rotation, translation = rotations(poses[...])

    def spread(row, f):
        return jnp.broadcast_to(row[:, f : f + 1], (SUB, LANE))

    for f in range(frags):
        turn = [[spread(rotation[i][j], f) for j in range(3)] for i in range(3)]
        move = [spread(translation[i], f) for i in range(3)]
        for b in range(f * per_frag, (f + 1) * per_frag, SUB):
            x = [points[j, b : b + SUB, :] for j in range(3)]
            for i in range(3):
                world[pl.ds(i * stride + b, SUB), :] = (
                    turn[i][0] * x[0] + turn[i][1] * x[1] + turn[i][2] * x[2] + move[i]
                )
            if normals is not None:
                n = [normals[j, b : b + SUB, :] for j in range(3)]
                for i in range(3):
                    world[pl.ds((3 + i) * stride + b, SUB), :] = (
                        turn[i][0] * n[0] + turn[i][1] * n[1] + turn[i][2] * n[2]
                    )


def write_directions(directions, table):
    frags = directions.shape[2]
    for v in range(2):
        for j in range(6):
            table[6 * v + j : 6 * v + j + 1, 0:frags] = directions[j, v : v + 1, :]


def index_tile(row_ref, first, offset):
    tile = pl.multiple_of(first // LANE * LANE, LANE)
    return pick(row_ref[0:1, pl.ds(tile, LANE)], offset + lax.rem(first, LANE))


def pack_kernel(points, poses, directions, src_s, src_v, maps, counts, out, world, table, used):
    devices = counts.shape[1]
    per_frag = points.shape[1] // poses.shape[1]
    write_world(points, None, poses, world)
    stride = world.shape[0] // 3
    write_directions(directions, table)
    used[0:1, 0:devices] = counts[...]

    def peer(p, carry):
        for s in range(SUB):
            block = src_s[0, p * SUB + s]
            out[pl.ds(p * MSG + s, 3, stride=SUB), :] = world[pl.ds(block, 3, stride=stride), :]
        rows = maps[pl.ds(pl.multiple_of(p * SUB, SUB), SUB), :]
        out[pl.ds(p * MSG + 3 * SUB, SUB), :] = rows.astype(jnp.float32)
        return carry

    lax.fori_loop(0, devices, peer, 0, unroll=4)
    slot = lax.shift_right_logical(iota(1), shift_of(GROUP))
    field = lax.bitwise_and(iota(1), GROUP - 1)
    for q in range(0, devices, SUB):
        block = index_tile(src_v, q * SUB, iota(0) * SUB + slot)
        frag = lax.shift_right_logical(block, shift_of(per_frag))
        limit = pick(used[0:1, :], iota(0) + q)
        extras = jnp.where(slot < limit, 1.0, 0.0)
        for j in range(12):
            extras = jnp.where(field == j, pick(table[j : j + 1, :], frag), extras)
        out[pl.ds(q * MSG + MSG - 1, SUB, stride=MSG), :] = extras


def cross(left, right):
    return [
        left[1] * right[2] - left[2] * right[1],
        left[2] * right[0] - left[0] * right[2],
        left[0] * right[1] - left[1] * right[0],
    ]


def dot3(left, right):
    return left[0] * right[0] + left[1] * right[1] + left[2] * right[2]


def pair_sums(x, y, n, dirs_a, dirs_b):
    p, q = cross(x, n), cross(y, n)
    scalars = [dot3(n, [x[i] - y[i] for i in range(3)])]
    for v in range(2):
        a, b = dirs_a[6 * v : 6 * v + 6], dirs_b[6 * v : 6 * v + 6]
        slide = [a[3 + i] - b[3 + i] for i in range(3)]
        scalars.append(dot3(p, a) - dot3(q, b) + dot3(n, slide))
    lane = iota(1)
    result = jnp.zeros((SUB, LANE), jnp.float32)
    for k, s in enumerate(scalars):
        for c in range(3):
            for at, value in ((6 * k + c, p[c]), (6 * k + 3 + c, n[c]), (18 + 3 * k + c, q[c])):
                total = jnp.sum(s * value, axis=1, keepdims=True)
                result = jnp.where(lane == at, total, result)
    return result


def frag_sums(row_ref, row, sums, per_frag):
    pairs = sums.shape[0]
    frag = lax.shift_right_logical(row_ref[row : row + 1, :], shift_of(per_frag))
    hot = jnp.broadcast_to(frag, (SUB, pairs)) == lax.broadcasted_iota(jnp.int32, (SUB, pairs), 0)
    return jnp.dot(
        hot.astype(jnp.float32),
        sums[...],
        precision=lax.Precision.HIGHEST,
        preferred_element_type=jnp.float32,
    )


def target_side(sums):
    lane = iota(1)
    k = (lane >= 6).astype(jnp.int32) + (lane >= 12).astype(jnp.int32)
    c = lane - 6 * k
    index = jnp.where(c < 3, 18 + 3 * k + c, lane)
    return -pick(sums, jnp.where(lane < 18, index, LANE - 1))


def local_kernel(
    points, normals, poses, directions, pairs_s, pairs_v, maps, dst_s,
    staged, totals, world, table, sources, targets, sums,
):
    per_frag = points.shape[1] // poses.shape[1]
    groups = pairs_s.shape[1] // SUB
    write_world(points, normals, poses, world)
    stride = world.shape[0] // 6
    write_directions(directions, table)

    def stage_remote(g, carry):
        for s in range(SUB):
            block = dst_s[0, g * SUB + s]
            staged[pl.ds(g * STAGE + s, 6, stride=SUB), :] = world[pl.ds(block, 6, stride=stride), :]
        return carry

    lax.fori_loop(0, dst_s.shape[1] // SUB, stage_remote, 0, unroll=4)

    def stage_local(g, carry):
        for s in range(SUB):
            source, target = pairs_s[0, g * SUB + s], pairs_s[1, g * SUB + s]
            sources[pl.ds(g * 3 * SUB + s, 3, stride=SUB), :] = world[pl.ds(source, 3, stride=stride), :]
            targets[pl.ds(g * STAGE + s, 6, stride=SUB), :] = world[pl.ds(target, 6, stride=stride), :]
        return carry

    lax.fori_loop(0, groups, stage_local, 0, unroll=4)

    def group(g, carry):
        first = pl.multiple_of(g * SUB, SUB)
        index = maps[pl.ds(first, SUB), :]
        x = [sources[pl.ds(pl.multiple_of(g * 3 * SUB, SUB) + SUB * i, SUB), :] for i in range(3)]
        yn = [
            pick(targets[pl.ds(pl.multiple_of(g * STAGE, SUB) + SUB * i, SUB), :], index)
            for i in range(6)
        ]
        dirs = []
        for end in range(2):
            block = index_tile(pairs_v.at[end : end + 1], first, iota(0))
            frag = lax.shift_right_logical(block, shift_of(per_frag))
            dirs.append([pick(table[j : j + 1, :], frag) for j in range(12)])
        sums[pl.ds(first, SUB), :] = pair_sums(x, yn[0:3], yn[3:6], dirs[0], dirs[1])
        return carry

    lax.fori_loop(0, groups, group, 0, unroll=2)
    totals[...] = frag_sums(pairs_v, 0, sums, per_frag) + target_side(
        frag_sums(pairs_v, 1, sums, per_frag)
    )


def remote_kernel(arrived, staged, directions, dst_v, totals_in, back, totals, table, sums, *, per_frag):
    devices = arrived.shape[0] // MSG
    write_directions(directions, table)
    slot = lax.shift_right_logical(iota(1), shift_of(GROUP))
    field = lax.bitwise_and(iota(1), GROUP - 1)
    own = slot == iota(0)

    def peer(d, carry):
        base = d * MSG
        first = pl.multiple_of(d * SUB, SUB)
        x = [arrived[pl.ds(base + SUB * i, SUB), :] for i in range(3)]
        index = arrived[pl.ds(base + 3 * SUB, SUB), :].astype(jnp.int32)
        extras = arrived[pl.ds(base + 4 * SUB, 1), :]
        yn = [
            pick(staged[pl.ds(pl.multiple_of(d * STAGE, SUB) + SUB * i, SUB), :], index)
            for i in range(6)
        ]
        dirs_a = [pick(extras, iota(0) * GROUP + j) for j in range(12)]
        valid = pick(extras, iota(0) * GROUP + 12)
        frag = lax.shift_right_logical(index_tile(dst_v, first, iota(0)), shift_of(per_frag))
        dirs_b = [pick(table[j : j + 1, :], frag) for j in range(12)]
        n = [yn[3 + i] * valid for i in range(3)]
        result = pair_sums(x, yn[0:3], n, dirs_a, dirs_b)
        sums[pl.ds(first, SUB), :] = result
        for half in range(2):
            spread = pick(result, field + half * GROUP)
            back[pl.ds(2 * d + half, 1), :] = jnp.sum(
                jnp.where(own, spread, 0.0), axis=0, keepdims=True
            )
        return carry

    lax.fori_loop(0, devices, peer, 0, unroll=2)
    totals[...] = totals_in[...] + target_side(frag_sums(dst_v, 0, sums, per_frag))


def final_kernel(back, totals, src_v, gradient, hess, *, per_frag):
    devices = back.shape[0] // 2
    slot = lax.shift_right_logical(iota(1), shift_of(GROUP))
    sums = [[jnp.zeros((SUB, LANE), jnp.float32) for half in range(2)] for f in range(SUB)]
    for q in range(0, devices, SUB):
        block = index_tile(src_v, q * SUB, iota(0) * SUB + slot)
        frag = lax.shift_right_logical(block, shift_of(per_frag))
        for half in range(2):
            rows = back[pl.ds(2 * q + half, SUB, stride=2), :]
            for f in range(SUB):
                sums[f][half] = sums[f][half] + jnp.where(frag == f, rows, 0.0)
    halves = []
    for half in range(2):
        tile = jnp.zeros((SUB, LANE), jnp.float32)
        for f in range(SUB):
            tile = jnp.where(iota(0) == f, jnp.sum(sums[f][half], axis=0, keepdims=True), tile)
        for step in (64, 32, 16):
            tile = tile + pltpu.roll(tile, step, 1)
        halves.append(tile)
    lane = iota(1)
    total = totals[...] + jnp.where(lane < GROUP, halves[0], jnp.where(lane < 18, halves[1], 0.0))
    total = total.T
    gradient[...] = total[0:6, :] * (1.0 / LANE)
    for v in range(2):
        part = total[6 + 6 * v : 12 + 6 * v, :] * (1.0 / (LANE * per_frag))
        for j in range(6):
            hess[j, v : v + 1, :] = part[j : j + 1, :]


def call(kernel, outs, scratch, spaces, **more):
    return pl.pallas_call(
        kernel,
        out_shape=outs,
        in_specs=[pl.BlockSpec(memory_space=pltpu.SMEM if s else pltpu.VMEM) for s in spaces],
        out_specs=[pl.BlockSpec(memory_space=pltpu.VMEM)] * len(outs),
        scratch_shapes=scratch,
        compiler_params=pltpu.CompilerParams(vmem_limit_bytes=VMEM_LIMIT),
        **more,
    )


def exchange(rows, devices):
    sent = rows.reshape(devices, 1, -1)
    sent = lax.all_to_all(sent, AXES, split_axis=0, concat_axis=0, tiled=True)
    return sent.reshape(rows.shape)


def local(
    points, normals, poses, directions, local_pairs, local_maps,
    remote_src, remote_maps, remote_dst, counts,
):
    devices = lax.axis_size("tile") * lax.axis_size("band")
    blocks, _, count = points.shape
    frags = poses.shape[1]
    slots = remote_src.shape[1]
    pairs = local_pairs.shape[1]
    assert count == LANE and frags == SUB and slots == devices * SUB and devices <= LANE
    per_frag = blocks // frags
    stride = blocks + SUB
    f32 = jnp.float32
    points = points.transpose(1, 0, 2)
    normals = normals.transpose(1, 0, 2)
    directions = directions.transpose(1, 0, 2)

    def array(*shape):
        return jax.ShapeDtypeStruct(shape, f32)

    table = pltpu.VMEM((2 * SUB, LANE), f32)
    (message,) = call(
        pack_kernel,
        [array(devices * MSG, LANE)],
        [pltpu.VMEM((3 * stride, LANE), f32), table, pltpu.VMEM((SUB, LANE), jnp.int32)],
        [0, 0, 0, 1, 0, 0, 0],
    )(points, poses, directions, remote_src, remote_src, remote_maps[0], counts)
    arrived = exchange(message, devices)
    staged, totals = call(
        local_kernel,
        [array(devices * STAGE, LANE), array(SUB, LANE)],
        [
            pltpu.VMEM((6 * stride, LANE), f32),
            table,
            pltpu.VMEM((pairs * 3, LANE), f32),
            pltpu.VMEM((pairs * 6, LANE), f32),
            pltpu.VMEM((pairs, LANE), f32),
        ],
        [0, 0, 0, 0, 1, 0, 0, 1],
        cost_estimate=pl.CostEstimate(
            flops=200 * pairs * LANE, bytes_accessed=4_000_000, transcendentals=0
        ),
    )(points, normals, poses, directions, local_pairs, local_pairs, local_maps, remote_dst)
    back, totals = call(
        functools.partial(remote_kernel, per_frag=per_frag),
        [array(devices * 2, LANE), array(SUB, LANE)],
        [table, pltpu.VMEM((slots, LANE), f32)],
        [0, 0, 0, 0, 0],
    )(arrived, staged, directions, remote_dst, totals)
    back = exchange(back, devices)
    gradient, hess = call(
        functools.partial(final_kernel, per_frag=per_frag),
        [array(6, frags), array(6, 2, frags)],
        [],
        [0, 0, 0],
    )(back, totals, remote_src)
    return (gradient, hess.transpose(1, 0, 2))


def solution(mesh):
    placed = (
        P(AXES, None, None),
        P(AXES, None, None),
        P(None, AXES),
        P(None, None, AXES),
        P(None, AXES),
        P(AXES, None),
        P(AXES, None),
        P(AXES, None, None),
        P(AXES, None),
        P(AXES, None),
    )
    return jax.shard_map(
        local,
        mesh=mesh,
        in_specs=placed,
        out_specs=(P(None, AXES), P(None, None, AXES)),
        check_vma=False,
    )
```

time: 145 us -> 48.7 us (0.34)
  matrix products: 39 us -> 0 us
  other arithmetic: 28.3 us -> 0 us
  waiting for transfers between devices: 31.7 us -> 5.92 us
  local copies, waits for them, and re-layouts: 26.7 us -> 3.91 us
  Pallas kernels: 0 us -> 20.3 us
  blocking collectives: 0 us -> 10.2 us
  starting transfers between devices: 16.8 us -> 7.3 us
    dot_general x12 -> x0, matrix products: 39 us -> none  [the longest x8 37.9 us: select_block(): jnp.einsum('gcm,gkm->gck', values, selector, precision=lax.Precision.HIGH...]
    all_to_all x3 -> x1, waiting for transfers between devices: 31.7 us -> 5.92 us  [exchange(): sent = lax.all_to_all(sent, AXES, split_axis=0, concat_axis=0, tiled=True)]
    pallas_call x0 -> x4, Pallas kernels: none -> 20.3 us  [the longest x1 9.24 us: local(): call(local_kernel, [array(devices * STAGE, LANE), array(SUB, LANE)], [plt...]
    reduce_sum x6 -> x0, other arithmetic: 16.1 us -> none  [the longest x2 9.05 us: pair_terms(): parts_a = [jnp.sum(residual[:, None] * jac_a, axis=2) * grad_scale]]
    gather x10 -> x0, local copies, waits for them, and re-layouts: 10.3 us -> none  [the longest x1 1.75 us: local(): world_pts[send_blocks]]
    all_to_all x0 -> x1, blocking collectives: none -> 10.2 us  [exchange(): sent = lax.all_to_all(sent, AXES, split_axis=0, concat_axis=0, tiled=True)]
    all_to_all x3 -> x1, starting transfers between devices: 16.8 us -> 7.3 us  [exchange(): sent = lax.all_to_all(sent, AXES, split_axis=0, concat_axis=0, tiled=True)]
    eq x8 -> x0, local copies, waits for them, and re-layouts: 6.2 us -> none  [select_block(): indices[:, :, None] == positions[None, None, :]]
  transfers between devices with their start and end apart: 3 -> 1, of which waited for: 2 -> 1; matrix products, arithmetic and copies ran while one was open for 37% -> 0% of each run, Pallas kernels for 0% -> 19%
where the time goes in v1:
time: 48.7 us; the launch traced here: 48.3 us
  Pallas kernels  20.3 us (42%)
  blocking collectives  10.2 us (21%)
  starting transfers between devices  7.3 us (15%)
  waiting for transfers between devices  5.92 us (12%)
  local copies, waits for them, and re-layouts  3.91 us (8%)
  between operations  0.73 us (1%)
    all_to_all x1, blocking collectives, exchange(): sent = lax.all_to_all(sent, AXES, split_axis=0, concat_axis=0, tiled=True)  10.2 us
    pallas_call x1, Pallas kernels, local(): call(local_kernel, [array(devices * STAGE, LANE), array(SUB, LANE)], [plt...  9.24 us
    pallas_call x1, Pallas kernels, local(): call(functools.partial(remote_kernel, per_frag=per_frag), [array(devices...  7.95 us
    all_to_all x1, starting transfers between devices, exchange(): sent = lax.all_to_all(sent, AXES, split_axis=0, concat_axis=0, tiled=True)  7.3 us
    all_to_all x1, waiting for transfers between devices, exchange(): sent = lax.all_to_all(sent, AXES, split_axis=0, concat_axis=0, tiled=True)  5.92 us
    unnamed x24, local copies, waits for them, and re-layouts  3.91 us
    pallas_call x1, Pallas kernels, local(): call(pack_kernel, [array(devices * MSG, LANE)], [pltpu.VMEM((3 * stride,...  2.1 us
    pallas_call x1, Pallas kernels, local(): call(functools.partial(final_kernel, per_frag=per_frag), [array(6, frags)...  0.99 us
  transfers between devices with their start and end apart: 1, of which 1 were waited for; matrix products, arithmetic and copies ran while one was open for 0% of the time, Pallas kernels for 19%

profile of v1, /device:TPU:0, one launch (start us, length us, event | category | flops | bytes accessed | tf_op | source)
XLA Modules:
  0.0 48.3 jit_solution(16981659285823559248)
XLA Ops:
  0.6 0.0 copy-start.7
  0.6 0.0 copy-start.8
  0.7 0.0 copy-start.11
  0.7 0.7 %copy-done.7 = f32[6,8]{1,0:T(8,128)S(1)} copy-done((f32[6,8]{1,0:T(8,128)S(1)}, f32[6,8]{1,0:T(8,128)}, u32[]{:S(2)}) %copy-start.7) | copy-done | bytes 216
  1.3 0.0 copy-done.8
  1.3 0.0 copy-done.11
  1.3 0.0 copy-start
  1.3 1.0 %copy-done = f32[256,3,128]{2,0,1:T(8,128)S(1)} copy-done((f32[256,3,128]{2,0,1:T(8,128)S(1)}, f32[256,3,128]{2,0,1:T(8,128)}, u32[]{:S(2)}) %copy-start) | copy-done | bytes 393240
  2.3 0.0 copy-start.4
  2.3 0.9 %copy-done.4 = s32[1,256,128]{2,1,0:T(8,128)S(1)} copy-done((s32[1,256,128]{2,1,0:T(8,128)S(1)}, s32[1,256,128]{2,1,0:T(8,128)}, u32[]{:S(2)}) %copy-start.4) | copy-done | bytes 131096
  3.2 0.0 copy-start.5
  3.2 0.7 %copy-done.5 = f32[2,6,8]{2,0,1:T(2,128)S(1)} copy-done((f32[2,6,8]{2,0,1:T(2,128)S(1)}, f32[2,6,8]{2,0,1:T(2,128)}, u32[]{:S(2)}) %copy-start.5) | copy-done | bytes 408
  3.9 2.1 %shard_map.113 = f32[1056,128]{1,0:T(8,128)} custom-call(f32[3,256,128]{2,1,0:T(8,128)S(1)} %bitcast.10, f32[6,8]{1,0:T(8,128)S(1)} %copy-done.7, f32[6,2,8]{2,1,0:T(2,128)S(1)} %bitcast.15, s32[1,256]{1,0:T(1,128)S(1)} %copy-done.8, s32[1,256]{1,0:T(1,128)S(1)} %copy-done.8, s32[256,128]{1,0:T(8,128)S(1)} %bitcast.14, s32[1,32]{1,0:T(1,128)S(1)} %copy-done.11), custom_call_target="tpu_custom_call" | custom-call | tf_op jit(solution)/shard_map/pallas_call | solution.py:314
  6.0 0.0 copy-start.1
  6.0 0.0 copy-start.2
  6.0 0.0 copy-start.3
  6.0 0.0 copy-start.6
  6.0 0.0 copy-start.9
  6.0 7.3 %all-to-all-start = ((f32[32,1,4224]{2,1,0:T(1,128)}), f32[32,1,4224]{2,1,0:T(1,128)S(1)}, u32[]{:S(2)}, u32[]{:S(2)}) async-start(f32[32,1,4224]{2,1,0:T(1,128)} %bitcast.3), calls=%async_computation | async-start | bytes 1081344 | tf_op jit(solution)/shard_map/all_to_all | solution.py:289
  13.4 0.0 copy-start.10
  13.4 0.0 copy-done.1
  13.4 0.0 copy-done.2
  13.4 0.0 copy-done.3
  13.4 0.0 copy-done.6
  13.4 0.0 copy-done.9
  13.4 0.6 %copy-done.10 = s32[1,256]{1,0:T(1,128)S(1)} copy-done((s32[1,256]{1,0:T(1,128)S(1)}, s32[1,256]{1,0:T(1,128)}, u32[]{:S(2)}) %copy-start.10) | copy-done | bytes 1048
  14.0 9.2 %shard_map.114 = (f32[1536,128]{1,0:T(8,128)S(1)}, f32[8,128]{1,0:T(8,128)S(1)}) custom-call(f32[3,256,128]{2,1,0:T(8,128)S(1)} %bitcast.11, f32[3,256,128]{2,1,0:T(8,128)S(1)} %bitcast.12, f32[6,8]{1,0:T(8,128)S(1)} %copy-done.7, f32[6,2,8]{2,1,0:T(2,128)S(1)} %bitcast.16, s32[2,256]{1,0:T(2,128)S(1)} %copy-done.9, s32[2,256]{1,0:T(2,128)S(1)} %copy-done.9, ...), custom_call_target="tpu_custom_call" | custom-call | flops 6553600 | bytes 4000000 | tf_op jit(solution)/shard_map/pallas_call | solution.py:321
  23.3 5.9 %all-to-all-done = f32[32,1,4224]{2,1,0:T(1,128)S(1)} async-done(((f32[32,1,4224]{2,1,0:T(1,128)}), f32[32,1,4224]{2,1,0:T(1,128)S(1)}, u32[]{:S(2)}, u32[]{:S(2)}) %all-to-all-start) | async-done | bytes 540704 | tf_op jit(solution)/shard_map/all_to_all | solution.py:289
  29.2 8.0 %shard_map.115 = (f32[64,128]{1,0:T(8,128)S(1)}, f32[8,128]{1,0:T(8,128)S(1)}) custom-call(f32[1056,128]{1,0:T(8,128)S(1)} %bitcast.9, f32[1536,128]{1,0:T(8,128)S(1)} %get-tuple-element.8.staged, f32[6,2,8]{2,1,0:T(2,128)S(1)} %bitcast.17, s32[1,256]{1,0:T(1,128)S(1)} %copy-done.10, f32[8,128]{1,0:T(8,128)S(1)} %get-tuple-element.9.totals_in), custom_call_target="tpu_custom_call" | custom-call | tf_op jit(solution)/shard_map/pallas_call | solution.py:336
  37.2 10.2 %all_to_all.10 = f32[32,1,256]{2,1,0:T(1,128)S(1)} all-to-all(f32[32,1,256]{2,1,0:T(1,128)S(1)} %bitcast.18), channel_id=1, replica_groups=mesh['tile'=8,'band'=4] {'tile','band'}, dimensions={0} | all-to-all | bytes 65536 | tf_op jit(solution)/shard_map/all_to_all | solution.py:289
  47.3 1.0 %shard_map.116 = (f32[6,8]{1,0:T(8,128)}, f32[6,2,8]{2,1,0:T(2,128)}) custom-call(f32[64,128]{1,0:T(8,128)S(1)} %bitcast.13, f32[8,128]{1,0:T(8,128)S(1)} %get-tuple-element.11.totals, s32[1,256]{1,0:T(1,128)S(1)} %copy-done.8), custom_call_target="tpu_custom_call" | custom-call | tf_op jit(solution)/shard_map/pallas_call | solution.py:343
Async XLA Ops:
  0.6 0.7 %copy-start.7 = (f32[6,8]{1,0:T(8,128)S(1)}, f32[6,8]{1,0:T(8,128)}, u32[]{:S(2)}) copy-start(f32[6,8]{1,0:T(8,128)} %poses.3) | copy-start | bytes 580
  0.6 0.7 %copy-start.8 = (s32[1,256]{1,0:T(1,128)S(1)}, s32[1,256]{1,0:T(1,128)}, u32[]{:S(2)}) copy-start(s32[1,256]{1,0:T(1,128)} %src_v.3) | copy-start | bytes 3076
  0.7 0.7 %copy-start.11 = (s32[1,32]{1,0:T(1,128)S(1)}, s32[1,32]{1,0:T(1,128)}, u32[]{:S(2)}) copy-start(s32[1,32]{1,0:T(1,128)} %counts.1) | copy-start | bytes 388
  1.3 1.0 %copy-start = (f32[256,3,128]{2,0,1:T(8,128)S(1)}, f32[256,3,128]{2,0,1:T(8,128)}, u32[]{:S(2)}) copy-start(f32[256,3,128]{2,0,1:T(8,128)} %param.10) | copy-start | bytes 1179652
  2.3 0.9 %copy-start.4 = (s32[1,256,128]{2,1,0:T(8,128)S(1)}, s32[1,256,128]{2,1,0:T(8,128)}, u32[]{:S(2)}) copy-start(s32[1,256,128]{2,1,0:T(8,128)} %param.17) | copy-start | bytes 393220
  3.2 0.7 %copy-start.5 = (f32[2,6,8]{2,0,1:T(2,128)S(1)}, f32[2,6,8]{2,0,1:T(2,128)}, u32[]{:S(2)}) copy-start(f32[2,6,8]{2,0,1:T(2,128)} %param.13) | copy-start | bytes 1156
  6.0 7.3 %copy-start.1 = (f32[256,3,128]{2,0,1:T(8,128)S(1)}, f32[256,3,128]{2,0,1:T(8,128)}, u32[]{:S(2)}) copy-start(f32[256,3,128]{2,0,1:T(8,128)} %param.10) | copy-start | bytes 1179652
  6.0 7.4 %copy-start.2 = (f32[256,3,128]{2,0,1:T(8,128)S(1)}, f32[256,3,128]{2,0,1:T(8,128)}, u32[]{:S(2)}) copy-start(f32[256,3,128]{2,0,1:T(8,128)} %param.11) | copy-start | bytes 1179652
  6.0 7.4 %copy-start.3 = (s32[256,128]{1,0:T(8,128)S(1)}, s32[256,128]{1,0:T(8,128)}, u32[]{:S(2)}) copy-start(s32[256,128]{1,0:T(8,128)} %maps.1) | copy-start | bytes 393220
  6.0 7.4 %copy-start.6 = (f32[2,6,8]{2,0,1:T(2,128)S(1)}, f32[2,6,8]{2,0,1:T(2,128)}, u32[]{:S(2)}) copy-start(f32[2,6,8]{2,0,1:T(2,128)} %param.13) | copy-start | bytes 1156
  6.0 7.4 %copy-start.9 = (s32[2,256]{1,0:T(2,128)S(1)}, s32[2,256]{1,0:T(2,128)}, u32[]{:S(2)}) copy-start(s32[2,256]{1,0:T(2,128)} %pairs_v.1) | copy-start | bytes 6148
  6.0 23.2 %all-to-all-start = ((f32[32,1,4224]{2,1,0:T(1,128)}), f32[32,1,4224]{2,1,0:T(1,128)S(1)}, u32[]{:S(2)}, u32[]{:S(2)}) async-start(f32[32,1,4224]{2,1,0:T(1,128)} %bitcast.3), calls=%async_computation | async-start | bytes 1081344 | tf_op jit(solution)/shard_map/all_to_all | solution.py:289
  13.4 0.7 %copy-start.10 = (s32[1,256]{1,0:T(1,128)S(1)}, s32[1,256]{1,0:T(1,128)}, u32[]{:S(2)}) copy-start(s32[1,256]{1,0:T(1,128)} %dst_v.1) | copy-start | bytes 3076

commit v2 on v1

v2 whole, which is shorter than its diff:
```python
import functools

import jax
import jax.numpy as jnp
from jax import lax
from jax.experimental import pallas as pl
from jax.experimental.pallas import tpu as pltpu
from jax.sharding import PartitionSpec as P

AXES = ("tile", "band")
SUB = 8
LANE = 128
MSG = 4 * SUB + 1
TARGET = 8 * SUB
SOURCE = 9 * SUB
TOGETHER = 4
GROUP = 16
VMEM_LIMIT = 16 * 1024 * 1024


def iota(axis):
    return lax.broadcasted_iota(jnp.int32, (SUB, LANE), axis)


def pick(values, index):
    values = jnp.broadcast_to(values, (SUB, LANE))
    return jnp.take_along_axis(values, index, axis=1, mode="promise_in_bounds")


def shift_of(size):
    shift = size.bit_length() - 1
    assert 1 << shift == size
    return shift


def rotations(poses):
    half = [poses[i : i + 1, :] * 0.5 for i in range(3)]
    w = 1.0 / jnp.sqrt(1.0 + half[0] * half[0] + half[1] * half[1] + half[2] * half[2])
    x, y, z = half[0] * w, half[1] * w, half[2] * w
    rotation = [
        [1.0 - 2.0 * (y * y + z * z), 2.0 * (x * y - w * z), 2.0 * (x * z + w * y)],
        [2.0 * (x * y + w * z), 1.0 - 2.0 * (x * x + z * z), 2.0 * (y * z - w * x)],
        [2.0 * (x * z - w * y), 2.0 * (y * z + w * x), 1.0 - 2.0 * (x * x + y * y)],
    ]
    return rotation, [poses[i : i + 1, :] for i in range(3, 6)]


def cross(left, right):
    return [
        left[1] * right[2] - left[2] * right[1],
        left[2] * right[0] - left[0] * right[2],
        left[0] * right[1] - left[1] * right[0],
    ]


def dot3(left, right):
    return left[0] * right[0] + left[1] * right[1] + left[2] * right[2]


def spread(row, f):
    return jnp.broadcast_to(row[:, f : f + 1], (SUB, LANE))


def write_points(points, poses, world):
    blocks, frags = points.shape[1], poses.shape[1]
    per_frag, stride = blocks // frags, blocks + SUB
    rotation, translation = rotations(poses[...])
    for f in range(frags):
        turn = [[spread(rotation[i][j], f) for j in range(3)] for i in range(3)]
        move = [spread(translation[i], f) for i in range(3)]
        for b in range(f * per_frag, (f + 1) * per_frag, SUB):
            x = [points[j, b : b + SUB, :] for j in range(3)]
            for i in range(3):
                world[pl.ds(i * stride + b, SUB), :] = dot3(turn[i], x) + move[i]


def write_fields(points, normals, poses, directions, world):
    blocks, frags = points.shape[1], poses.shape[1]
    per_frag, stride = blocks // frags, blocks + SUB
    rotation, translation = rotations(poses[...])
    for f in range(frags):
        turn = [[spread(rotation[i][j], f) for j in range(3)] for i in range(3)]
        move = [spread(translation[i], f) for i in range(3)]
        way = [[spread(directions[j, v : v + 1, :], f) for j in range(6)] for v in range(2)]
        for b in range(f * per_frag, (f + 1) * per_frag, SUB):
            x = [points[j, b : b + SUB, :] for j in range(3)]
            m = [normals[j, b : b + SUB, :] for j in range(3)]
            y = [dot3(turn[i], x) + move[i] for i in range(3)]
            n = [dot3(turn[i], m) for i in range(3)]
            speed = []
            for v in range(2):
                swing = cross(way[v][0:3], y)
                speed.append([swing[i] + way[v][3 + i] for i in range(3)])
            along = [dot3(n, speed[v]) for v in range(2)]
            for i, row in enumerate(y + n + along + speed[0] + speed[1]):
                world[pl.ds(i * stride + b, SUB), :] = row


def index_tile(row_ref, first, offset):
    tile = first // LANE * LANE
    return pick(row_ref[0:1, pl.ds(tile, LANE)], offset + first % LANE)


def pack_kernel(
    points_h, poses_h, directions_h, src_h, maps_h, counts_h, out,
    points, poses, directions, src_s, src_v, maps, used, world, table, sems,
):
    devices = counts_h.shape[1]
    per_frag = points.shape[1] // poses.shape[1]
    stride = points.shape[1] + SUB
    pairs = [
        (poses_h, poses), (points_h, points), (src_h, src_s), (maps_h, maps),
        (directions_h, directions), (src_h, src_v), (counts_h, used),
    ]
    copies = [pltpu.make_async_copy(a, b, sems.at[i]) for i, (a, b) in enumerate(pairs)]
    for copy in copies:
        copy.start()
    copies[0].wait()
    copies[1].wait()
    write_points(points, poses, world)
    copies[2].wait()
    copies[3].wait()

    def peer(p, carry):
        for s in range(SUB):
            block = src_s[0, p * SUB + s]
            out[pl.ds(p * MSG + s, 3, stride=SUB), :] = world[pl.ds(block, 3, stride=stride), :]
        rows = maps[pl.ds(pl.multiple_of(p * SUB, SUB), SUB), :]
        out[pl.ds(p * MSG + 3 * SUB, SUB), :] = rows.astype(jnp.float32)
        return carry

    lax.fori_loop(0, devices, peer, 0, unroll=4)
    for copy in copies[4:]:
        copy.wait()
    frags = directions.shape[2]
    for v in range(2):
        for j in range(6):
            table[6 * v + j : 6 * v + j + 1, 0:frags] = directions[j, v : v + 1, :]
    limits = jnp.broadcast_to(used[0:1, :], (SUB, devices))
    peers = lax.broadcasted_iota(jnp.int32, (SUB, devices), 1)
    row = lax.broadcasted_iota(jnp.int32, (SUB, devices), 0)
    slot = lax.shift_right_logical(iota(1), shift_of(GROUP))
    field = lax.bitwise_and(iota(1), GROUP - 1)
    for q in range(0, devices, SUB):
        block = index_tile(src_v, q * SUB, iota(0) * SUB + slot)
        frag = lax.shift_right_logical(block, shift_of(per_frag))
        limit = jnp.sum(
            jnp.where(peers == row + q, limits.astype(jnp.float32), 0.0), axis=1, keepdims=True
        )
        extras = jnp.where(slot.astype(jnp.float32) < limit, 1.0, 0.0)
        for j in range(12):
            extras = jnp.where(field == j, pick(table[j : j + 1, :], frag), extras)
        out[pl.ds(q * MSG + MSG - 1, SUB, stride=MSG), :] = extras


def pair_sums(scalars, p, n, q):
    field = lax.bitwise_and(iota(1), GROUP - 1)
    tiles = [jnp.zeros((SUB, LANE), jnp.float32) for half in range(2)]
    for k, s in enumerate(scalars):
        for c in range(3):
            for at, value in ((6 * k + c, p[c]), (6 * k + 3 + c, n[c]), (18 + 3 * k + c, q[c])):
                total = jnp.sum(s * value, axis=1, keepdims=True)
                half = at // GROUP
                tiles[half] = jnp.where(field == at % GROUP, total, tiles[half])
    return tiles


def frag_sums(row, sums, per_frag):
    pairs = sums.shape[0]
    frag = lax.shift_right_logical(row, shift_of(per_frag))
    hot = jnp.broadcast_to(frag, (SUB, pairs)) == lax.broadcasted_iota(jnp.int32, (SUB, pairs), 0)
    total = jnp.dot(
        hot.astype(jnp.float32),
        sums[...],
        precision=lax.Precision.HIGHEST,
        preferred_element_type=jnp.float32,
    )
    return [total[:, 0:LANE], total[:, LANE:]]


def target_side(sums):
    lane = lax.bitwise_and(iota(1), GROUP - 1)
    k = (lane >= 6).astype(jnp.int32) + (lane >= 12).astype(jnp.int32)
    c = lane - 6 * k
    first = jnp.where(c < 3, pick(sums[1], jnp.minimum(2 + 3 * k + c, GROUP - 1)), sums[0])
    return [-first, -sums[1]]


def local_kernel(
    points, normals, poses, directions, pairs_s, pairs_v, maps, dst_s,
    staged, totals, world, sources, targets, sums,
):
    per_frag = points.shape[1] // poses.shape[1]
    stride = points.shape[1] + SUB
    groups = pairs_s.shape[1] // SUB
    write_fields(points, normals, poses, directions, world)

    def stage_remote(g, carry):
        for s in range(SUB):
            block = dst_s[0, g * SUB + s]
            staged[pl.ds(g * TARGET + s, 8, stride=SUB), :] = world[pl.ds(block, 8, stride=stride), :]
        return carry

    lax.fori_loop(0, dst_s.shape[1] // SUB, stage_remote, 0, unroll=4)

    def stage_local(g, carry):
        for s in range(SUB):
            a, b = pairs_s[0, g * SUB + s], pairs_s[1, g * SUB + s]
            targets[pl.ds(g * TARGET + s, 8, stride=SUB), :] = world[pl.ds(b, 8, stride=stride), :]
            sources[pl.ds(g * SOURCE + s, 3, stride=SUB), :] = world[pl.ds(a, 3, stride=stride), :]
            sources[pl.ds(g * SOURCE + 3 * SUB + s, 6, stride=SUB), :] = world[
                pl.ds(a + 8 * stride, 6, stride=stride), :
            ]
        return carry

    lax.fori_loop(0, groups, stage_local, 0, unroll=4)

    def step(i, carry):
        done = []
        for u in range(TOGETHER):
            g = i * TOGETHER + u
            index = maps[pl.ds(pl.multiple_of(g * SUB, SUB), SUB), :]
            base = pl.multiple_of(g * SOURCE, SUB)
            source = [sources[pl.ds(base + SUB * k, SUB), :] for k in range(9)]
            base = pl.multiple_of(g * TARGET, SUB)
            target = [pick(targets[pl.ds(base + SUB * k, SUB), :], index) for k in range(8)]
            x, y, n = source[0:3], target[0:3], target[3:6]
            scalars = [dot3(n, [x[k] - y[k] for k in range(3)])]
            for v in range(2):
                scalars.append(dot3(n, source[3 + 3 * v : 6 + 3 * v]) - target[6 + v])
            done.append(pair_sums(scalars, cross(x, n), n, cross(y, n)))
        for u in range(TOGETHER):
            first = pl.multiple_of((i * TOGETHER + u) * SUB, SUB)
            for half in range(2):
                sums[pl.ds(first, SUB), half * LANE : (half + 1) * LANE] = done[u][half]
        return carry

    lax.fori_loop(0, groups // TOGETHER, step, 0)
    side_a = frag_sums(pairs_v[0:1, :], sums, per_frag)
    side_b = target_side(frag_sums(pairs_v[1:2, :], sums, per_frag))
    for half in range(2):
        totals[half * SUB : (half + 1) * SUB, :] = side_a[half] + side_b[half]


def remote_kernel(arrived, staged, back, sums):
    devices = arrived.shape[0] // MSG
    own = lax.shift_right_logical(iota(1), shift_of(GROUP)) == iota(0)

    def step(i, carry):
        done = []
        for u in range(TOGETHER):
            d = i * TOGETHER + u
            x = [arrived[pl.ds(d * MSG + SUB * k, SUB), :] for k in range(3)]
            index = arrived[pl.ds(d * MSG + 3 * SUB, SUB), :].astype(jnp.int32)
            extras = arrived[pl.ds(d * MSG + 4 * SUB, 1), :]
            base = pl.multiple_of(d * TARGET, SUB)
            target = [pick(staged[pl.ds(base + SUB * k, SUB), :], index) for k in range(8)]
            way = [pick(extras, iota(0) * GROUP + j) for j in range(13)]
            y, n = target[0:3], target[3:6]
            p = cross(x, n)
            scalars = [dot3(n, [x[k] - y[k] for k in range(3)])]
            for v in range(2):
                a = way[6 * v : 6 * v + 6]
                scalars.append(dot3(p, a[0:3]) + dot3(n, a[3:6]) - target[6 + v])
            scalars = [s * way[12] for s in scalars]
            done.append(pair_sums(scalars, p, n, cross(y, n)))
        rows = [
            [jnp.sum(jnp.where(own, tile, 0.0), axis=0, keepdims=True) for tile in tiles]
            for tiles in done
        ]
        for u in range(TOGETHER):
            d = i * TOGETHER + u
            for half in range(2):
                back[pl.ds(2 * d + half, 1), :] = rows[u][half]
                sums[pl.ds(pl.multiple_of(d * SUB, SUB), SUB), half * LANE : (half + 1) * LANE] = done[
                    u
                ][half]
        return carry

    lax.fori_loop(0, devices // TOGETHER, step, 0)


def total_kernel(sums, dst_v, totals_in, totals, *, per_frag):
    side_b = target_side(frag_sums(dst_v[...], sums, per_frag))
    for half in range(2):
        rows = slice(half * SUB, (half + 1) * SUB)
        totals[rows, :] = totals_in[rows, :] + side_b[half]


def final_kernel(back, totals, src_v, gradient, hess, *, per_frag):
    devices = back.shape[0] // 2
    slot = lax.shift_right_logical(iota(1), shift_of(GROUP))
    sums = [[jnp.zeros((SUB, LANE), jnp.float32) for half in range(2)] for f in range(SUB)]
    for q in range(0, devices, SUB):
        block = index_tile(src_v, q * SUB, iota(0) * SUB + slot)
        frag = lax.shift_right_logical(block, shift_of(per_frag))
        for half in range(2):
            rows = back[pl.ds(2 * q + half, SUB, stride=2), :]
            for f in range(SUB):
                sums[f][half] = sums[f][half] + jnp.where(frag == f, rows, 0.0)
    halves = []
    for half in range(2):
        tile = jnp.zeros((SUB, LANE), jnp.float32)
        for f in range(SUB):
            tile = jnp.where(iota(0) == f, jnp.sum(sums[f][half], axis=0, keepdims=True), tile)
        for step in (64, 32, 16):
            tile = tile + pltpu.roll(tile, step, 1)
        halves.append(tile + totals[half * SUB : (half + 1) * SUB, :])
    total = jnp.where(iota(1) < GROUP, halves[0], halves[1]).T
    gradient[...] = total[0:6, :] * (1.0 / LANE)
    for v in range(2):
        part = total[6 + 6 * v : 12 + 6 * v, :] * (1.0 / (LANE * per_frag))
        for j in range(6):
            hess[j, v : v + 1, :] = part[j : j + 1, :]


def call(kernel, outs, scratch, spaces, **more):
    kinds = {"v": pltpu.VMEM, "s": pltpu.SMEM, "h": pltpu.HBM}
    return pl.pallas_call(
        kernel,
        out_shape=outs,
        in_specs=[pl.BlockSpec(memory_space=kinds[s]) for s in spaces],
        out_specs=[pl.BlockSpec(memory_space=pltpu.VMEM)] * len(outs),
        scratch_shapes=scratch,
        compiler_params=pltpu.CompilerParams(vmem_limit_bytes=VMEM_LIMIT),
        **more,
    )


def exchange(rows, devices):
    sent = rows.reshape(devices, 1, -1)
    sent = lax.all_to_all(sent, AXES, split_axis=0, concat_axis=0, tiled=True)
    return sent.reshape(rows.shape)


def local(
    points, normals, poses, directions, local_pairs, local_maps,
    remote_src, remote_maps, remote_dst, counts,
):
    devices = lax.axis_size("tile") * lax.axis_size("band")
    blocks, _, count = points.shape
    frags = poses.shape[1]
    slots = remote_src.shape[1]
    pairs = local_pairs.shape[1]
    assert count == LANE and frags == SUB and slots == devices * SUB and devices <= LANE
    per_frag = blocks // frags
    stride = blocks + SUB
    f32 = jnp.float32
    points = points.transpose(1, 0, 2)
    normals = normals.transpose(1, 0, 2)
    directions = directions.transpose(1, 0, 2)

    def array(*shape):
        return jax.ShapeDtypeStruct(shape, f32)

    def vmem(*shape, dtype=f32):
        return pltpu.VMEM(shape, dtype)

    (message,) = call(
        pack_kernel,
        [array(devices * MSG, LANE)],
        [
            vmem(3, blocks, LANE),
            vmem(6, frags),
            vmem(6, 2, frags),
            pltpu.SMEM((1, slots), jnp.int32),
            vmem(1, slots, dtype=jnp.int32),
            vmem(slots, LANE, dtype=jnp.int32),
            vmem(1, devices, dtype=jnp.int32),
            vmem(3 * stride, LANE),
            vmem(2 * SUB, LANE),
            pltpu.SemaphoreType.DMA((7,)),
        ],
        "hhhhhh",
    )(points, poses, directions, remote_src, remote_maps[0], counts)
    arrived = exchange(message, devices)
    staged, totals = call(
        local_kernel,
        [array(devices * TARGET, LANE), array(2 * SUB, LANE)],
        [
            vmem(14 * stride, LANE),
            vmem(pairs // SUB * SOURCE, LANE),
            vmem(pairs // SUB * TARGET, LANE),
            vmem(pairs, 2 * LANE),
        ],
        "vvvvsvvs",
        cost_estimate=pl.CostEstimate(
            flops=200 * pairs * LANE, bytes_accessed=4_000_000, transcendentals=0
        ),
    )(points, normals, poses, directions, local_pairs, local_pairs, local_maps, remote_dst)
    back, sums = call(
        remote_kernel, [array(devices * 2, LANE), array(slots, 2 * LANE)], [], "vv"
    )(arrived, staged)
    back = exchange(back, devices)
    (totals,) = call(
        functools.partial(total_kernel, per_frag=per_frag),
        [array(2 * SUB, LANE)],
        [],
        "vvv",
        cost_estimate=pl.CostEstimate(
            flops=2 * SUB * slots * 2 * LANE, bytes_accessed=1_000_000, transcendentals=0
        ),
    )(sums, remote_dst, totals)
    gradient, hess = call(
        functools.partial(final_kernel, per_frag=per_frag),
        [array(6, frags), array(6, 2, frags)],
        [],
        "vvv",
    )(back, totals, remote_src)
    return (gradient, hess.transpose(1, 0, 2))


def solution(mesh):
    placed = (
        P(AXES, None, None),
        P(AXES, None, None),
        P(None, AXES),
        P(None, None, AXES),
        P(None, AXES),
        P(AXES, None),
        P(AXES, None),
        P(AXES, None, None),
        P(AXES, None),
        P(AXES, None),
    )
    return jax.shard_map(
        local,
        mesh=mesh,
        in_specs=placed,
        out_specs=(P(None, AXES), P(None, None, AXES)),
        check_vma=False,
    )
```

time: 48.7 us -> 47.1 us (0.967)
  blocking collectives: 10.2 us -> 0 us
  waiting for transfers between devices: 5.92 us -> 15.8 us
  Pallas kernels: 20.3 us -> 15.8 us
  starting transfers between devices: 7.3 us -> 10.4 us
    all_to_all x1 -> x0, blocking collectives: 10.2 us -> none  [exchange(): sent = lax.all_to_all(sent, AXES, split_axis=0, concat_axis=0, tiled=True)]
    all_to_all x1 -> x2, waiting for transfers between devices: 5.92 us -> 15.8 us  [exchange(): sent = lax.all_to_all(sent, AXES, split_axis=0, concat_axis=0, tiled=True)]
    pallas_call x3 -> x4, Pallas kernels: 19.3 us -> 14.8 us  [the longest x1 6.32 us: local(): call(local_kernel, [array(devices * TARGET, LANE), array(2 * SUB, LANE)],...]
    all_to_all x1 -> x2, starting transfers between devices: 7.3 us -> 10.4 us  [exchange(): sent = lax.all_to_all(sent, AXES, split_axis=0, concat_axis=0, tiled=True)]
  transfers between devices with their start and end apart: 1 -> 2, of which waited for: 1 -> 2; matrix products, arithmetic and copies ran while one was open for 0% -> 0% of each run, Pallas kernels for 19% -> 14%
where the time goes in v2:
time: 47.1 us; the launch traced here: 46.7 us
  Pallas kernels  15.8 us (34%)
  waiting for transfers between devices  15.8 us (34%)
  starting transfers between devices  10.4 us (22%)
  local copies, waits for them, and re-layouts  3.92 us (8%)
  between operations  0.77 us (2%)
    all_to_all x2, waiting for transfers between devices, exchange(): sent = lax.all_to_all(sent, AXES, split_axis=0, concat_axis=0, tiled=True)  15.8 us
    all_to_all x2, starting transfers between devices, exchange(): sent = lax.all_to_all(sent, AXES, split_axis=0, concat_axis=0, tiled=True)  10.4 us
    pallas_call x1, Pallas kernels, local(): call(local_kernel, [array(devices * TARGET, LANE), array(2 * SUB, LANE)],...  6.32 us
    pallas_call x1, Pallas kernels, local(): call(remote_kernel, [array(devices * 2, LANE), array(slots, 2 * LANE)], [...  6.06 us
    unnamed x24, local copies, waits for them, and re-layouts  3.92 us
    pallas_call x1, Pallas kernels, local(): call(pack_kernel, [array(devices * MSG, LANE)], [vmem(3, blocks, LANE), v...  2.16 us
    pallas_call x1, Pallas kernels, local(): call(functools.partial(final_kernel, per_frag=per_frag), [array(6, frags)...  0.99 us
  transfers between devices with their start and end apart: 2, of which 2 were waited for; matrix products, arithmetic and copies ran while one was open for 0% of the time, Pallas kernels for 14%

profile of v2, /device:TPU:0, one launch (start us, length us, event | category | flops | bytes accessed | tf_op | source)
XLA Modules:
  0.0 46.7 jit_solution(16589887641705358465)
XLA Ops:
  0.6 0.0 copy-start.7
  0.6 0.0 copy-start.9
  0.7 0.0 copy-start.11
  0.7 0.7 %copy-done.7 = f32[6,8]{1,0:T(8,128)S(1)} copy-done((f32[6,8]{1,0:T(8,128)S(1)}, f32[6,8]{1,0:T(8,128)}, u32[]{:S(2)}) %copy-start.7) | copy-done | bytes 216
  1.3 0.0 copy-done.9
  1.3 0.0 copy-done.11
  1.3 0.0 copy-start
  1.3 1.0 %copy-done = f32[256,3,128]{2,0,1:T(8,128)S(1)} copy-done((f32[256,3,128]{2,0,1:T(8,128)S(1)}, f32[256,3,128]{2,0,1:T(8,128)}, u32[]{:S(2)}) %copy-start) | copy-done | bytes 393240
  2.3 0.0 copy-start.3
  2.3 0.9 %copy-done.3 = s32[1,256,128]{2,1,0:T(8,128)S(1)} copy-done((s32[1,256,128]{2,1,0:T(8,128)S(1)}, s32[1,256,128]{2,1,0:T(8,128)}, u32[]{:S(2)}) %copy-start.3) | copy-done | bytes 131096
  3.2 0.0 copy-start.5
  3.2 0.7 %copy-done.5 = f32[2,6,8]{2,0,1:T(2,128)S(1)} copy-done((f32[2,6,8]{2,0,1:T(2,128)S(1)}, f32[2,6,8]{2,0,1:T(2,128)}, u32[]{:S(2)}) %copy-start.5) | copy-done | bytes 408
  3.9 2.2 %shard_map.113 = f32[1056,128]{1,0:T(8,128)} custom-call(f32[3,256,128]{2,1,0:T(8,128)S(1)} %bitcast.10, f32[6,8]{1,0:T(8,128)S(1)} %copy-done.7, f32[6,2,8]{2,1,0:T(2,128)S(1)} %bitcast.15, s32[1,256]{1,0:T(1,128)S(1)} %copy-done.9, s32[256,128]{1,0:T(8,128)S(1)} %bitcast.13, s32[1,32]{1,0:T(1,128)S(1)} %copy-done.11), custom_call_target="tpu_custom_call" | custom-call | tf_op jit(solution)/shard_map/pallas_call | solution.py:359
  6.1 0.0 copy-start.1
  6.1 0.0 copy-start.2
  6.1 0.0 copy-start.4
  6.1 0.0 copy-start.6
  6.1 0.0 copy-start.8
  6.1 7.3 %all-to-all-start = ((f32[32,1,4224]{2,1,0:T(1,128)}), f32[32,1,4224]{2,1,0:T(1,128)S(1)}, u32[]{:S(2)}, u32[]{:S(2)}) async-start(f32[32,1,4224]{2,1,0:T(1,128)} %bitcast.3), calls=%async_computation | async-start | bytes 1081344 | tf_op jit(solution)/shard_map/all_to_all | solution.py:332
  13.5 0.0 copy-start.10
  13.5 0.0 copy-done.1
  13.5 0.0 copy-done.2
  13.5 0.0 copy-done.4
  13.5 0.0 copy-done.6
  13.5 0.0 copy-done.8
  13.5 0.6 %copy-done.10 = s32[1,256]{1,0:T(1,128)S(1)} copy-done((s32[1,256]{1,0:T(1,128)S(1)}, s32[1,256]{1,0:T(1,128)}, u32[]{:S(2)}) %copy-start.10) | copy-done | bytes 1048
  14.1 6.3 %shard_map.114 = (f32[2048,128]{1,0:T(8,128)S(1)}, f32[16,128]{1,0:T(8,128)S(1)}) custom-call(f32[3,256,128]{2,1,0:T(8,128)S(1)} %bitcast.11, f32[3,256,128]{2,1,0:T(8,128)S(1)} %bitcast.12, f32[6,8]{1,0:T(8,128)S(1)} %copy-done.7, f32[6,2,8]{2,1,0:T(2,128)S(1)} %bitcast.16, s32[2,256]{1,0:T(2,128)S(1)} %copy-done.8, s32[2,256]{1,0:T(2,128)S(1)} %copy-done.8, ...), custom_call_target="tpu_custom_call" | custom-call | flops 6553600 | bytes 4000000 | tf_op jit(solution)/shard_map/pallas_call | solution.py:377
  20.5 8.8 %all-to-all-done = f32[32,1,4224]{2,1,0:T(1,128)S(1)} async-done(((f32[32,1,4224]{2,1,0:T(1,128)}), f32[32,1,4224]{2,1,0:T(1,128)S(1)}, u32[]{:S(2)}, u32[]{:S(2)}) %all-to-all-start) | async-done | bytes 540704 | tf_op jit(solution)/shard_map/all_to_all | solution.py:332
  29.3 6.1 %shard_map.115 = (f32[64,128]{1,0:T(8,128)}, f32[256,256]{1,0:T(8,128)S(1)}) custom-call(f32[1056,128]{1,0:T(8,128)S(1)} %bitcast.9, f32[2048,128]{1,0:T(8,128)S(1)} %get-tuple-element.8.staged), custom_call_target="tpu_custom_call" | custom-call | tf_op jit(solution)/shard_map/pallas_call | solution.py:391
  35.4 3.1 %all-to-all-start.1 = ((f32[32,1,256]{2,1,0:T(1,128)}), f32[32,1,256]{2,1,0:T(1,128)S(1)}, u32[]{:S(2)}, u32[]{:S(2)}) async-start(f32[32,1,256]{2,1,0:T(1,128)} %bitcast.6), calls=%async_computation.1 | async-start | bytes 65536 | tf_op jit(solution)/shard_map/all_to_all | solution.py:332
  38.5 0.3 shard_map.116.totals
  38.8 7.0 %all-to-all-done.1 = f32[32,1,256]{2,1,0:T(1,128)S(1)} async-done(((f32[32,1,256]{2,1,0:T(1,128)}), f32[32,1,256]{2,1,0:T(1,128)S(1)}, u32[]{:S(2)}, u32[]{:S(2)}) %all-to-all-start.1) | async-done | bytes 32800 | tf_op jit(solution)/shard_map/all_to_all | solution.py:332
  45.7 1.0 %shard_map.117 = (f32[6,8]{1,0:T(8,128)}, f32[6,2,8]{2,1,0:T(2,128)}) custom-call(f32[64,128]{1,0:T(8,128)S(1)} %bitcast.14, f32[16,128]{1,0:T(8,128)S(1)} %shard_map.116.totals, s32[1,256]{1,0:T(1,128)S(1)} %copy-done.9), custom_call_target="tpu_custom_call" | custom-call | tf_op jit(solution)/shard_map/pallas_call | solution.py:404
Async XLA Ops:
  0.6 0.7 %copy-start.7 = (f32[6,8]{1,0:T(8,128)S(1)}, f32[6,8]{1,0:T(8,128)}, u32[]{:S(2)}) copy-start(f32[6,8]{1,0:T(8,128)} %poses.1) | copy-start | bytes 580
  0.6 0.7 %copy-start.9 = (s32[1,256]{1,0:T(1,128)S(1)}, s32[1,256]{1,0:T(1,128)}, u32[]{:S(2)}) copy-start(s32[1,256]{1,0:T(1,128)} %src_v.1) | copy-start | bytes 3076
  0.7 0.7 %copy-start.11 = (s32[1,32]{1,0:T(1,128)S(1)}, s32[1,32]{1,0:T(1,128)}, u32[]{:S(2)}) copy-start(s32[1,32]{1,0:T(1,128)} %counts_h.1) | copy-start | bytes 388
  1.3 1.0 %copy-start = (f32[256,3,128]{2,0,1:T(8,128)S(1)}, f32[256,3,128]{2,0,1:T(8,128)}, u32[]{:S(2)}) copy-start(f32[256,3,128]{2,0,1:T(8,128)} %param.10) | copy-start | bytes 1179652
  2.3 0.9 %copy-start.3 = (s32[1,256,128]{2,1,0:T(8,128)S(1)}, s32[1,256,128]{2,1,0:T(8,128)}, u32[]{:S(2)}) copy-start(s32[1,256,128]{2,1,0:T(8,128)} %param.17) | copy-start | bytes 393220
  3.2 0.7 %copy-start.5 = (f32[2,6,8]{2,0,1:T(2,128)S(1)}, f32[2,6,8]{2,0,1:T(2,128)}, u32[]{:S(2)}) copy-start(f32[2,6,8]{2,0,1:T(2,128)} %param.13) | copy-start | bytes 1156
  6.1 7.4 %copy-start.1 = (f32[256,3,128]{2,0,1:T(8,128)S(1)}, f32[256,3,128]{2,0,1:T(8,128)}, u32[]{:S(2)}) copy-start(f32[256,3,128]{2,0,1:T(8,128)} %param.10) | copy-start | bytes 1179652
  6.1 7.4 %copy-start.2 = (f32[256,3,128]{2,0,1:T(8,128)S(1)}, f32[256,3,128]{2,0,1:T(8,128)}, u32[]{:S(2)}) copy-start(f32[256,3,128]{2,0,1:T(8,128)} %param.11) | copy-start | bytes 1179652
  6.1 7.4 %copy-start.4 = (s32[256,128]{1,0:T(8,128)S(1)}, s32[256,128]{1,0:T(8,128)}, u32[]{:S(2)}) copy-start(s32[256,128]{1,0:T(8,128)} %maps.1) | copy-start | bytes 393220
  6.1 7.4 %copy-start.6 = (f32[2,6,8]{2,0,1:T(2,128)S(1)}, f32[2,6,8]{2,0,1:T(2,128)}, u32[]{:S(2)}) copy-start(f32[2,6,8]{2,0,1:T(2,128)} %param.13) | copy-start | bytes 1156
  6.1 7.4 %copy-start.8 = (s32[2,256]{1,0:T(2,128)S(1)}, s32[2,256]{1,0:T(2,128)}, u32[]{:S(2)}) copy-start(s32[2,256]{1,0:T(2,128)} %pairs_v.1) | copy-start | bytes 6148
  6.1 23.2 %all-to-all-start = ((f32[32,1,4224]{2,1,0:T(1,128)}), f32[32,1,4224]{2,1,0:T(1,128)S(1)}, u32[]{:S(2)}, u32[]{:S(2)}) async-start(f32[32,1,4224]{2,1,0:T(1,128)} %bitcast.3), calls=%async_computation | async-start | bytes 1081344 | tf_op jit(solution)/shard_map/all_to_all | solution.py:332
  13.5 0.7 %copy-start.10 = (s32[1,256]{1,0:T(1,128)S(1)}, s32[1,256]{1,0:T(1,128)}, u32[]{:S(2)}) copy-start(s32[1,256]{1,0:T(1,128)} %dst_v.1) | copy-start | bytes 3076
  35.4 10.4 %all-to-all-start.1 = ((f32[32,1,256]{2,1,0:T(1,128)}), f32[32,1,256]{2,1,0:T(1,128)S(1)}, u32[]{:S(2)}, u32[]{:S(2)}) async-start(f32[32,1,256]{2,1,0:T(1,128)} %bitcast.6), calls=%async_computation.1 | async-start | bytes 65536 | tf_op jit(solution)/shard_map/all_to_all | solution.py:332

commit v3 on v2

--- a/solution.py
+++ b/solution.py
@@ -16,6 +16,8 @@
 TOGETHER = 4
 GROUP = 16
 VMEM_LIMIT = 16 * 1024 * 1024
+PACK_LIMIT = 60 * 1024 * 1024
+PEERS = 32
 
 
 def iota(axis):
@@ -61,13 +63,23 @@
     return jnp.broadcast_to(row[:, f : f + 1], (SUB, LANE))
 
 
+def splat_rotation(poses, f):
+    half = [jnp.full((SUB, LANE), poses[i, f] * 0.5, jnp.float32) for i in range(3)]
+    w = 1.0 / jnp.sqrt(1.0 + half[0] * half[0] + half[1] * half[1] + half[2] * half[2])
+    x, y, z = half[0] * w, half[1] * w, half[2] * w
+    rotation = [
+        [1.0 - 2.0 * (y * y + z * z), 2.0 * (x * y - w * z), 2.0 * (x * z + w * y)],
+        [2.0 * (x * y + w * z), 1.0 - 2.0 * (x * x + z * z), 2.0 * (y * z - w * x)],
+        [2.0 * (x * z - w * y), 2.0 * (y * z + w * x), 1.0 - 2.0 * (x * x + y * y)],
+    ]
+    return rotation, [jnp.full((SUB, LANE), poses[i, f], jnp.float32) for i in range(3, 6)]
+
+
 def write_points(points, poses, world):
     blocks, frags = points.shape[1], poses.shape[1]
     per_frag, stride = blocks // frags, blocks + SUB
-    rotation, translation = rotations(poses[...])
     for f in range(frags):
-        turn = [[spread(rotation[i][j], f) for j in range(3)] for i in range(3)]
-        move = [spread(translation[i], f) for i in range(3)]
+        turn, move = splat_rotation(poses, f)
         for b in range(f * per_frag, (f + 1) * per_frag, SUB):
             x = [points[j, b : b + SUB, :] for j in range(3)]
             for i in range(3):
@@ -102,41 +114,26 @@
 
 
 def pack_kernel(
-    points_h, poses_h, directions_h, src_h, maps_h, counts_h, out,
-    points, poses, directions, src_s, src_v, maps, used, world, table, sems,
+    points_h, poses_h, directions_h, src_h, maps_h, counts_h, out_h,
+    points, poses, directions, src_s, src_v, maps, used, world, table, out, sems, out_sems,
 ):
     devices = counts_h.shape[1]
     per_frag = points.shape[1] // poses.shape[1]
     stride = points.shape[1] + SUB
     pairs = [
-        (poses_h, poses), (points_h, points), (src_h, src_s), (maps_h, maps),
-        (directions_h, directions), (src_h, src_v), (counts_h, used),
+        (directions_h, directions), (src_h, src_v), (counts_h, used), (poses_h, poses),
+        (points_h, points), (src_h, src_s), (maps_h, maps),
     ]
     copies = [pltpu.make_async_copy(a, b, sems.at[i]) for i, (a, b) in enumerate(pairs)]
     for copy in copies:
         copy.start()
-    copies[0].wait()
-    copies[1].wait()
-    write_points(points, poses, world)
-    copies[2].wait()
-    copies[3].wait()
-
-    def peer(p, carry):
-        for s in range(SUB):
-            block = src_s[0, p * SUB + s]
-            out[pl.ds(p * MSG + s, 3, stride=SUB), :] = world[pl.ds(block, 3, stride=stride), :]
-        rows = maps[pl.ds(pl.multiple_of(p * SUB, SUB), SUB), :]
-        out[pl.ds(p * MSG + 3 * SUB, SUB), :] = rows.astype(jnp.float32)
-        return carry
-
-    lax.fori_loop(0, devices, peer, 0, unroll=4)
-    for copy in copies[4:]:
+    for copy in copies[0:3]:
         copy.wait()
     frags = directions.shape[2]
     for v in range(2):
         for j in range(6):
             table[6 * v + j : 6 * v + j + 1, 0:frags] = directions[j, v : v + 1, :]
-    limits = jnp.broadcast_to(used[0:1, :], (SUB, devices))
+    limits = jnp.broadcast_to(used[0:1, :], (SUB, devices)).astype(jnp.float32)
     peers = lax.broadcasted_iota(jnp.int32, (SUB, devices), 1)
     row = lax.broadcasted_iota(jnp.int32, (SUB, devices), 0)
     slot = lax.shift_right_logical(iota(1), shift_of(GROUP))
@@ -144,13 +141,35 @@
     for q in range(0, devices, SUB):
         block = index_tile(src_v, q * SUB, iota(0) * SUB + slot)
         frag = lax.shift_right_logical(block, shift_of(per_frag))
-        limit = jnp.sum(
-            jnp.where(peers == row + q, limits.astype(jnp.float32), 0.0), axis=1, keepdims=True
-        )
+        limit = jnp.sum(jnp.where(peers == row + q, limits, 0.0), axis=1, keepdims=True)
         extras = jnp.where(slot.astype(jnp.float32) < limit, 1.0, 0.0)
         for j in range(12):
             extras = jnp.where(field == j, pick(table[j : j + 1, :], frag), extras)
         out[pl.ds(q * MSG + MSG - 1, SUB, stride=MSG), :] = extras
+    for copy in copies[3:]:
+        copy.wait()
+    write_points(points, poses, world)
+
+    def peer(p):
+        for s in range(SUB):
+            block = src_s[0, p * SUB + s]
+            out[pl.ds(p * MSG + s, 3, stride=SUB), :] = world[pl.ds(block, 3, stride=stride), :]
+        rows = maps[pl.ds(pl.multiple_of(p * SUB, SUB), SUB), :]
+        out[pl.ds(p * MSG + 3 * SUB, SUB), :] = rows.astype(jnp.float32)
+
+    def piece(i):
+        rows = pl.ds(pl.multiple_of(i * SUB * MSG, SUB), SUB * MSG)
+        return pltpu.make_async_copy(out.at[rows], out_h.at[rows], out_sems.at[i])
+
+    def pack(i, carry):
+        for u in range(SUB):
+            peer(i * SUB + u)
+        piece(i).start()
+        return carry
+
+    lax.fori_loop(0, devices // SUB, pack, 0)
+    for i in range(devices // SUB):
+        piece(i).wait()
 
 
 def pair_sums(scalars, p, n, q):
@@ -242,52 +261,140 @@
         totals[half * SUB : (half + 1) * SUB, :] = side_a[half] + side_b[half]
 
 
-def remote_kernel(arrived, staged, back, sums):
-    devices = arrived.shape[0] // MSG
+def halves_of(values):
+    high = values.astype(jnp.bfloat16)
+    return high, (values - high.astype(jnp.float32)).astype(jnp.bfloat16)
+
+
+def remote_kernel(arrived, staged, back, sums, parts, turned, coeffs, index, partial):
+    bf16, f32 = jnp.bfloat16, jnp.float32
+    pairs = parts.shape[0]
+    peers = pairs // SUB
+    nums = lax.dot_general
+
+    def wide(shape, axis):
+        return lax.broadcasted_iota(jnp.int32, shape, axis)
+
+    points2 = lax.bitwise_and(wide((LANE, 2 * LANE), 1), LANE - 1)
+    same = (points2 == wide((LANE, 2 * LANE), 0)).astype(f32).astype(bf16)
+    fields2 = lax.bitwise_and(wide((GROUP, 2 * LANE), 1), GROUP - 1)
+    gather = (fields2 == wide((GROUP, 2 * LANE), 0)).astype(f32).astype(bf16)
     own = lax.shift_right_logical(iota(1), shift_of(GROUP)) == iota(0)
-
-    def step(i, carry):
-        done = []
-        for u in range(TOGETHER):
-            d = i * TOGETHER + u
-            x = [arrived[pl.ds(d * MSG + SUB * k, SUB), :] for k in range(3)]
-            index = arrived[pl.ds(d * MSG + 3 * SUB, SUB), :].astype(jnp.int32)
-            extras = arrived[pl.ds(d * MSG + 4 * SUB, 1), :]
-            base = pl.multiple_of(d * TARGET, SUB)
-            target = [pick(staged[pl.ds(base + SUB * k, SUB), :], index) for k in range(8)]
-            way = [pick(extras, iota(0) * GROUP + j) for j in range(13)]
-            y, n = target[0:3], target[3:6]
-            p = cross(x, n)
-            scalars = [dot3(n, [x[k] - y[k] for k in range(3)])]
-            for v in range(2):
-                a = way[6 * v : 6 * v + 6]
-                scalars.append(dot3(p, a[0:3]) + dot3(n, a[3:6]) - target[6 + v])
-            scalars = [s * way[12] for s in scalars]
-            done.append(pair_sums(scalars, p, n, cross(y, n)))
-        rows = [
-            [jnp.sum(jnp.where(own, tile, 0.0), axis=0, keepdims=True) for tile in tiles]
-            for tiles in done
-        ]
-        for u in range(TOGETHER):
-            d = i * TOGETHER + u
-            for half in range(2):
-                back[pl.ds(2 * d + half, 1), :] = rows[u][half]
-                sums[pl.ds(pl.multiple_of(d * SUB, SUB), SUB), half * LANE : (half + 1) * LANE] = done[
-                    u
-                ][half]
+    partial[27 * SUB :, :] = jnp.zeros((partial.shape[0] - 27 * SUB, LANE), f32)
+
+    def block(c, carry):
+        first = c * peers
+
+        def turn(i, left, at):
+            for u in range(0, peers, 2):
+                both = jnp.concatenate([at(u), at(u + 1)], axis=0)
+                high, low = halves_of(both)
+                parts[u * SUB : (u + 2) * SUB, i * 2 * LANE : i * 2 * LANE + LANE] = high
+                parts[u * SUB : (u + 2) * SUB, i * 2 * LANE + LANE : (i + 1) * 2 * LANE] = low
+            return nums(
+                left,
+                parts[:, i * 2 * LANE : (i + 1) * 2 * LANE],
+                (((1,), (1,)), ((), ())),
+                preferred_element_type=f32,
+            )
+
+        for u in range(peers):
+            row = (first + u) * MSG + 3 * SUB
+            index[u * SUB : (u + 1) * SUB, :] = arrived[pl.ds(row, SUB), :].astype(jnp.int32)
+
+        def extras(u):
+            row = arrived[pl.ds((first + u) * MSG + 4 * SUB, 1), :]
+            return jnp.where(own, jnp.broadcast_to(row, (SUB, LANE)), 0.0)
+
+        def target(k):
+            def at(u):
+                base = pl.multiple_of((first + u) * TARGET, SUB)
+                return pick(staged[pl.ds(base + SUB * k, SUB), :], index[u * SUB : (u + 1) * SUB, :])
+
+            return at
+
+        def source(k):
+            return lambda u: arrived[pl.ds((first + u) * MSG + SUB * k, SUB), :]
+
+        coeffs[...] = turn(11, gather, extras)
+        for k in range(8):
+            turned[k * LANE : (k + 1) * LANE, :] = turn(k, same, target(k))
+        for k in range(3):
+            turned[(8 + k) * LANE : (9 + k) * LANE, :] = turn(8 + k, same, source(k))
+        for t in range(0, pairs, LANE):
+            lanes = slice(t, t + LANE)
+
+            def add(i, totals):
+                start = pl.multiple_of(i * SUB, SUB)
+                field = [turned[pl.ds(start + k * LANE, SUB), lanes] for k in range(11)]
+                way = [coeffs[j : j + 1, lanes] for j in range(12)]
+                y, n, x = field[0:3], field[3:6], field[8:11]
+                p, q = cross(x, n), cross(y, n)
+                scalars = [dot3(n, [x[k] - y[k] for k in range(3)])]
+                for v in range(2):
+                    a = way[6 * v : 6 * v + 6]
+                    scalars.append(dot3(p, a[0:3]) + dot3(n, a[3:6]) - field[6 + v])
+                terms = []
+                for s in scalars:
+                    terms += [s * value for value in p + n]
+                for s in scalars:
+                    terms += [s * value for value in q]
+                return tuple(total + term for total, term in zip(totals, terms))
+
+            zero = jnp.zeros((SUB, LANE), f32)
+            totals = lax.fori_loop(0, LANE // SUB, add, (zero,) * 27, unroll=4)
+            for j in range(27):
+                partial[j * SUB : (j + 1) * SUB, :] = totals[j]
+            total = partial[pl.ds(0, 4 * SUB, stride=SUB), :]
+            for s in range(1, SUB):
+                total = total + partial[pl.ds(s, 4 * SUB, stride=SUB), :]
+            at = pl.multiple_of(c * pairs, LANE) + t
+            sums[:, pl.ds(at, LANE)] = total * coeffs[12:13, lanes]
+        start = pl.multiple_of(c * pairs, LANE)
+        high, low = halves_of(sums[:, pl.ds(start, pairs)])
+        entry = wide((8 * SUB, 2 * LANE), 1)
+        entry = lax.bitwise_and(entry, GROUP - 1) + GROUP * lax.shift_right_logical(entry, 7)
+        place = (lax.bitwise_and(wide((8 * SUB, 2 * LANE), 0), 4 * SUB - 1) == entry).astype(f32)
+        rows = nums(
+            jnp.concatenate([high, low], axis=0),
+            place.astype(bf16),
+            (((0,), (0,)), ((), ())),
+            preferred_element_type=f32,
+        )
+        slot = lax.bitwise_and(wide((pairs, 2 * LANE), 0), SUB - 1)
+        lane = lax.bitwise_and(wide((pairs, 2 * LANE), 1), LANE - 1)
+        high, low = halves_of(jnp.where(lax.shift_right_logical(lane, 4) == slot, rows, 0.0))
+        mine = lax.shift_right_logical(wide((peers, pairs), 1), 3) == wide((peers, pairs), 0)
+        mine = mine.astype(f32).astype(bf16)
+        rows = jnp.dot(mine, high, preferred_element_type=f32) + jnp.dot(
+            mine, low, preferred_element_type=f32
+        )
+        for half in range(2):
+            back[pl.ds(2 * first + half, peers, stride=2), :] = rows[
+                :, half * LANE : (half + 1) * LANE
+            ]
         return carry
 
-    lax.fori_loop(0, devices // TOGETHER, step, 0)
-
-
-def total_kernel(sums, dst_v, totals_in, totals, *, per_frag):
-    side_b = target_side(frag_sums(dst_v[...], sums, per_frag))
-    for half in range(2):
-        rows = slice(half * SUB, (half + 1) * SUB)
-        totals[rows, :] = totals_in[rows, :] + side_b[half]
-
-
-def final_kernel(back, totals, src_v, gradient, hess, *, per_frag):
+    lax.fori_loop(0, sums.shape[1] // pairs, block, 0)
+
+
+def total_kernel(sums, dst_v, totals, *, per_frag):
+    pairs = sums.shape[1]
+    frag = lax.shift_right_logical(dst_v[...], shift_of(per_frag))
+    hot = jnp.broadcast_to(frag, (SUB, pairs)) == lax.broadcasted_iota(jnp.int32, (SUB, pairs), 0)
+    total = -lax.dot_general(
+        sums[...],
+        hot.astype(jnp.float32),
+        (((1,), (1,)), ((), ())),
+        precision=lax.Precision.HIGHEST,
+        preferred_element_type=jnp.float32,
+    )
+    for k in range(3):
+        totals[6 * k : 6 * k + 3, :] = total[18 + 3 * k : 21 + 3 * k, :]
+        totals[6 * k + 3 : 6 * k + 6, :] = total[6 * k + 3 : 6 * k + 6, :]
+
+
+def final_kernel(back, totals, extra, src_v, gradient, hess, *, per_frag):
     devices = back.shape[0] // 2
     slot = lax.shift_right_logical(iota(1), shift_of(GROUP))
     sums = [[jnp.zeros((SUB, LANE), jnp.float32) for half in range(2)] for f in range(SUB)]
@@ -306,7 +413,7 @@
         for step in (64, 32, 16):
             tile = tile + pltpu.roll(tile, step, 1)
         halves.append(tile + totals[half * SUB : (half + 1) * SUB, :])
-    total = jnp.where(iota(1) < GROUP, halves[0], halves[1]).T
+    total = jnp.where(iota(1) < GROUP, halves[0], halves[1]).T[0:18, :] + extra[...]
     gradient[...] = total[0:6, :] * (1.0 / LANE)
     for v in range(2):
         part = total[6 + 6 * v : 12 + 6 * v, :] * (1.0 / (LANE * per_frag))
@@ -314,15 +421,15 @@
             hess[j, v : v + 1, :] = part[j : j + 1, :]
 
 
-def call(kernel, outs, scratch, spaces, **more):
+def call(kernel, outs, scratch, spaces, limit=VMEM_LIMIT, out_space="v", **more):
     kinds = {"v": pltpu.VMEM, "s": pltpu.SMEM, "h": pltpu.HBM}
     return pl.pallas_call(
         kernel,
         out_shape=outs,
         in_specs=[pl.BlockSpec(memory_space=kinds[s]) for s in spaces],
-        out_specs=[pl.BlockSpec(memory_space=pltpu.VMEM)] * len(outs),
+        out_specs=[pl.BlockSpec(memory_space=kinds[out_space])] * len(outs),
         scratch_shapes=scratch,
-        compiler_params=pltpu.CompilerParams(vmem_limit_bytes=VMEM_LIMIT),
+        compiler_params=pltpu.CompilerParams(vmem_limit_bytes=limit),
         **more,
     )
 
@@ -342,7 +449,7 @@
     frags = poses.shape[1]
     slots = remote_src.shape[1]
     pairs = local_pairs.shape[1]
-    assert count == LANE and frags == SUB and slots == devices * SUB and devices <= LANE
+    assert count == LANE and frags == SUB and slots == devices * SUB and devices % PEERS == 0
     per_frag = blocks // frags
     stride = blocks + SUB
     f32 = jnp.float32
@@ -361,7 +468,7 @@
         [array(devices * MSG, LANE)],
         [
             vmem(3, blocks, LANE),
-            vmem(6, frags),
+            pltpu.SMEM((6, frags), f32),
             vmem(6, 2, frags),
             pltpu.SMEM((1, slots), jnp.int32),
             vmem(1, slots, dtype=jnp.int32),
@@ -369,9 +476,13 @@
             vmem(1, devices, dtype=jnp.int32),
             vmem(3 * stride, LANE),
             vmem(2 * SUB, LANE),
+            vmem(devices * MSG, LANE),
             pltpu.SemaphoreType.DMA((7,)),
+            pltpu.SemaphoreType.DMA((devices // SUB,)),
         ],
         "hhhhhh",
+        limit=PACK_LIMIT,
+        out_space="h",
     )(points, poses, directions, remote_src, remote_maps[0], counts)
     arrived = exchange(message, devices)
     staged, totals = call(
@@ -388,25 +499,35 @@
             flops=200 * pairs * LANE, bytes_accessed=4_000_000, transcendentals=0
         ),
     )(points, normals, poses, directions, local_pairs, local_pairs, local_maps, remote_dst)
+    part = PEERS * SUB
     back, sums = call(
-        remote_kernel, [array(devices * 2, LANE), array(slots, 2 * LANE)], [], "vv"
+        remote_kernel,
+        [array(devices * 2, LANE), array(4 * SUB, slots)],
+        [
+            vmem(part, 12 * 2 * LANE, dtype=jnp.bfloat16),
+            vmem(11 * LANE, part),
+            vmem(GROUP, part),
+            vmem(part, LANE, dtype=jnp.int32),
+            vmem(4 * SUB * SUB, LANE),
+        ],
+        "vv",
     )(arrived, staged)
     back = exchange(back, devices)
-    (totals,) = call(
+    (extra,) = call(
         functools.partial(total_kernel, per_frag=per_frag),
-        [array(2 * SUB, LANE)],
+        [array(18, frags)],
         [],
-        "vvv",
+        "vv",
         cost_estimate=pl.CostEstimate(
             flops=2 * SUB * slots * 2 * LANE, bytes_accessed=1_000_000, transcendentals=0
         ),
-    )(sums, remote_dst, totals)
+    )(sums, remote_dst)
     gradient, hess = call(
         functools.partial(final_kernel, per_frag=per_frag),
         [array(6, frags), array(6, 2, frags)],
         [],
-        "vvv",
-    )(back, totals, remote_src)
+        "vvvv",
+    )(back, totals, extra, remote_src)
     return (gradient, hess.transpose(1, 0, 2))
 
 

time: 47.1 us -> 41 us (0.87)
  Pallas kernels: 15.8 us -> 12.3 us
  local copies, waits for them, and re-layouts: 3.92 us -> 1.33 us
    pallas_call x3, Pallas kernels: 8.5 us -> 4.99 us  [the longest x1 2.6 us: local(): call(remote_kernel, [array(devices * 2, LANE), array(4 * SUB, slots)], [v...]
    unnamed x24 -> x16, local copies, waits for them, and re-layouts: 3.92 us -> 1.33 us
  transfers between devices with their start and end apart: 2 -> 2, of which waited for: 2 -> 2; matrix products, arithmetic and copies ran while one was open for 0% -> 0% of each run, Pallas kernels for 14% -> 16%
where the time goes in v3:
time: 41 us; the launch traced here: 40.8 us
  waiting for transfers between devices  15.9 us (39%)
  Pallas kernels  12.3 us (30%)
  starting transfers between devices  10.4 us (25%)
  local copies, waits for them, and re-layouts  1.33 us (3%)
  between operations  0.77 us (2%)
    all_to_all x2, waiting for transfers between devices, exchange(): sent = lax.all_to_all(sent, AXES, split_axis=0, concat_axis=0, tiled=True)  15.9 us
    all_to_all x2, starting transfers between devices, exchange(): sent = lax.all_to_all(sent, AXES, split_axis=0, concat_axis=0, tiled=True)  10.4 us
    pallas_call x1, Pallas kernels, local(): call(local_kernel, [array(devices * TARGET, LANE), array(2 * SUB, LANE)],...  6.32 us
    pallas_call x1, Pallas kernels, local(): call(remote_kernel, [array(devices * 2, LANE), array(4 * SUB, slots)], [v...  2.6 us
    pallas_call x1, Pallas kernels, local(): call(pack_kernel, [array(devices * MSG, LANE)], [vmem(3, blocks, LANE), p...  2.23 us
    unnamed x16, local copies, waits for them, and re-layouts  1.33 us
    pallas_call x1, Pallas kernels, local(): call(functools.partial(final_kernel, per_frag=per_frag), [array(6, frags)...  0.99 us
  transfers between devices with their start and end apart: 2, of which 2 were waited for; matrix products, arithmetic and copies ran while one was open for 0% of the time, Pallas kernels for 16%

profile of v3, /device:TPU:0, one launch (start us, length us, event | category | flops | bytes accessed | tf_op | source)
XLA Modules:
  0.0 40.8 jit_solution(11033056366938540754)
XLA Ops:
  0.6 2.2 %shard_map.113 = f32[1056,128]{1,0:T(8,128)} custom-call(f32[3,256,128]{2,1,0:T(8,128)} %bitcast.10, f32[6,8]{1,0:T(8,128)} %poses.1, f32[6,2,8]{2,1,0:T(2,128)} %bitcast.14, s32[1,256]{1,0:T(1,128)} %src_v.1, s32[256,128]{1,0:T(8,128)} %bitcast.17, s32[1,32]{1,0:T(1,128)} %counts_h.1), custom_call_target="tpu_custom_call" | custom-call | tf_op jit(solution)/shard_map/pallas_call | solution.py:466
  2.9 0.0 copy-start
  2.9 0.0 copy-start.1
  2.9 0.0 copy-start.2
  2.9 0.0 copy-start.3
  2.9 0.0 copy-start.4
  2.9 0.0 copy-start.5
  2.9 7.3 %all-to-all-start = ((f32[32,1,4224]{2,1,0:T(1,128)}), f32[32,1,4224]{2,1,0:T(1,128)S(1)}, u32[]{:S(2)}, u32[]{:S(2)}) async-start(f32[32,1,4224]{2,1,0:T(1,128)} %bitcast.16), calls=%async_computation | async-start | bytes 1081344 | tf_op jit(solution)/shard_map/all_to_all | solution.py:439
  10.3 0.0 copy-start.7
  10.3 0.0 copy-done
  10.3 0.0 copy-done.1
  10.3 0.0 copy-done.2
  10.3 0.0 copy-done.3
  10.3 0.0 copy-done.4
  10.3 0.0 copy-done.5
  10.3 0.6 %copy-done.7 = s32[1,256]{1,0:T(1,128)S(1)} copy-done((s32[1,256]{1,0:T(1,128)S(1)}, s32[1,256]{1,0:T(1,128)}, u32[]{:S(2)}) %copy-start.7) | copy-done | bytes 1048
  10.9 6.3 %shard_map.114 = (f32[2048,128]{1,0:T(8,128)S(1)}, f32[16,128]{1,0:T(8,128)S(1)}) custom-call(f32[3,256,128]{2,1,0:T(8,128)S(1)} %bitcast.11, f32[3,256,128]{2,1,0:T(8,128)S(1)} %bitcast.12, f32[6,8]{1,0:T(8,128)S(1)} %copy-done.4, f32[6,2,8]{2,1,0:T(2,128)S(1)} %bitcast.15, s32[2,256]{1,0:T(2,128)S(1)} %copy-done.5, s32[2,256]{1,0:T(2,128)S(1)} %copy-done.5, ...), custom_call_target="tpu_custom_call" | custom-call | flops 6553600 | bytes 4000000 | tf_op jit(solution)/shard_map/pallas_call | solution.py:488
  17.3 8.8 %all-to-all-done = f32[32,1,4224]{2,1,0:T(1,128)S(1)} async-done(((f32[32,1,4224]{2,1,0:T(1,128)}), f32[32,1,4224]{2,1,0:T(1,128)S(1)}, u32[]{:S(2)}, u32[]{:S(2)}) %all-to-all-start) | async-done | bytes 540704 | tf_op jit(solution)/shard_map/all_to_all | solution.py:439
  26.1 2.6 %shard_map.115 = (f32[64,128]{1,0:T(8,128)}, f32[32,256]{1,0:T(8,128)S(1)}) custom-call(f32[1056,128]{1,0:T(8,128)S(1)} %bitcast.9, f32[2048,128]{1,0:T(8,128)S(1)} %get-tuple-element.8.staged), custom_call_target="tpu_custom_call" | custom-call | tf_op jit(solution)/shard_map/pallas_call | solution.py:503
  28.7 3.1 %all-to-all-start.1 = ((f32[32,1,256]{2,1,0:T(1,128)}), f32[32,1,256]{2,1,0:T(1,128)S(1)}, u32[]{:S(2)}, u32[]{:S(2)}) async-start(f32[32,1,256]{2,1,0:T(1,128)} %bitcast.6), calls=%async_computation.1 | async-start | bytes 65536 | tf_op jit(solution)/shard_map/all_to_all | solution.py:439
  31.8 0.2 shard_map.116.extra
  32.0 7.1 %all-to-all-done.1 = f32[32,1,256]{2,1,0:T(1,128)S(1)} async-done(((f32[32,1,256]{2,1,0:T(1,128)}), f32[32,1,256]{2,1,0:T(1,128)S(1)}, u32[]{:S(2)}, u32[]{:S(2)}) %all-to-all-start.1) | async-done | bytes 32800 | tf_op jit(solution)/shard_map/all_to_all | solution.py:439
  39.1 0.0 copy-start.6
  39.1 0.7 %copy-done.6 = s32[1,256]{1,0:T(1,128)S(1)} copy-done((s32[1,256]{1,0:T(1,128)S(1)}, s32[1,256]{1,0:T(1,128)}, u32[]{:S(2)}) %copy-start.6) | copy-done | bytes 1048
  39.8 1.0 %shard_map.117 = (f32[6,8]{1,0:T(8,128)}, f32[6,2,8]{2,1,0:T(2,128)}) custom-call(f32[64,128]{1,0:T(8,128)S(1)} %bitcast.13, f32[16,128]{1,0:T(8,128)S(1)} %get-tuple-element.10.totals, f32[18,8]{1,0:T(8,128)S(1)} %shard_map.116.extra, s32[1,256]{1,0:T(1,128)S(1)} %copy-done.6), custom_call_target="tpu_custom_call" | custom-call | tf_op jit(solution)/shard_map/pallas_call | solution.py:525
Async XLA Ops:
  2.9 7.4 %copy-start = (f32[256,3,128]{2,0,1:T(8,128)S(1)}, f32[256,3,128]{2,0,1:T(8,128)}, u32[]{:S(2)}) copy-start(f32[256,3,128]{2,0,1:T(8,128)} %param.10) | copy-start | bytes 1179652
  2.9 7.4 %copy-start.1 = (f32[256,3,128]{2,0,1:T(8,128)S(1)}, f32[256,3,128]{2,0,1:T(8,128)}, u32[]{:S(2)}) copy-start(f32[256,3,128]{2,0,1:T(8,128)} %param.11) | copy-start | bytes 1179652
  2.9 7.4 %copy-start.2 = (s32[256,128]{1,0:T(8,128)S(1)}, s32[256,128]{1,0:T(8,128)}, u32[]{:S(2)}) copy-start(s32[256,128]{1,0:T(8,128)} %maps.1) | copy-start | bytes 393220
  2.9 7.4 %copy-start.3 = (f32[2,6,8]{2,0,1:T(2,128)S(1)}, f32[2,6,8]{2,0,1:T(2,128)}, u32[]{:S(2)}) copy-start(f32[2,6,8]{2,0,1:T(2,128)} %param.13) | copy-start | bytes 1156
  2.9 7.4 %copy-start.4 = (f32[6,8]{1,0:T(8,128)S(1)}, f32[6,8]{1,0:T(8,128)}, u32[]{:S(2)}) copy-start(f32[6,8]{1,0:T(8,128)} %poses.1) | copy-start | bytes 580
  2.9 7.4 %copy-start.5 = (s32[2,256]{1,0:T(2,128)S(1)}, s32[2,256]{1,0:T(2,128)}, u32[]{:S(2)}) copy-start(s32[2,256]{1,0:T(2,128)} %pairs_v.1) | copy-start | bytes 6148
  2.9 23.2 %all-to-all-start = ((f32[32,1,4224]{2,1,0:T(1,128)}), f32[32,1,4224]{2,1,0:T(1,128)S(1)}, u32[]{:S(2)}, u32[]{:S(2)}) async-start(f32[32,1,4224]{2,1,0:T(1,128)} %bitcast.16), calls=%async_computation | async-start | bytes 1081344 | tf_op jit(solution)/shard_map/all_to_all | solution.py:439
  10.3 0.7 %copy-start.7 = (s32[1,256]{1,0:T(1,128)S(1)}, s32[1,256]{1,0:T(1,128)}, u32[]{:S(2)}) copy-start(s32[1,256]{1,0:T(1,128)} %dst_v.1) | copy-start | bytes 3076
  28.7 10.4 %all-to-all-start.1 = ((f32[32,1,256]{2,1,0:T(1,128)}), f32[32,1,256]{2,1,0:T(1,128)S(1)}, u32[]{:S(2)}, u32[]{:S(2)}) async-start(f32[32,1,256]{2,1,0:T(1,128)} %bitcast.6), calls=%async_computation.1 | async-start | bytes 65536 | tf_op jit(solution)/shard_map/all_to_all | solution.py:439
  39.1 0.7 %copy-start.6 = (s32[1,256]{1,0:T(1,128)S(1)}, s32[1,256]{1,0:T(1,128)}, u32[]{:S(2)}) copy-start(s32[1,256]{1,0:T(1,128)} %src_v.1) | copy-start | bytes 3076

commit v4 on v3

--- a/solution.py
+++ b/solution.py
@@ -16,7 +16,7 @@
 TOGETHER = 4
 GROUP = 16
 VMEM_LIMIT = 16 * 1024 * 1024
-PACK_LIMIT = 60 * 1024 * 1024
+PACK_LIMIT = 56 * 1024 * 1024
 PEERS = 32
 
 
@@ -114,8 +114,8 @@
 
 
 def pack_kernel(
-    points_h, poses_h, directions_h, src_h, maps_h, counts_h, out_h,
-    points, poses, directions, src_s, src_v, maps, used, world, table, out, sems, out_sems,
+    points_h, poses_h, directions_h, src_h, maps_h, counts_h, out,
+    points, poses, directions, src_s, src_v, maps, used, world, table, sems,
 ):
     devices = counts_h.shape[1]
     per_frag = points.shape[1] // poses.shape[1]
@@ -157,19 +157,12 @@
         rows = maps[pl.ds(pl.multiple_of(p * SUB, SUB), SUB), :]
         out[pl.ds(p * MSG + 3 * SUB, SUB), :] = rows.astype(jnp.float32)
 
-    def piece(i):
-        rows = pl.ds(pl.multiple_of(i * SUB * MSG, SUB), SUB * MSG)
-        return pltpu.make_async_copy(out.at[rows], out_h.at[rows], out_sems.at[i])
-
     def pack(i, carry):
         for u in range(SUB):
             peer(i * SUB + u)
-        piece(i).start()
         return carry
 
     lax.fori_loop(0, devices // SUB, pack, 0)
-    for i in range(devices // SUB):
-        piece(i).wait()
 
 
 def pair_sums(scalars, p, n, q):
@@ -378,7 +371,11 @@
     lax.fori_loop(0, sums.shape[1] // pairs, block, 0)
 
 
-def total_kernel(sums, dst_v, totals, *, per_frag):
+def total_kernel(sums, dst_v, src_v, totals, frags, *, per_frag):
+    slot = lax.shift_right_logical(iota(1), shift_of(GROUP))
+    for q in range(0, frags.shape[0], SUB):
+        block = index_tile(src_v, q * SUB, iota(0) * SUB + slot)
+        frags[q : q + SUB, :] = lax.shift_right_logical(block, shift_of(per_frag))
     pairs = sums.shape[1]
     frag = lax.shift_right_logical(dst_v[...], shift_of(per_frag))
     hot = jnp.broadcast_to(frag, (SUB, pairs)) == lax.broadcasted_iota(jnp.int32, (SUB, pairs), 0)
@@ -394,13 +391,11 @@
         totals[6 * k + 3 : 6 * k + 6, :] = total[6 * k + 3 : 6 * k + 6, :]
 
 
-def final_kernel(back, totals, extra, src_v, gradient, hess, *, per_frag):
+def final_kernel(back, totals, extra, frags, gradient, hess, *, per_frag):
     devices = back.shape[0] // 2
-    slot = lax.shift_right_logical(iota(1), shift_of(GROUP))
     sums = [[jnp.zeros((SUB, LANE), jnp.float32) for half in range(2)] for f in range(SUB)]
     for q in range(0, devices, SUB):
-        block = index_tile(src_v, q * SUB, iota(0) * SUB + slot)
-        frag = lax.shift_right_logical(block, shift_of(per_frag))
+        frag = frags[q : q + SUB, :]
         for half in range(2):
             rows = back[pl.ds(2 * q + half, SUB, stride=2), :]
             for f in range(SUB):
@@ -421,17 +416,21 @@
             hess[j, v : v + 1, :] = part[j : j + 1, :]
 
 
-def call(kernel, outs, scratch, spaces, limit=VMEM_LIMIT, out_space="v", **more):
+def call(kernel, outs, scratch, spaces, limit=VMEM_LIMIT, **more):
     kinds = {"v": pltpu.VMEM, "s": pltpu.SMEM, "h": pltpu.HBM}
     return pl.pallas_call(
         kernel,
         out_shape=outs,
         in_specs=[pl.BlockSpec(memory_space=kinds[s]) for s in spaces],
-        out_specs=[pl.BlockSpec(memory_space=kinds[out_space])] * len(outs),
+        out_specs=[pl.BlockSpec(memory_space=pltpu.VMEM)] * len(outs),
         scratch_shapes=scratch,
         compiler_params=pltpu.CompilerParams(vmem_limit_bytes=limit),
         **more,
     )
+
+
+def in_hbm(values):
+    return pltpu.with_memory_space_constraint(values, pltpu.HBM)
 
 
 def exchange(rows, devices):
@@ -465,7 +464,7 @@
 
     (message,) = call(
         pack_kernel,
-        [array(devices * MSG, LANE)],
+        [pltpu.VMEM((devices * MSG, LANE), f32)],
         [
             vmem(3, blocks, LANE),
             pltpu.SMEM((6, frags), f32),
@@ -476,14 +475,11 @@
             vmem(1, devices, dtype=jnp.int32),
             vmem(3 * stride, LANE),
             vmem(2 * SUB, LANE),
-            vmem(devices * MSG, LANE),
             pltpu.SemaphoreType.DMA((7,)),
-            pltpu.SemaphoreType.DMA((devices // SUB,)),
         ],
         "hhhhhh",
         limit=PACK_LIMIT,
-        out_space="h",
-    )(points, poses, directions, remote_src, remote_maps[0], counts)
+    )(*[in_hbm(x) for x in (points, poses, directions, remote_src, remote_maps[0], counts)])
     arrived = exchange(message, devices)
     staged, totals = call(
         local_kernel,
@@ -513,21 +509,21 @@
         "vv",
     )(arrived, staged)
     back = exchange(back, devices)
-    (extra,) = call(
+    extra, table = call(
         functools.partial(total_kernel, per_frag=per_frag),
-        [array(18, frags)],
+        [array(18, frags), jax.ShapeDtypeStruct((devices, LANE), jnp.int32)],
         [],
-        "vv",
+        "vvv",
         cost_estimate=pl.CostEstimate(
             flops=2 * SUB * slots * 2 * LANE, bytes_accessed=1_000_000, transcendentals=0
         ),
-    )(sums, remote_dst)
+    )(sums, remote_dst, remote_src)
     gradient, hess = call(
         functools.partial(final_kernel, per_frag=per_frag),
         [array(6, frags), array(6, 2, frags)],
         [],
         "vvvv",
-    )(back, totals, extra, remote_src)
+    )(back, totals, extra, table)
     return (gradient, hess.transpose(1, 0, 2))
 
 

time: 41 us -> 40.4 us (0.985)
  waiting for transfers between devices: 15.9 us -> 15.2 us
    all_to_all x2, waiting for transfers between devices: 15.9 us -> 15.2 us  [exchange(): sent = lax.all_to_all(sent, AXES, split_axis=0, concat_axis=0, tiled=True)]
where the time goes in v4:
time: 40.4 us; the launch traced here: 40.1 us
  waiting for transfers between devices  15.2 us (38%)
  Pallas kernels  12.4 us (31%)
  starting transfers between devices  10.4 us (26%)
  local copies, waits for them, and re-layouts  1.33 us (3%)
  between operations  0.78 us (2%)
    all_to_all x2, waiting for transfers between devices, exchange(): sent = lax.all_to_all(sent, AXES, split_axis=0, concat_axis=0, tiled=True)  15.2 us
    all_to_all x2, starting transfers between devices, exchange(): sent = lax.all_to_all(sent, AXES, split_axis=0, concat_axis=0, tiled=True)  10.4 us
    pallas_call x1, Pallas kernels, local(): call(local_kernel, [array(devices * TARGET, LANE), array(2 * SUB, LANE)],...  6.32 us
    pallas_call x1, Pallas kernels, local(): call(remote_kernel, [array(devices * 2, LANE), array(4 * SUB, slots)], [v...  2.59 us
    pallas_call x1, Pallas kernels, local(): call(pack_kernel, [pltpu.VMEM((devices * MSG, LANE), f32)], [vmem(3, bloc...  2.37 us
    unnamed x16, local copies, waits for them, and re-layouts  1.33 us
    pallas_call x1, Pallas kernels, local(): call(functools.partial(final_kernel, per_frag=per_frag), [array(6, frags)...  0.92 us
  transfers between devices with their start and end apart: 2, of which 2 were waited for; matrix products, arithmetic and copies ran while one was open for 0% of the time, Pallas kernels for 16%

profile of v4, /device:TPU:0, one launch (start us, length us, event | category | flops | bytes accessed | tf_op | source)
XLA Modules:
  0.0 40.1 jit_solution(8442224002032010731)
XLA Ops:
  0.6 2.4 %shard_map.113 = f32[1056,128]{1,0:T(8,128)} custom-call(f32[3,256,128]{2,1,0:T(8,128)} %bitcast.10, f32[6,8]{1,0:T(8,128)} %poses.1, f32[6,2,8]{2,1,0:T(2,128)} %bitcast.14, s32[1,256]{1,0:T(1,128)} %src_v.1, s32[256,128]{1,0:T(8,128)} %bitcast.16, s32[1,32]{1,0:T(1,128)} %counts_h.1), custom_call_target="tpu_custom_call" | custom-call | tf_op jit(solution)/shard_map/pallas_call | solution.py:465
  3.0 0.0 copy-start
  3.0 0.0 copy-start.1
  3.0 0.0 copy-start.2
  3.0 0.0 copy-start.3
  3.1 0.0 copy-start.4
  3.1 0.0 copy-start.5
  3.1 7.3 %all-to-all-start = ((f32[32,1,4224]{2,1,0:T(1,128)}), f32[32,1,4224]{2,1,0:T(1,128)S(1)}, u32[]{:S(2)}, u32[]{:S(2)}) async-start(f32[32,1,4224]{2,1,0:T(1,128)} %bitcast.3), calls=%async_computation | async-start | bytes 1081344 | tf_op jit(solution)/shard_map/all_to_all | solution.py:438
  10.4 0.0 copy-start.7
  10.4 0.0 copy-done
  10.4 0.0 copy-done.1
  10.4 0.0 copy-done.2
  10.4 0.0 copy-done.3
  10.4 0.0 copy-done.4
  10.5 0.0 copy-done.5
  10.5 0.6 %copy-done.7 = s32[1,256]{1,0:T(1,128)S(1)} copy-done((s32[1,256]{1,0:T(1,128)S(1)}, s32[1,256]{1,0:T(1,128)}, u32[]{:S(2)}) %copy-start.7) | copy-done | bytes 1048
  11.1 6.3 %shard_map.114 = (f32[2048,128]{1,0:T(8,128)S(1)}, f32[16,128]{1,0:T(8,128)S(1)}) custom-call(f32[3,256,128]{2,1,0:T(8,128)S(1)} %bitcast.11, f32[3,256,128]{2,1,0:T(8,128)S(1)} %bitcast.12, f32[6,8]{1,0:T(8,128)S(1)} %copy-done.4, f32[6,2,8]{2,1,0:T(2,128)S(1)} %bitcast.15, s32[2,256]{1,0:T(2,128)S(1)} %copy-done.5, s32[2,256]{1,0:T(2,128)S(1)} %copy-done.5, ...), custom_call_target="tpu_custom_call" | custom-call | flops 6553600 | bytes 4000000 | tf_op jit(solution)/shard_map/pallas_call | solution.py:484
  17.4 8.8 %all-to-all-done = f32[32,1,4224]{2,1,0:T(1,128)S(1)} async-done(((f32[32,1,4224]{2,1,0:T(1,128)}), f32[32,1,4224]{2,1,0:T(1,128)S(1)}, u32[]{:S(2)}, u32[]{:S(2)}) %all-to-all-start) | async-done | bytes 540704 | tf_op jit(solution)/shard_map/all_to_all | solution.py:438
  26.2 2.6 %shard_map.115 = (f32[64,128]{1,0:T(8,128)}, f32[32,256]{1,0:T(8,128)S(1)}) custom-call(f32[1056,128]{1,0:T(8,128)S(1)} %bitcast.9, f32[2048,128]{1,0:T(8,128)S(1)} %get-tuple-element.10.staged), custom_call_target="tpu_custom_call" | custom-call | tf_op jit(solution)/shard_map/pallas_call | solution.py:499
  28.8 3.1 %all-to-all-start.1 = ((f32[32,1,256]{2,1,0:T(1,128)}), f32[32,1,256]{2,1,0:T(1,128)S(1)}, u32[]{:S(2)}, u32[]{:S(2)}) async-start(f32[32,1,256]{2,1,0:T(1,128)} %bitcast.6), calls=%async_computation.1 | async-start | bytes 65536 | tf_op jit(solution)/shard_map/all_to_all | solution.py:438
  32.0 0.0 copy-start.6
  32.0 0.7 %copy-done.6 = s32[1,256]{1,0:T(1,128)S(1)} copy-done((s32[1,256]{1,0:T(1,128)S(1)}, s32[1,256]{1,0:T(1,128)}, u32[]{:S(2)}) %copy-start.6) | copy-done | bytes 1048
  32.6 0.2 shard_map.116
  32.8 6.4 %all-to-all-done.1 = f32[32,1,256]{2,1,0:T(1,128)S(1)} async-done(((f32[32,1,256]{2,1,0:T(1,128)}), f32[32,1,256]{2,1,0:T(1,128)S(1)}, u32[]{:S(2)}, u32[]{:S(2)}) %all-to-all-start.1) | async-done | bytes 32800 | tf_op jit(solution)/shard_map/all_to_all | solution.py:438
  39.2 0.9 %shard_map.117 = (f32[6,8]{1,0:T(8,128)}, f32[6,2,8]{2,1,0:T(2,128)}) custom-call(f32[64,128]{1,0:T(8,128)S(1)} %bitcast.13, f32[16,128]{1,0:T(8,128)S(1)} %get-tuple-element.12.totals, f32[18,8]{1,0:T(8,128)S(1)} %get-tuple-element.14.extra, s32[32,128]{1,0:T(8,128)S(1)} %get-tuple-element.15.frags), custom_call_target="tpu_custom_call" | custom-call | tf_op jit(solution)/shard_map/pallas_call | solution.py:521
Async XLA Ops:
  3.0 7.4 %copy-start = (f32[256,3,128]{2,0,1:T(8,128)S(1)}, f32[256,3,128]{2,0,1:T(8,128)}, u32[]{:S(2)}) copy-start(f32[256,3,128]{2,0,1:T(8,128)} %param.10) | copy-start | bytes 1179652
  3.0 7.4 %copy-start.1 = (f32[256,3,128]{2,0,1:T(8,128)S(1)}, f32[256,3,128]{2,0,1:T(8,128)}, u32[]{:S(2)}) copy-start(f32[256,3,128]{2,0,1:T(8,128)} %param.11) | copy-start | bytes 1179652
  3.0 7.4 %copy-start.2 = (s32[256,128]{1,0:T(8,128)S(1)}, s32[256,128]{1,0:T(8,128)}, u32[]{:S(2)}) copy-start(s32[256,128]{1,0:T(8,128)} %maps.1) | copy-start | bytes 393220
  3.0 7.4 %copy-start.3 = (f32[2,6,8]{2,0,1:T(2,128)S(1)}, f32[2,6,8]{2,0,1:T(2,128)}, u32[]{:S(2)}) copy-start(f32[2,6,8]{2,0,1:T(2,128)} %param.13) | copy-start | bytes 1156
  3.1 7.4 %copy-start.4 = (f32[6,8]{1,0:T(8,128)S(1)}, f32[6,8]{1,0:T(8,128)}, u32[]{:S(2)}) copy-start(f32[6,8]{1,0:T(8,128)} %poses.1) | copy-start | bytes 580
  3.1 7.4 %copy-start.5 = (s32[2,256]{1,0:T(2,128)S(1)}, s32[2,256]{1,0:T(2,128)}, u32[]{:S(2)}) copy-start(s32[2,256]{1,0:T(2,128)} %pairs_v.1) | copy-start | bytes 6148
  3.1 23.2 %all-to-all-start = ((f32[32,1,4224]{2,1,0:T(1,128)}), f32[32,1,4224]{2,1,0:T(1,128)S(1)}, u32[]{:S(2)}, u32[]{:S(2)}) async-start(f32[32,1,4224]{2,1,0:T(1,128)} %bitcast.3), calls=%async_computation | async-start | bytes 1081344 | tf_op jit(solution)/shard_map/all_to_all | solution.py:438
  10.4 0.7 %copy-start.7 = (s32[1,256]{1,0:T(1,128)S(1)}, s32[1,256]{1,0:T(1,128)}, u32[]{:S(2)}) copy-start(s32[1,256]{1,0:T(1,128)} %dst_v.1) | copy-start | bytes 3076
  28.8 10.4 %all-to-all-start.1 = ((f32[32,1,256]{2,1,0:T(1,128)}), f32[32,1,256]{2,1,0:T(1,128)S(1)}, u32[]{:S(2)}, u32[]{:S(2)}) async-start(f32[32,1,256]{2,1,0:T(1,128)} %bitcast.6), calls=%async_computation.1 | async-start | bytes 65536 | tf_op jit(solution)/shard_map/all_to_all | solution.py:438
  32.0 0.7 %copy-start.6 = (s32[1,256]{1,0:T(1,128)S(1)}, s32[1,256]{1,0:T(1,128)}, u32[]{:S(2)}) copy-start(s32[1,256]{1,0:T(1,128)} %src_v.1) | copy-start | bytes 3076

commit v5 on v3

v5 whole, which is shorter than its diff:
```python
import functools

import jax
import jax.numpy as jnp
from jax import lax
from jax.experimental import pallas as pl
from jax.experimental.pallas import tpu as pltpu
from jax.sharding import PartitionSpec as P

AXES = ("tile", "band")
SUB = 8
LANE = 128
MSG = 4 * SUB + 1
TARGET = 6 * SUB
SOURCE = 3 * SUB
ROWS = 32
GROUP = 16
VMEM_LIMIT = 16 * 1024 * 1024
PACK_LIMIT = 56 * 1024 * 1024
PEERS = 32


def iota(axis):
    return lax.broadcasted_iota(jnp.int32, (SUB, LANE), axis)


def pick(values, index):
    values = jnp.broadcast_to(values, (SUB, LANE))
    return jnp.take_along_axis(values, index, axis=1, mode="promise_in_bounds")


def shift_of(size):
    shift = size.bit_length() - 1
    assert 1 << shift == size
    return shift


def cross(left, right):
    return [
        left[1] * right[2] - left[2] * right[1],
        left[2] * right[0] - left[0] * right[2],
        left[0] * right[1] - left[1] * right[0],
    ]


def dot3(left, right):
    return left[0] * right[0] + left[1] * right[1] + left[2] * right[2]


def splat_rotation(poses, f):
    half = [jnp.full((SUB, LANE), poses[i, f] * 0.5, jnp.float32) for i in range(3)]
    w = 1.0 / jnp.sqrt(1.0 + half[0] * half[0] + half[1] * half[1] + half[2] * half[2])
    x, y, z = half[0] * w, half[1] * w, half[2] * w
    rotation = [
        [1.0 - 2.0 * (y * y + z * z), 2.0 * (x * y - w * z), 2.0 * (x * z + w * y)],
        [2.0 * (x * y + w * z), 1.0 - 2.0 * (x * x + z * z), 2.0 * (y * z - w * x)],
        [2.0 * (x * z - w * y), 2.0 * (y * z + w * x), 1.0 - 2.0 * (x * x + y * y)],
    ]
    return rotation, [jnp.full((SUB, LANE), poses[i, f], jnp.float32) for i in range(3, 6)]


def write_world(fields, poses, world):
    blocks, frags = fields[0].shape[1], poses.shape[1]
    per_frag, stride = blocks // frags, blocks + SUB
    for f in range(frags):
        turn, move = splat_rotation(poses, f)
        for b in range(f * per_frag, (f + 1) * per_frag, SUB):
            for at, field in enumerate(fields):
                x = [field[j, b : b + SUB, :] for j in range(3)]
                for i in range(3):
                    row = dot3(turn[i], x)
                    world[pl.ds((3 * at + i) * stride + b, SUB), :] = row + move[i] if at == 0 else row


def write_directions(directions, table):
    frags = directions.shape[2]
    for v in range(2):
        for j in range(6):
            table[6 * v + j : 6 * v + j + 1, 0:frags] = directions[j, v : v + 1, :]


def index_tile(row_ref, first, offset):
    tile = first // LANE * LANE
    return pick(row_ref[0:1, pl.ds(tile, LANE)], offset + first % LANE)


def pack_kernel(
    points_h, poses_h, directions_h, src_h, maps_h, counts_h, out_h,
    points, poses, directions, src_s, src_v, maps, used, world, table, out, sems, out_sems,
):
    devices = counts_h.shape[1]
    per_frag = points.shape[1] // poses.shape[1]
    stride = points.shape[1] + SUB
    pairs = [
        (directions_h, directions), (src_h, src_v), (counts_h, used), (poses_h, poses),
        (points_h, points), (src_h, src_s), (maps_h, maps),
    ]
    copies = [pltpu.make_async_copy(a, b, sems.at[i]) for i, (a, b) in enumerate(pairs)]
    for copy in copies:
        copy.start()
    for copy in copies[0:3]:
        copy.wait()
    write_directions(directions, table)
    limits = jnp.broadcast_to(used[0:1, :], (SUB, devices)).astype(jnp.float32)
    peers = lax.broadcasted_iota(jnp.int32, (SUB, devices), 1)
    row = lax.broadcasted_iota(jnp.int32, (SUB, devices), 0)
    slot = lax.shift_right_logical(iota(1), shift_of(GROUP))
    field = lax.bitwise_and(iota(1), GROUP - 1)
    for q in range(0, devices, SUB):
        block = index_tile(src_v, q * SUB, iota(0) * SUB + slot)
        frag = lax.shift_right_logical(block, shift_of(per_frag))
        limit = jnp.sum(jnp.where(peers == row + q, limits, 0.0), axis=1, keepdims=True)
        extras = jnp.where(slot.astype(jnp.float32) < limit, 1.0, 0.0)
        for j in range(12):
            extras = jnp.where(field == j, pick(table[j : j + 1, :], frag), extras)
        extras = jnp.where(field == 13, frag.astype(jnp.float32), extras)
        out[pl.ds(q * MSG + MSG - 1, SUB, stride=MSG), :] = extras
    for copy in copies[3:]:
        copy.wait()
    write_world([points], poses, world)

    def peer(p):
        for s in range(SUB):
            block = src_s[0, p * SUB + s]
            out[pl.ds(p * MSG + s, 3, stride=SUB), :] = world[pl.ds(block, 3, stride=stride), :]
        rows = maps[pl.ds(pl.multiple_of(p * SUB, SUB), SUB), :]
        out[pl.ds(p * MSG + 3 * SUB, SUB), :] = rows.astype(jnp.float32)

    def piece(i):
        rows = pl.ds(pl.multiple_of(i * SUB * MSG, SUB), SUB * MSG)
        return pltpu.make_async_copy(out.at[rows], out_h.at[rows], out_sems.at[i])

    def pack(i, carry):
        for u in range(SUB):
            peer(i * SUB + u)
        piece(i).start()
        return carry

    lax.fori_loop(0, devices // SUB, pack, 0)
    for i in range(devices // SUB):
        piece(i).wait()


def halves_of(values):
    high = values.astype(jnp.bfloat16)
    return high, (values - high.astype(jnp.float32)).astype(jnp.bfloat16)


def turn(at, left, parts, i):
    columns = i * 2 * LANE
    for u in range(0, parts.shape[0] // SUB, 2):
        high, low = halves_of(jnp.concatenate([at(u), at(u + 1)], axis=0))
        parts[u * SUB : (u + 2) * SUB, columns : columns + LANE] = high
        parts[u * SUB : (u + 2) * SUB, columns + LANE : columns + 2 * LANE] = low
    return lax.dot_general(
        left,
        parts[:, columns : columns + 2 * LANE],
        (((1,), (1,)), ((), ())),
        preferred_element_type=jnp.float32,
    )


def turn_fields(source, target, index, same, parts, turned):
    for k in range(6):

        def at(u, k=k):
            return pick(target(u, k), index(u))

        turned[k * LANE : (k + 1) * LANE, :] = turn(at, same, parts, k)
    for k in range(3):
        turned[(6 + k) * LANE : (7 + k) * LANE, :] = turn(
            lambda u, k=k: source(u, k), same, parts, 6 + k
        )


def join_directions(side_a, side_b, joined):
    joined[0:12, :] = side_a[0:12, :]
    for v in range(2):
        joined[6 * v + 3 : 6 * v + 6, :] = side_a[6 * v + 3 : 6 * v + 6, :] - side_b[6 * v + 3 : 6 * v + 6, :]
        joined[12 + 3 * v : 15 + 3 * v, :] = side_b[6 * v : 6 * v + 3, :]


def point_sums(turned, joined, partial, lanes):
    def add(i, totals):
        start = pl.multiple_of(i * SUB, SUB)
        field = [turned[pl.ds(start + k * LANE, SUB), lanes] for k in range(9)]
        way = [joined[j : j + 1, lanes] for j in range(18)]
        y, n, x = field[0:3], field[3:6], field[6:9]
        p, q = cross(x, n), cross(y, n)
        scalars = [dot3(n, [x[k] - y[k] for k in range(3)])]
        for v in range(2):
            a, b = way[6 * v : 6 * v + 6], way[12 + 3 * v : 15 + 3 * v]
            scalars.append(dot3(p, a[0:3]) + dot3(n, a[3:6]) - dot3(q, b))
        terms = []
        for s in scalars:
            terms += [s * value for value in p + n]
        for s in scalars:
            terms += [s * value for value in q]
        return tuple(total + term for total, term in zip(totals, terms))

    zero = jnp.zeros((SUB, LANE), jnp.float32)
    totals = lax.fori_loop(0, LANE // SUB, add, (zero,) * 27, unroll=4)
    for j in range(27):
        partial[j * SUB : (j + 1) * SUB, :] = totals[j]
    for j in range(27, ROWS):
        partial[j * SUB : (j + 1) * SUB, :] = zero
    total = partial[pl.ds(0, ROWS, stride=SUB), :]
    for s in range(1, SUB):
        total = total + partial[pl.ds(s, ROWS, stride=SUB), :]
    return total


def frag_of(row, per_frag):
    return lax.shift_right_logical(row, shift_of(per_frag))


def look_up(table, frag, out):
    for at in range(0, frag.shape[1], LANE):
        index = jnp.broadcast_to(frag[:, at : at + LANE], (SUB, LANE))
        for j in range(0, 2 * SUB, SUB):
            out[j : j + SUB, at : at + LANE] = pick(table[j : j + SUB, :], index)


def by_frag(sums, frag):
    pairs = sums.shape[1]
    hot = jnp.broadcast_to(frag, (SUB, pairs)) == lax.broadcasted_iota(jnp.int32, (SUB, pairs), 0)
    return lax.dot_general(
        sums[...],
        hot.astype(jnp.float32),
        (((1,), (1,)), ((), ())),
        precision=lax.Precision.HIGHEST,
        preferred_element_type=jnp.float32,
    )


def target_side(total):
    rows = []
    for k in range(3):
        rows += [total[18 + 3 * k : 21 + 3 * k, :], total[6 * k + 3 : 6 * k + 6, :]]
    return -jnp.concatenate(rows, axis=0)


def constants(same, gather, place, mine):
    def wide(ref, axis):
        return lax.broadcasted_iota(jnp.int32, ref.shape, axis)

    def put(ref, hit):
        ref[...] = hit.astype(jnp.float32).astype(jnp.bfloat16)

    put(same, lax.bitwise_and(wide(same, 1), LANE - 1) == wide(same, 0))
    put(gather, lax.bitwise_and(wide(gather, 1), GROUP - 1) == wide(gather, 0))
    entry = lax.bitwise_and(wide(place, 1), GROUP - 1) + GROUP * lax.shift_right_logical(
        wide(place, 1), shift_of(LANE)
    )
    put(place, lax.bitwise_and(wide(place, 0), ROWS - 1) == entry)
    put(mine, lax.shift_right_logical(wide(mine, 1), shift_of(SUB)) == wide(mine, 0))


def local_kernel(
    points, normals, poses, directions, pairs_s, pairs_v, maps, dst_s, dst_v,
    staged, remote_b, totals, same, gather, place, mine,
    world, table, sources, targets, sums, side_a, side_b, joined, parts, turned, partial,
):
    per_frag = points.shape[1] // poses.shape[1]
    stride = points.shape[1] + SUB
    constants(same, gather, place, mine)
    table[...] = jnp.zeros_like(table)
    write_directions(directions, table)
    look_up(table, frag_of(dst_v[...], per_frag), remote_b)
    frag_a, frag_b = frag_of(pairs_v[0:1, :], per_frag), frag_of(pairs_v[1:2, :], per_frag)
    look_up(table, frag_a, side_a)
    look_up(table, frag_b, side_b)
    join_directions(side_a, side_b, joined)
    write_world([points, normals], poses, world)

    def stage_remote(g, carry):
        for s in range(SUB):
            block = dst_s[0, g * SUB + s]
            staged[pl.ds(g * TARGET + s, 6, stride=SUB), :] = world[pl.ds(block, 6, stride=stride), :]
        return carry

    lax.fori_loop(0, dst_s.shape[1] // SUB, stage_remote, 0, unroll=4)

    def stage_local(g, carry):
        for s in range(SUB):
            a, b = pairs_s[0, g * SUB + s], pairs_s[1, g * SUB + s]
            targets[pl.ds(g * TARGET + s, 6, stride=SUB), :] = world[pl.ds(b, 6, stride=stride), :]
            sources[pl.ds(g * SOURCE + s, 3, stride=SUB), :] = world[pl.ds(a, 3, stride=stride), :]
        return carry

    lax.fori_loop(0, pairs_s.shape[1] // SUB, stage_local, 0, unroll=4)
    turn_fields(
        lambda u, k: sources[u * SOURCE + k * SUB : u * SOURCE + (k + 1) * SUB, :],
        lambda u, k: targets[u * TARGET + k * SUB : u * TARGET + (k + 1) * SUB, :],
        lambda u: maps[u * SUB : (u + 1) * SUB, :],
        same[...],
        parts,
        turned,
    )
    for t in range(0, sums.shape[1], LANE):
        sums[:, t : t + LANE] = point_sums(turned, joined, partial, slice(t, t + LANE))
    totals[...] = by_frag(sums, frag_a)[0:18, :] + target_side(by_frag(sums, frag_b))


def remote_kernel(
    arrived, staged, remote_b, same, gather, place, mine,
    back, sums, side_a, joined, frags, index, parts, turned, partial,
):
    f32 = jnp.float32
    pairs = parts.shape[0]
    peers = pairs // SUB
    own = lax.shift_right_logical(iota(1), shift_of(GROUP)) == iota(0)

    def block(c, carry):
        first = c * peers
        lanes = pl.ds(pl.multiple_of(c * pairs, LANE), pairs)
        for u in range(peers):
            row = (first + u) * MSG + 3 * SUB
            index[u * SUB : (u + 1) * SUB, :] = arrived[pl.ds(row, SUB), :].astype(jnp.int32)

        def extras(u):
            row = arrived[pl.ds((first + u) * MSG + 4 * SUB, 1), :]
            frags[u * SUB : (u + 1) * SUB, :] = pick(row, iota(0) * GROUP + 13)
            return jnp.where(own, jnp.broadcast_to(row, (SUB, LANE)), 0.0)

        side_a[...] = turn(extras, gather[...], parts, 9)
        join_directions(side_a, remote_b.at[:, lanes], joined)
        turn_fields(
            lambda u, k: arrived[pl.ds((first + u) * MSG + SUB * k, SUB), :],
            lambda u, k: staged[
                pl.ds(pl.multiple_of((first + u) * TARGET, SUB) + SUB * k, SUB), :
            ],
            lambda u: index[u * SUB : (u + 1) * SUB, :],
            same[...],
            parts,
            turned,
        )
        for t in range(0, pairs, LANE):
            total = point_sums(turned, joined, partial, slice(t, t + LANE))
            at = pl.multiple_of(c * pairs, LANE) + t
            sums[:, pl.ds(at, LANE)] = total * side_a[12:13, t : t + LANE]
        rows = lax.dot_general(
            jnp.concatenate(halves_of(sums[:, lanes]), axis=0),
            place[...],
            (((0,), (0,)), ((), ())),
            preferred_element_type=f32,
        )
        slot = lax.shift_right_logical(iota(1), shift_of(GROUP)).astype(f32)[0:1, :]
        hit = frags[...] == jnp.broadcast_to(slot, (pairs, LANE))
        for half in range(2):
            part = jnp.where(hit, rows[:, half * LANE : (half + 1) * LANE], 0.0)
            high, low = halves_of(part)
            back[pl.ds(2 * first + half, peers, stride=2), :] = jnp.dot(
                mine[...], high, preferred_element_type=f32
            ) + jnp.dot(mine[...], low, preferred_element_type=f32)
        return carry

    lax.fori_loop(0, sums.shape[1] // pairs, block, 0)


def total_kernel(sums, dst_v, local_totals, totals, *, per_frag):
    totals[...] = local_totals[...] + target_side(by_frag(sums, frag_of(dst_v[...], per_frag)))


def final_kernel(back, totals, gradient, hess, *, per_frag):
    devices = back.shape[0] // 2
    index = iota(0) * GROUP + lax.bitwise_and(iota(1), GROUP - 1)
    halves = []
    for half in range(2):
        tile = back[pl.ds(half, SUB, stride=2), :]
        for q in range(SUB, devices, SUB):
            tile = tile + back[pl.ds(2 * q + half, SUB, stride=2), :]
        halves.append(pick(jnp.sum(tile, axis=0, keepdims=True), index))
    total = jnp.where(iota(1) < GROUP, halves[0], halves[1]).T[0:18, :] + totals[...]
    gradient[...] = total[0:6, :] * (1.0 / LANE)
    for v in range(2):
        part = total[6 + 6 * v : 12 + 6 * v, :] * (1.0 / (LANE * per_frag))
        for j in range(6):
            hess[j, v : v + 1, :] = part[j : j + 1, :]


def call(kernel, outs, scratch, spaces, limit=VMEM_LIMIT, out_space="v", **more):
    kinds = {"v": pltpu.VMEM, "s": pltpu.SMEM, "h": pltpu.HBM}
    return pl.pallas_call(
        kernel,
        out_shape=outs,
        in_specs=[pl.BlockSpec(memory_space=kinds[s]) for s in spaces],
        out_specs=[pl.BlockSpec(memory_space=kinds[out_space])] * len(outs),
        scratch_shapes=scratch,
        compiler_params=pltpu.CompilerParams(vmem_limit_bytes=limit),
        **more,
    )


def in_hbm(values):
    return pltpu.with_memory_space_constraint(values, pltpu.HBM)


def exchange(rows, devices):
    sent = rows.reshape(devices, 1, -1)
    sent = lax.all_to_all(sent, AXES, split_axis=0, concat_axis=0, tiled=True)
    return sent.reshape(rows.shape)


def local(
    points, normals, poses, directions, local_pairs, local_maps,
    remote_src, remote_maps, remote_dst, counts,
):
    devices = lax.axis_size("tile") * lax.axis_size("band")
    blocks, _, count = points.shape
    frags = poses.shape[1]
    slots = remote_src.shape[1]
    pairs = local_pairs.shape[1]
    assert count == LANE and frags == SUB and slots == devices * SUB and devices % PEERS == 0
    per_frag = blocks // frags
    stride = blocks + SUB
    f32 = jnp.float32
    points = points.transpose(1, 0, 2)
    normals = normals.transpose(1, 0, 2)
    directions = directions.transpose(1, 0, 2)

    def array(*shape, dtype=f32):
        return jax.ShapeDtypeStruct(shape, dtype)

    def vmem(*shape, dtype=f32):
        return pltpu.VMEM(shape, dtype)

    i32, bf16 = jnp.int32, jnp.bfloat16
    part = PEERS * SUB
    (message,) = call(
        pack_kernel,
        [array(devices * MSG, LANE)],
        [
            vmem(3, blocks, LANE),
            pltpu.SMEM((6, frags), f32),
            vmem(6, 2, frags),
            pltpu.SMEM((1, slots), i32),
            vmem(1, slots, dtype=i32),
            vmem(slots, LANE, dtype=i32),
            vmem(1, devices, dtype=i32),
            vmem(3 * stride, LANE),
            vmem(2 * SUB, LANE),
            vmem(devices * MSG, LANE),
            pltpu.SemaphoreType.DMA((7,)),
            pltpu.SemaphoreType.DMA((devices // SUB,)),
        ],
        "hhhhhh",
        limit=PACK_LIMIT,
        out_space="h",
    )(*[in_hbm(x) for x in (points, poses, directions, remote_src, remote_maps[0], counts)])
    arrived = exchange(message, devices)
    staged, remote_b, totals, same, gather, place, mine = call(
        local_kernel,
        [
            array(devices * TARGET, LANE),
            array(2 * SUB, slots),
            array(18, frags),
            array(LANE, 2 * LANE, dtype=bf16),
            array(GROUP, 2 * LANE, dtype=bf16),
            array(2 * ROWS, 2 * LANE, dtype=bf16),
            array(PEERS, part, dtype=bf16),
        ],
        [
            vmem(6 * stride, LANE),
            vmem(2 * SUB, LANE),
            vmem(pairs // SUB * SOURCE, LANE),
            vmem(pairs // SUB * TARGET, LANE),
            vmem(ROWS, pairs),
            vmem(2 * SUB, pairs),
            vmem(2 * SUB, pairs),
            vmem(3 * SUB, pairs),
            vmem(pairs, 9 * 2 * LANE, dtype=bf16),
            vmem(9 * LANE, pairs),
            vmem(ROWS * SUB, LANE),
        ],
        "vvsvsvvsv",
        cost_estimate=pl.CostEstimate(
            flops=200 * pairs * LANE, bytes_accessed=4_000_000, transcendentals=0
        ),
    )(
        points, normals, poses, directions, local_pairs, local_pairs, local_maps,
        remote_dst, remote_dst,
    )
    back, sums = call(
        remote_kernel,
        [array(devices * 2, LANE), array(ROWS, slots)],
        [
            vmem(2 * SUB, part),
            vmem(3 * SUB, part),
            vmem(part, LANE),
            vmem(part, LANE, dtype=i32),
            vmem(part, 10 * 2 * LANE, dtype=bf16),
            vmem(9 * LANE, part),
            vmem(ROWS * SUB, LANE),
        ],
        "vvvvvvv",
    )(arrived, staged, remote_b, same, gather, place, mine)
    back = exchange(back, devices)
    (totals,) = call(
        functools.partial(total_kernel, per_frag=per_frag),
        [array(18, frags)],
        [],
        "vvv",
        cost_estimate=pl.CostEstimate(
            flops=2 * SUB * slots * 2 * LANE, bytes_accessed=1_000_000, transcendentals=0
        ),
    )(sums, remote_dst, totals)
    gradient, hess = call(
        functools.partial(final_kernel, per_frag=per_frag),
        [array(6, frags), array(6, 2, frags)],
        [],
        "vv",
    )(back, totals)
    return (gradient, hess.transpose(1, 0, 2))


def solution(mesh):
    placed = (
        P(AXES, None, None),
        P(AXES, None, None),
        P(None, AXES),
        P(None, None, AXES),
        P(None, AXES),
        P(AXES, None),
        P(AXES, None),
        P(AXES, None, None),
        P(AXES, None),
        P(AXES, None),
    )
    return jax.shard_map(
        local,
        mesh=mesh,
        in_specs=placed,
        out_specs=(P(None, AXES), P(None, None, AXES)),
        check_vma=False,
    )
```

time: 41 us -> 40 us (0.976)
  Pallas kernels: 12.3 us -> 9.5 us
  waiting for transfers between devices: 15.9 us -> 18.4 us
  local copies, waits for them, and re-layouts: 1.33 us -> 0.65 us
    pallas_call x2, Pallas kernels: 8.92 us -> 6.36 us  [the longest x1 3.89 us: local(): call(local_kernel, [array(devices * TARGET, LANE), array(2 * SUB, slots),...]
    all_to_all x2, waiting for transfers between devices: 15.9 us -> 18.4 us  [exchange(): sent = lax.all_to_all(sent, AXES, split_axis=0, concat_axis=0, tiled=True)]
    unnamed x16 -> x14, local copies, waits for them, and re-layouts: 1.33 us -> 0.65 us
  transfers between devices with their start and end apart: 2 -> 2, of which waited for: 2 -> 2; matrix products, arithmetic and copies ran while one was open for 0% -> 0% of each run, Pallas kernels for 16% -> 10%
where the time goes in v5:
time: 40 us; the launch traced here: 39.7 us
  waiting for transfers between devices  18.4 us (46%)
  starting transfers between devices  10.4 us (26%)
  Pallas kernels  9.5 us (24%)
  between operations  0.77 us (2%)
  local copies, waits for them, and re-layouts  0.65 us (2%)
    all_to_all x2, waiting for transfers between devices, exchange(): sent = lax.all_to_all(sent, AXES, split_axis=0, concat_axis=0, tiled=True)  18.4 us
    all_to_all x2, starting transfers between devices, exchange(): sent = lax.all_to_all(sent, AXES, split_axis=0, concat_axis=0, tiled=True)  10.4 us
    pallas_call x1, Pallas kernels, local(): call(local_kernel, [array(devices * TARGET, LANE), array(2 * SUB, slots),...  3.89 us
    pallas_call x1, Pallas kernels, local(): call(remote_kernel, [array(devices * 2, LANE), array(ROWS, slots)], [vmem...  2.47 us
    pallas_call x1, Pallas kernels, local(): call(pack_kernel, [array(devices * MSG, LANE)], [vmem(3, blocks, LANE), p...  2.23 us
  transfers between devices with their start and end apart: 2, of which 2 were waited for; matrix products, arithmetic and copies ran while one was open for 0% of the time, Pallas kernels for 10%

profile of v5, /device:TPU:0, one launch (start us, length us, event | category | flops | bytes accessed | tf_op | source)
XLA Modules:
  0.0 39.7 jit_solution(1691559576246072240)
XLA Ops:
  0.6 2.2 %shard_map.113 = f32[1056,128]{1,0:T(8,128)} custom-call(f32[3,256,128]{2,1,0:T(8,128)} %bitcast.10, f32[6,8]{1,0:T(8,128)} %poses.1, f32[6,2,8]{2,1,0:T(2,128)} %bitcast.14, s32[1,256]{1,0:T(1,128)} %src_h.1, s32[256,128]{1,0:T(8,128)} %bitcast.17, s32[1,32]{1,0:T(1,128)} %counts_h.1), custom_call_target="tpu_custom_call" | custom-call | tf_op jit(solution)/shard_map/pallas_call | solution.py:430
  2.9 0.0 copy-start
  2.9 0.0 copy-start.1
  2.9 0.0 copy-start.2
  2.9 0.0 copy-start.3
  2.9 0.0 copy-start.4
  2.9 0.0 copy-start.6
  2.9 7.3 %all-to-all-start = ((f32[32,1,4224]{2,1,0:T(1,128)}), f32[32,1,4224]{2,1,0:T(1,128)S(1)}, u32[]{:S(2)}, u32[]{:S(2)}) async-start(f32[32,1,4224]{2,1,0:T(1,128)} %bitcast.16), calls=%async_computation | async-start | bytes 1081344 | tf_op jit(solution)/shard_map/all_to_all | solution.py:401
  10.3 0.0 copy-start.5
  10.3 0.0 copy-done
  10.3 0.0 copy-done.1
  10.3 0.0 copy-done.2
  10.3 0.0 copy-done.3
  10.3 0.0 copy-done.4
  10.3 0.0 copy-done.6
  10.3 0.6 %copy-done.5 = s32[1,256]{1,0:T(1,128)S(1)} copy-done((s32[1,256]{1,0:T(1,128)S(1)}, s32[1,256]{1,0:T(1,128)}, u32[]{:S(2)}) %copy-start.5) | copy-done | bytes 1048
  10.9 3.9 %shard_map.114 = (f32[1536,128]{1,0:T(8,128)S(1)}, f32[16,256]{1,0:T(8,128)S(1)}, f32[18,8]{1,0:T(8,128)S(1)}, bf16[128,256]{1,0:T(8,128)(2,1)S(1)}, bf16[16,256...) custom-call(f32[3,256,128]{2,1,0:T(8,128)S(1)} %bitcast.11, ...), custom_call_target="tpu_custom_call" | custom-call | flops 6553600 | bytes 4000000 | tf_op jit(solution)/shard_map/pallas_call | solution.py:452
  14.8 11.3 %all-to-all-done = f32[32,1,4224]{2,1,0:T(1,128)S(1)} async-done(((f32[32,1,4224]{2,1,0:T(1,128)}), f32[32,1,4224]{2,1,0:T(1,128)S(1)}, u32[]{:S(2)}, u32[]{:S(2)}) %all-to-all-start) | async-done | bytes 540704 | tf_op jit(solution)/shard_map/all_to_all | solution.py:401
  26.1 2.5 %shard_map.115 = (f32[64,128]{1,0:T(8,128)}, f32[32,256]{1,0:T(8,128)S(1)}) custom-call(f32[1056,128]{1,0:T(8,128)S(1)} %bitcast.9, f32[1536,128]{1,0:T(8,128)S(1)} %get-tuple-element.13.staged, f32[16,256]{1,0:T(8,128)S(1)} %get-tuple-element.14.remote_b, bf16[128,256]{1,0:T(8,128)(2,1)S(1)} %get-tuple-element.15.same, ...), custom_call_target="tpu_custom_call" | custom-call | tf_op jit(solution)/shard_map/pallas_call | solution.py:484
  28.6 3.1 %all-to-all-start.1 = ((f32[32,1,256]{2,1,0:T(1,128)}), f32[32,1,256]{2,1,0:T(1,128)S(1)}, u32[]{:S(2)}, u32[]{:S(2)}) async-start(f32[32,1,256]{2,1,0:T(1,128)} %bitcast.6), calls=%async_computation.1 | async-start | bytes 65536 | tf_op jit(solution)/shard_map/all_to_all | solution.py:401
  31.7 0.2 shard_map.116.totals
  31.9 7.1 %all-to-all-done.1 = f32[32,1,256]{2,1,0:T(1,128)S(1)} async-done(((f32[32,1,256]{2,1,0:T(1,128)}), f32[32,1,256]{2,1,0:T(1,128)S(1)}, u32[]{:S(2)}, u32[]{:S(2)}) %all-to-all-start.1) | async-done | bytes 32800 | tf_op jit(solution)/shard_map/all_to_all | solution.py:401
  39.0 0.7 %shard_map.117 = (f32[6,8]{1,0:T(8,128)}, f32[6,2,8]{2,1,0:T(2,128)}) custom-call(f32[64,128]{1,0:T(8,128)S(1)} %bitcast.13, f32[18,8]{1,0:T(8,128)S(1)} %shard_map.116.totals), custom_call_target="tpu_custom_call" | custom-call | tf_op jit(solution)/shard_map/pallas_call | solution.py:508
Async XLA Ops:
  2.9 7.4 %copy-start = (f32[256,3,128]{2,0,1:T(8,128)S(1)}, f32[256,3,128]{2,0,1:T(8,128)}, u32[]{:S(2)}) copy-start(f32[256,3,128]{2,0,1:T(8,128)} %param.10) | copy-start | bytes 1179652
  2.9 7.4 %copy-start.1 = (f32[256,3,128]{2,0,1:T(8,128)S(1)}, f32[256,3,128]{2,0,1:T(8,128)}, u32[]{:S(2)}) copy-start(f32[256,3,128]{2,0,1:T(8,128)} %param.11) | copy-start | bytes 1179652
  2.9 7.4 %copy-start.2 = (s32[256,128]{1,0:T(8,128)S(1)}, s32[256,128]{1,0:T(8,128)}, u32[]{:S(2)}) copy-start(s32[256,128]{1,0:T(8,128)} %maps.1) | copy-start | bytes 393220
  2.9 7.4 %copy-start.3 = (f32[2,6,8]{2,0,1:T(2,128)S(1)}, f32[2,6,8]{2,0,1:T(2,128)}, u32[]{:S(2)}) copy-start(f32[2,6,8]{2,0,1:T(2,128)} %param.13) | copy-start | bytes 1156
  2.9 7.4 %copy-start.4 = (f32[6,8]{1,0:T(8,128)S(1)}, f32[6,8]{1,0:T(8,128)}, u32[]{:S(2)}) copy-start(f32[6,8]{1,0:T(8,128)} %poses.1) | copy-start | bytes 580
  2.9 7.4 %copy-start.6 = (s32[2,256]{1,0:T(2,128)S(1)}, s32[2,256]{1,0:T(2,128)}, u32[]{:S(2)}) copy-start(s32[2,256]{1,0:T(2,128)} %pairs_v.1) | copy-start | bytes 6148
  2.9 23.2 %all-to-all-start = ((f32[32,1,4224]{2,1,0:T(1,128)}), f32[32,1,4224]{2,1,0:T(1,128)S(1)}, u32[]{:S(2)}, u32[]{:S(2)}) async-start(f32[32,1,4224]{2,1,0:T(1,128)} %bitcast.16), calls=%async_computation | async-start | bytes 1081344 | tf_op jit(solution)/shard_map/all_to_all | solution.py:401
  10.3 0.7 %copy-start.5 = (s32[1,256]{1,0:T(1,128)S(1)}, s32[1,256]{1,0:T(1,128)}, u32[]{:S(2)}) copy-start(s32[1,256]{1,0:T(1,128)} %dst_v.3) | copy-start | bytes 3076
  28.6 10.4 %all-to-all-start.1 = ((f32[32,1,256]{2,1,0:T(1,128)}), f32[32,1,256]{2,1,0:T(1,128)S(1)}, u32[]{:S(2)}, u32[]{:S(2)}) async-start(f32[32,1,256]{2,1,0:T(1,128)} %bitcast.6), calls=%async_computation.1 | async-start | bytes 65536 | tf_op jit(solution)/shard_map/all_to_all | solution.py:401

commit v6 on v5

--- a/solution.py
+++ b/solution.py
@@ -303,8 +303,8 @@
 
 
 def remote_kernel(
-    arrived, staged, remote_b, same, gather, place, mine,
-    back, sums, side_a, joined, frags, index, parts, turned, partial,
+    arrived, staged, remote_b, local_totals, dst_v, same, gather, place, mine,
+    back, totals, sums, side_a, joined, frags, index, parts, turned, partial, *, per_frag,
 ):
     f32 = jnp.float32
     pairs = parts.shape[0]
@@ -356,9 +356,6 @@
         return carry
 
     lax.fori_loop(0, sums.shape[1] // pairs, block, 0)
-
-
-def total_kernel(sums, dst_v, local_totals, totals, *, per_frag):
     totals[...] = local_totals[...] + target_side(by_frag(sums, frag_of(dst_v[...], per_frag)))
 
 
@@ -481,10 +478,11 @@
         points, normals, poses, directions, local_pairs, local_pairs, local_maps,
         remote_dst, remote_dst,
     )
-    back, sums = call(
-        remote_kernel,
-        [array(devices * 2, LANE), array(ROWS, slots)],
+    back, totals = call(
+        functools.partial(remote_kernel, per_frag=per_frag),
+        [array(devices * 2, LANE), array(18, frags)],
         [
+            vmem(ROWS, slots),
             vmem(2 * SUB, part),
             vmem(3 * SUB, part),
             vmem(part, LANE),
@@ -493,18 +491,9 @@
             vmem(9 * LANE, part),
             vmem(ROWS * SUB, LANE),
         ],
-        "vvvvvvv",
-    )(arrived, staged, remote_b, same, gather, place, mine)
+        "vvvvvvvvv",
+    )(arrived, staged, remote_b, totals, remote_dst, same, gather, place, mine)
     back = exchange(back, devices)
-    (totals,) = call(
-        functools.partial(total_kernel, per_frag=per_frag),
-        [array(18, frags)],
-        [],
-        "vvv",
-        cost_estimate=pl.CostEstimate(
-            flops=2 * SUB * slots * 2 * LANE, bytes_accessed=1_000_000, transcendentals=0
-        ),
-    )(sums, remote_dst, totals)
     gradient, hess = call(
         functools.partial(final_kernel, per_frag=per_frag),
         [array(6, frags), array(6, 2, frags)],

time: 40 us -> 39.2 us (0.980)
  blocking collectives: 0 us -> 10.2 us
  waiting for transfers between devices: 18.4 us -> 11.3 us
  starting transfers between devices: 10.4 us -> 7.3 us
  Pallas kernels: 9.5 us -> 8.72 us
    all_to_all x0 -> x1, blocking collectives: none -> 10.2 us  [exchange(): sent = lax.all_to_all(sent, AXES, split_axis=0, concat_axis=0, tiled=True)]
    all_to_all x2 -> x1, waiting for transfers between devices: 18.4 us -> 11.3 us  [exchange(): sent = lax.all_to_all(sent, AXES, split_axis=0, concat_axis=0, tiled=True)]
    all_to_all x2 -> x1, starting transfers between devices: 10.4 us -> 7.3 us  [exchange(): sent = lax.all_to_all(sent, AXES, split_axis=0, concat_axis=0, tiled=True)]
    pallas_call x2 -> x1, Pallas kernels: 2.63 us -> 1.87 us  [local(): call(functools.partial(remote_kernel, per_frag=per_frag), [array(devices...]
  transfers between devices with their start and end apart: 2 -> 1, of which waited for: 2 -> 1; matrix products, arithmetic and copies ran while one was open for 0% -> 0% of each run, Pallas kernels for 10% -> 10%
where the time goes in v6:
time: 39.2 us; the launch traced here: 38.9 us
  waiting for transfers between devices  11.3 us (29%)
  blocking collectives  10.2 us (26%)
  Pallas kernels  8.72 us (22%)
  starting transfers between devices  7.3 us (19%)
  between operations  0.75 us (2%)
  local copies, waits for them, and re-layouts  0.65 us (2%)
    all_to_all x1, waiting for transfers between devices, exchange(): sent = lax.all_to_all(sent, AXES, split_axis=0, concat_axis=0, tiled=True)  11.3 us
    all_to_all x1, blocking collectives, exchange(): sent = lax.all_to_all(sent, AXES, split_axis=0, concat_axis=0, tiled=True)  10.2 us
    all_to_all x1, starting transfers between devices, exchange(): sent = lax.all_to_all(sent, AXES, split_axis=0, concat_axis=0, tiled=True)  7.3 us
    pallas_call x1, Pallas kernels, local(): call(local_kernel, [array(devices * TARGET, LANE), array(2 * SUB, slots),...  3.87 us
    pallas_call x1, Pallas kernels, local(): call(pack_kernel, [array(devices * MSG, LANE)], [vmem(3, blocks, LANE), p...  2.24 us
    pallas_call x1, Pallas kernels, local(): call(functools.partial(remote_kernel, per_frag=per_frag), [array(devices...  1.87 us
  transfers between devices with their start and end apart: 1, of which 1 were waited for; matrix products, arithmetic and copies ran while one was open for 0% of the time, Pallas kernels for 10%

profile of v6, /device:TPU:0, one launch (start us, length us, event | category | flops | bytes accessed | tf_op | source)
XLA Modules:
  0.0 38.9 jit_solution(14771037821766024111)
XLA Ops:
  0.6 2.2 %shard_map.113 = f32[1056,128]{1,0:T(8,128)} custom-call(f32[3,256,128]{2,1,0:T(8,128)} %bitcast.10, f32[6,8]{1,0:T(8,128)} %poses.1, f32[6,2,8]{2,1,0:T(2,128)} %bitcast.15, s32[1,256]{1,0:T(1,128)} %src_h.1, s32[256,128]{1,0:T(8,128)} %bitcast.18, s32[1,32]{1,0:T(1,128)} %counts_h.1), custom_call_target="tpu_custom_call" | custom-call | tf_op jit(solution)/shard_map/pallas_call | solution.py:427
  2.9 0.0 copy-start
  2.9 0.0 copy-start.1
  2.9 0.0 copy-start.2
  2.9 0.0 copy-start.3
  2.9 0.0 copy-start.4
  2.9 0.0 copy-start.6
  2.9 7.3 %all-to-all-start = ((f32[32,1,4224]{2,1,0:T(1,128)}), f32[32,1,4224]{2,1,0:T(1,128)S(1)}, u32[]{:S(2)}, u32[]{:S(2)}) async-start(f32[32,1,4224]{2,1,0:T(1,128)} %bitcast.17), calls=%async_computation | async-start | bytes 1081344 | tf_op jit(solution)/shard_map/all_to_all | solution.py:398
  10.3 0.0 copy-start.5
  10.3 0.0 copy-done
  10.3 0.0 copy-done.1
  10.3 0.0 copy-done.2
  10.3 0.0 copy-done.3
  10.3 0.0 copy-done.4
  10.3 0.0 copy-done.6
  10.3 0.6 %copy-done.5 = s32[1,256]{1,0:T(1,128)S(1)} copy-done((s32[1,256]{1,0:T(1,128)S(1)}, s32[1,256]{1,0:T(1,128)}, u32[]{:S(2)}) %copy-start.5) | copy-done | bytes 1048
  10.9 3.9 %shard_map.114 = (f32[1536,128]{1,0:T(8,128)S(1)}, f32[16,256]{1,0:T(8,128)S(1)}, f32[18,8]{1,0:T(8,128)S(1)}, bf16[128,256]{1,0:T(8,128)(2,1)S(1)}, bf16[16,256...) custom-call(f32[3,256,128]{2,1,0:T(8,128)S(1)} %bitcast.11, ...), custom_call_target="tpu_custom_call" | custom-call | flops 6553600 | bytes 4000000 | tf_op jit(solution)/shard_map/pallas_call | solution.py:449
  14.8 11.3 %all-to-all-done = f32[32,1,4224]{2,1,0:T(1,128)S(1)} async-done(((f32[32,1,4224]{2,1,0:T(1,128)}), f32[32,1,4224]{2,1,0:T(1,128)S(1)}, u32[]{:S(2)}, u32[]{:S(2)}) %all-to-all-start) | async-done | bytes 540704 | tf_op jit(solution)/shard_map/all_to_all | solution.py:398
  26.1 1.9 %shard_map.115 = (f32[64,128]{1,0:T(8,128)S(1)}, f32[18,8]{1,0:T(8,128)S(1)}) custom-call(f32[1056,128]{1,0:T(8,128)S(1)} %bitcast.9, f32[1536,128]{1,0:T(8,128)S(1)} %get-tuple-element.13.staged, f32[16,256]{1,0:T(8,128)S(1)} %get-tuple-element.14.remote_b, f32[18,8]{1,0:T(8,128)S(1)} %get-tuple-element.15.local_totals, s32[1,256]{1,0:T(1,128)S(1)} %copy-done.5, ...), custom_call_target="tpu_custom_call" | custom-call | tf_op jit(solution)/shard_map/pallas_call | solution.py:481
  28.0 10.2 %all_to_all.10 = f32[32,1,256]{2,1,0:T(1,128)S(1)} all-to-all(f32[32,1,256]{2,1,0:T(1,128)S(1)} %bitcast.14), channel_id=1, replica_groups=mesh['tile'=8,'band'=4] {'tile','band'}, dimensions={0} | all-to-all | bytes 65536 | tf_op jit(solution)/shard_map/all_to_all | solution.py:398
  38.2 0.7 %shard_map.116 = (f32[6,8]{1,0:T(8,128)}, f32[6,2,8]{2,1,0:T(2,128)}) custom-call(f32[64,128]{1,0:T(8,128)S(1)} %bitcast.13, f32[18,8]{1,0:T(8,128)S(1)} %get-tuple-element.21.totals), custom_call_target="tpu_custom_call" | custom-call | tf_op jit(solution)/shard_map/pallas_call | solution.py:497
Async XLA Ops:
  2.9 7.4 %copy-start = (f32[256,3,128]{2,0,1:T(8,128)S(1)}, f32[256,3,128]{2,0,1:T(8,128)}, u32[]{:S(2)}) copy-start(f32[256,3,128]{2,0,1:T(8,128)} %param.10) | copy-start | bytes 1179652
  2.9 7.4 %copy-start.1 = (f32[256,3,128]{2,0,1:T(8,128)S(1)}, f32[256,3,128]{2,0,1:T(8,128)}, u32[]{:S(2)}) copy-start(f32[256,3,128]{2,0,1:T(8,128)} %param.11) | copy-start | bytes 1179652
  2.9 7.4 %copy-start.2 = (s32[256,128]{1,0:T(8,128)S(1)}, s32[256,128]{1,0:T(8,128)}, u32[]{:S(2)}) copy-start(s32[256,128]{1,0:T(8,128)} %maps.1) | copy-start | bytes 393220
  2.9 7.4 %copy-start.3 = (f32[2,6,8]{2,0,1:T(2,128)S(1)}, f32[2,6,8]{2,0,1:T(2,128)}, u32[]{:S(2)}) copy-start(f32[2,6,8]{2,0,1:T(2,128)} %param.13) | copy-start | bytes 1156
  2.9 7.4 %copy-start.4 = (f32[6,8]{1,0:T(8,128)S(1)}, f32[6,8]{1,0:T(8,128)}, u32[]{:S(2)}) copy-start(f32[6,8]{1,0:T(8,128)} %poses.1) | copy-start | bytes 580
  2.9 7.4 %copy-start.6 = (s32[2,256]{1,0:T(2,128)S(1)}, s32[2,256]{1,0:T(2,128)}, u32[]{:S(2)}) copy-start(s32[2,256]{1,0:T(2,128)} %pairs_v.1) | copy-start | bytes 6148
  2.9 23.2 %all-to-all-start = ((f32[32,1,4224]{2,1,0:T(1,128)}), f32[32,1,4224]{2,1,0:T(1,128)S(1)}, u32[]{:S(2)}, u32[]{:S(2)}) async-start(f32[32,1,4224]{2,1,0:T(1,128)} %bitcast.17), calls=%async_computation | async-start | bytes 1081344 | tf_op jit(solution)/shard_map/all_to_all | solution.py:398
  10.3 0.7 %copy-start.5 = (s32[1,256]{1,0:T(1,128)S(1)}, s32[1,256]{1,0:T(1,128)}, u32[]{:S(2)}) copy-start(s32[1,256]{1,0:T(1,128)} %dst_v.3) | copy-start | bytes 3076

commit v7 on v6

--- a/solution.py
+++ b/solution.py
@@ -59,17 +59,28 @@
     return rotation, [jnp.full((SUB, LANE), poses[i, f], jnp.float32) for i in range(3, 6)]
 
 
-def write_world(fields, poses, world):
-    blocks, frags = fields[0].shape[1], poses.shape[1]
-    per_frag, stride = blocks // frags, blocks + SUB
-    for f in range(frags):
-        turn, move = splat_rotation(poses, f)
+def write_rotations(poses, turns):
+    for f in range(poses.shape[1]):
+        rotation, move = splat_rotation(poses, f)
+        for i, tile in enumerate(rotation[0] + rotation[1] + rotation[2] + move):
+            at = (12 * f + i) * SUB
+            turns[at : at + SUB, :] = tile
+
+
+def write_world(fields, turns, world, frags):
+    blocks = fields[0].shape[1]
+    total = turns.shape[0] // (12 * SUB)
+    per_frag, stride = blocks // total, blocks + SUB
+    for f in frags:
+        tile = [turns[(12 * f + i) * SUB : (12 * f + i + 1) * SUB, :] for i in range(12)]
         for b in range(f * per_frag, (f + 1) * per_frag, SUB):
             for at, field in enumerate(fields):
                 x = [field[j, b : b + SUB, :] for j in range(3)]
                 for i in range(3):
-                    row = dot3(turn[i], x)
-                    world[pl.ds((3 * at + i) * stride + b, SUB), :] = row + move[i] if at == 0 else row
+                    row = dot3(tile[3 * i : 3 * i + 3], x)
+                    if at == 0:
+                        row = row + tile[9 + i]
+                    world[pl.ds((3 * at + i) * stride + b, SUB), :] = row
 
 
 def write_directions(directions, table):
@@ -86,19 +97,25 @@
 
 def pack_kernel(
     points_h, poses_h, directions_h, src_h, maps_h, counts_h, out_h,
-    points, poses, directions, src_s, src_v, maps, used, world, table, out, sems, out_sems,
+    points, poses, directions, src_s, src_v, maps, used, world, turns, table, out, sems, out_sems,
 ):
     devices = counts_h.shape[1]
     per_frag = points.shape[1] // poses.shape[1]
     stride = points.shape[1] + SUB
-    pairs = [
-        (directions_h, directions), (src_h, src_v), (counts_h, used), (poses_h, poses),
-        (points_h, points), (src_h, src_s), (maps_h, maps),
-    ]
+    frags = poses.shape[1]
+    half = points.shape[1] // 2
+    pieces = [slice(i * half, (i + 1) * half) for i in range(2)]
+    pairs = [(poses_h, poses), (directions_h, directions), (src_h, src_v), (counts_h, used)]
+    pairs += [(points_h.at[j, rows], points.at[j, rows]) for rows in pieces for j in range(3)]
+    rows = maps.shape[0] // 2
+    pairs += [(src_h, src_s)]
+    pairs += [(maps_h.at[pl.ds(i, rows)], maps.at[pl.ds(i, rows)]) for i in (0, rows)]
     copies = [pltpu.make_async_copy(a, b, sems.at[i]) for i, (a, b) in enumerate(pairs)]
-    for copy in copies:
-        copy.start()
-    for copy in copies[0:3]:
+    for i in (0, 4, 5, 6, 7, 8, 9, 10, 11, 12, 1, 2, 3):
+        copies[i].start()
+    copies[0].wait()
+    write_rotations(poses, turns)
+    for copy in copies[1:4]:
         copy.wait()
     write_directions(directions, table)
     limits = jnp.broadcast_to(used[0:1, :], (SUB, devices)).astype(jnp.float32)
@@ -115,9 +132,12 @@
             extras = jnp.where(field == j, pick(table[j : j + 1, :], frag), extras)
         extras = jnp.where(field == 13, frag.astype(jnp.float32), extras)
         out[pl.ds(q * MSG + MSG - 1, SUB, stride=MSG), :] = extras
-    for copy in copies[3:]:
+    for i in range(2):
+        for copy in copies[4 + 3 * i : 7 + 3 * i]:
+            copy.wait()
+        write_world([points], turns, world, range(i * frags // 2, (i + 1) * frags // 2))
+    for copy in copies[10:]:
         copy.wait()
-    write_world([points], poses, world)
 
     def peer(p):
         for s in range(SUB):
@@ -146,41 +166,46 @@
     return high, (values - high.astype(jnp.float32)).astype(jnp.bfloat16)
 
 
-def turn(at, left, parts, i):
-    columns = i * 2 * LANE
-    for u in range(0, parts.shape[0] // SUB, 2):
+def turn(at, left, parts, i, t):
+    columns = slice(i * 2 * LANE, i * 2 * LANE + LANE), slice(i * 2 * LANE + LANE, (i + 1) * 2 * LANE)
+    for u in range(t // SUB, (t + LANE) // SUB, 2):
         high, low = halves_of(jnp.concatenate([at(u), at(u + 1)], axis=0))
-        parts[u * SUB : (u + 2) * SUB, columns : columns + LANE] = high
-        parts[u * SUB : (u + 2) * SUB, columns + LANE : columns + 2 * LANE] = low
+        parts[u * SUB : (u + 2) * SUB, columns[0]] = high
+        parts[u * SUB : (u + 2) * SUB, columns[1]] = low
     return lax.dot_general(
         left,
-        parts[:, columns : columns + 2 * LANE],
+        parts[t : t + LANE, i * 2 * LANE : (i + 1) * 2 * LANE],
         (((1,), (1,)), ((), ())),
         preferred_element_type=jnp.float32,
     )
 
 
-def turn_fields(source, target, index, same, parts, turned):
+def turn_fields(source, target, index, same, parts, turned, t):
+    lanes = slice(t, t + LANE)
     for k in range(6):
 
         def at(u, k=k):
             return pick(target(u, k), index(u))
 
-        turned[k * LANE : (k + 1) * LANE, :] = turn(at, same, parts, k)
+        turned[k * LANE : (k + 1) * LANE, lanes] = turn(at, same, parts, k, t)
     for k in range(3):
-        turned[(6 + k) * LANE : (7 + k) * LANE, :] = turn(
-            lambda u, k=k: source(u, k), same, parts, 6 + k
+        turned[(6 + k) * LANE : (7 + k) * LANE, lanes] = turn(
+            lambda u, k=k: source(u, k), same, parts, 6 + k, t
         )
 
 
-def join_directions(side_a, side_b, joined):
-    joined[0:12, :] = side_a[0:12, :]
+def join_directions(side_a, side_b, joined, lanes, lanes_b):
+    joined[0:12, lanes] = side_a[0:12, lanes]
     for v in range(2):
-        joined[6 * v + 3 : 6 * v + 6, :] = side_a[6 * v + 3 : 6 * v + 6, :] - side_b[6 * v + 3 : 6 * v + 6, :]
-        joined[12 + 3 * v : 15 + 3 * v, :] = side_b[6 * v : 6 * v + 3, :]
-
-
-def point_sums(turned, joined, partial, lanes):
+        turn_rows, move_rows = slice(6 * v, 6 * v + 3), slice(6 * v + 3, 6 * v + 6)
+        joined[move_rows, lanes] = side_a[move_rows, lanes] - side_b[move_rows, lanes_b]
+        joined[12 + 3 * v : 15 + 3 * v, lanes] = side_b[turn_rows, lanes_b]
+
+
+def point_sums(turned, joined, partial, t):
+    lanes = slice(t, t + LANE)
+    first = t // LANE * ROWS * SUB
+
     def add(i, totals):
         start = pl.multiple_of(i * SUB, SUB)
         field = [turned[pl.ds(start + k * LANE, SUB), lanes] for k in range(9)]
@@ -199,14 +224,12 @@
         return tuple(total + term for total, term in zip(totals, terms))
 
     zero = jnp.zeros((SUB, LANE), jnp.float32)
-    totals = lax.fori_loop(0, LANE // SUB, add, (zero,) * 27, unroll=4)
-    for j in range(27):
-        partial[j * SUB : (j + 1) * SUB, :] = totals[j]
-    for j in range(27, ROWS):
-        partial[j * SUB : (j + 1) * SUB, :] = zero
-    total = partial[pl.ds(0, ROWS, stride=SUB), :]
+    totals = lax.fori_loop(0, LANE // SUB, add, (zero,) * 27, unroll=LANE // SUB)
+    for j in range(ROWS):
+        partial[first + j * SUB : first + (j + 1) * SUB, :] = totals[j] if j < 27 else zero
+    total = partial[pl.ds(first, ROWS, stride=SUB), :]
     for s in range(1, SUB):
-        total = total + partial[pl.ds(s, ROWS, stride=SUB), :]
+        total = total + partial[pl.ds(first + s, ROWS, stride=SUB), :]
     return total
 
 
@@ -225,7 +248,7 @@
     pairs = sums.shape[1]
     hot = jnp.broadcast_to(frag, (SUB, pairs)) == lax.broadcasted_iota(jnp.int32, (SUB, pairs), 0)
     return lax.dot_general(
-        sums[...],
+        sums,
         hot.astype(jnp.float32),
         (((1,), (1,)), ((), ())),
         precision=lax.Precision.HIGHEST,
@@ -259,7 +282,7 @@
 def local_kernel(
     points, normals, poses, directions, pairs_s, pairs_v, maps, dst_s, dst_v,
     staged, remote_b, totals, same, gather, place, mine,
-    world, table, sources, targets, sums, side_a, side_b, joined, parts, turned, partial,
+    world, turns, table, sources, targets, side_a, side_b, joined, parts, turned, partial,
 ):
     per_frag = points.shape[1] // poses.shape[1]
     stride = points.shape[1] + SUB
@@ -270,8 +293,10 @@
     frag_a, frag_b = frag_of(pairs_v[0:1, :], per_frag), frag_of(pairs_v[1:2, :], per_frag)
     look_up(table, frag_a, side_a)
     look_up(table, frag_b, side_b)
-    join_directions(side_a, side_b, joined)
-    write_world([points, normals], poses, world)
+    every = slice(0, pairs_s.shape[1])
+    join_directions(side_a, side_b, joined, every, every)
+    write_rotations(poses, turns)
+    write_world([points, normals], turns, world, range(poses.shape[1]))
 
     def stage_remote(g, carry):
         for s in range(SUB):
@@ -289,74 +314,81 @@
         return carry
 
     lax.fori_loop(0, pairs_s.shape[1] // SUB, stage_local, 0, unroll=4)
-    turn_fields(
-        lambda u, k: sources[u * SOURCE + k * SUB : u * SOURCE + (k + 1) * SUB, :],
-        lambda u, k: targets[u * TARGET + k * SUB : u * TARGET + (k + 1) * SUB, :],
-        lambda u: maps[u * SUB : (u + 1) * SUB, :],
-        same[...],
-        parts,
-        turned,
-    )
-    for t in range(0, sums.shape[1], LANE):
-        sums[:, t : t + LANE] = point_sums(turned, joined, partial, slice(t, t + LANE))
-    totals[...] = by_frag(sums, frag_a)[0:18, :] + target_side(by_frag(sums, frag_b))
+    total = jnp.zeros(totals.shape, jnp.float32)
+    for t in range(0, pairs_s.shape[1], LANE):
+        turn_fields(
+            lambda u, k: sources[u * SOURCE + k * SUB : u * SOURCE + (k + 1) * SUB, :],
+            lambda u, k: targets[u * TARGET + k * SUB : u * TARGET + (k + 1) * SUB, :],
+            lambda u: maps[u * SUB : (u + 1) * SUB, :],
+            same[...],
+            parts,
+            turned,
+            t,
+        )
+        sums = point_sums(turned, joined, partial, t)
+        total = total + by_frag(sums, frag_a[:, t : t + LANE])[0:18, :]
+        total = total + target_side(by_frag(sums, frag_b[:, t : t + LANE]))
+    totals[...] = total
 
 
 def remote_kernel(
     arrived, staged, remote_b, local_totals, dst_v, same, gather, place, mine,
-    back, totals, sums, side_a, joined, frags, index, parts, turned, partial, *, per_frag,
+    back, totals, side_a, joined, frags, index, parts, turned, partial, *, per_frag,
 ):
     f32 = jnp.float32
     pairs = parts.shape[0]
     peers = pairs // SUB
     own = lax.shift_right_logical(iota(1), shift_of(GROUP)) == iota(0)
-
-    def block(c, carry):
+    slot = lax.shift_right_logical(iota(1), shift_of(GROUP)).astype(f32)[0:1, :]
+
+    def block(c, total):
         first = c * peers
-        lanes = pl.ds(pl.multiple_of(c * pairs, LANE), pairs)
-        for u in range(peers):
-            row = (first + u) * MSG + 3 * SUB
-            index[u * SUB : (u + 1) * SUB, :] = arrived[pl.ds(row, SUB), :].astype(jnp.int32)
 
         def extras(u):
             row = arrived[pl.ds((first + u) * MSG + 4 * SUB, 1), :]
             frags[u * SUB : (u + 1) * SUB, :] = pick(row, iota(0) * GROUP + 13)
             return jnp.where(own, jnp.broadcast_to(row, (SUB, LANE)), 0.0)
 
-        side_a[...] = turn(extras, gather[...], parts, 9)
-        join_directions(side_a, remote_b.at[:, lanes], joined)
-        turn_fields(
-            lambda u, k: arrived[pl.ds((first + u) * MSG + SUB * k, SUB), :],
-            lambda u, k: staged[
-                pl.ds(pl.multiple_of((first + u) * TARGET, SUB) + SUB * k, SUB), :
-            ],
-            lambda u: index[u * SUB : (u + 1) * SUB, :],
-            same[...],
-            parts,
-            turned,
-        )
+        rows = [jnp.zeros((peers, LANE), f32) for half in range(2)]
         for t in range(0, pairs, LANE):
-            total = point_sums(turned, joined, partial, slice(t, t + LANE))
-            at = pl.multiple_of(c * pairs, LANE) + t
-            sums[:, pl.ds(at, LANE)] = total * side_a[12:13, t : t + LANE]
-        rows = lax.dot_general(
-            jnp.concatenate(halves_of(sums[:, lanes]), axis=0),
-            place[...],
-            (((0,), (0,)), ((), ())),
-            preferred_element_type=f32,
-        )
-        slot = lax.shift_right_logical(iota(1), shift_of(GROUP)).astype(f32)[0:1, :]
-        hit = frags[...] == jnp.broadcast_to(slot, (pairs, LANE))
+            lanes = slice(t, t + LANE)
+            lanes_b = pl.ds(pl.multiple_of(c * pairs, LANE) + t, LANE)
+            for u in range(t // SUB, (t + LANE) // SUB):
+                row = (first + u) * MSG + 3 * SUB
+                index[u * SUB : (u + 1) * SUB, :] = arrived[pl.ds(row, SUB), :].astype(jnp.int32)
+            side_a[:, lanes] = turn(extras, gather[...], parts, 9, t)
+            join_directions(side_a, remote_b, joined, lanes, lanes_b)
+            turn_fields(
+                lambda u, k: arrived[pl.ds((first + u) * MSG + SUB * k, SUB), :],
+                lambda u, k: staged[
+                    pl.ds(pl.multiple_of((first + u) * TARGET, SUB) + SUB * k, SUB), :
+                ],
+                lambda u: index[u * SUB : (u + 1) * SUB, :],
+                same[...],
+                parts,
+                turned,
+                t,
+            )
+            sums = point_sums(turned, joined, partial, t) * side_a[12:13, lanes]
+            placed = lax.dot_general(
+                jnp.concatenate(halves_of(sums), axis=0),
+                place[...],
+                (((0,), (0,)), ((), ())),
+                preferred_element_type=f32,
+            )
+            hit = frags[lanes, :] == jnp.broadcast_to(slot, (LANE, LANE))
+            for half in range(2):
+                part = jnp.where(hit, placed[:, half * LANE : (half + 1) * LANE], 0.0)
+                for piece in halves_of(part):
+                    rows[half] = rows[half] + jnp.dot(
+                        mine[:, lanes], piece, preferred_element_type=f32
+                    )
+            total = total + target_side(by_frag(sums, frag_of(dst_v[0:1, lanes_b], per_frag)))
         for half in range(2):
-            part = jnp.where(hit, rows[:, half * LANE : (half + 1) * LANE], 0.0)
-            high, low = halves_of(part)
-            back[pl.ds(2 * first + half, peers, stride=2), :] = jnp.dot(
-                mine[...], high, preferred_element_type=f32
-            ) + jnp.dot(mine[...], low, preferred_element_type=f32)
-        return carry
-
-    lax.fori_loop(0, sums.shape[1] // pairs, block, 0)
-    totals[...] = local_totals[...] + target_side(by_frag(sums, frag_of(dst_v[...], per_frag)))
+            back[pl.ds(2 * first + half, peers, stride=2), :] = rows[half]
+        return total
+
+    totals[...] = lax.fori_loop(0, back.shape[0] // (2 * peers), block, local_totals[...])
 
 
 def final_kernel(back, totals, gradient, hess, *, per_frag):
@@ -436,9 +468,10 @@
             vmem(slots, LANE, dtype=i32),
             vmem(1, devices, dtype=i32),
             vmem(3 * stride, LANE),
+            vmem(12 * frags * SUB, LANE),
             vmem(2 * SUB, LANE),
             vmem(devices * MSG, LANE),
-            pltpu.SemaphoreType.DMA((7,)),
+            pltpu.SemaphoreType.DMA((13,)),
             pltpu.SemaphoreType.DMA((devices // SUB,)),
         ],
         "hhhhhh",
@@ -459,16 +492,16 @@
         ],
         [
             vmem(6 * stride, LANE),
+            vmem(12 * frags * SUB, LANE),
             vmem(2 * SUB, LANE),
             vmem(pairs // SUB * SOURCE, LANE),
             vmem(pairs // SUB * TARGET, LANE),
-            vmem(ROWS, pairs),
             vmem(2 * SUB, pairs),
             vmem(2 * SUB, pairs),
             vmem(3 * SUB, pairs),
             vmem(pairs, 9 * 2 * LANE, dtype=bf16),
             vmem(9 * LANE, pairs),
-            vmem(ROWS * SUB, LANE),
+            vmem(pairs // LANE * ROWS * SUB, LANE),
         ],
         "vvsvsvvsv",
         cost_estimate=pl.CostEstimate(
@@ -482,14 +515,13 @@
         functools.partial(remote_kernel, per_frag=per_frag),
         [array(devices * 2, LANE), array(18, frags)],
         [
-            vmem(ROWS, slots),
             vmem(2 * SUB, part),
             vmem(3 * SUB, part),
             vmem(part, LANE),
             vmem(part, LANE, dtype=i32),
             vmem(part, 10 * 2 * LANE, dtype=bf16),
             vmem(9 * LANE, part),
-            vmem(ROWS * SUB, LANE),
+            vmem(part // LANE * ROWS * SUB, LANE),
         ],
         "vvvvvvvvv",
     )(arrived, staged, remote_b, totals, remote_dst, same, gather, place, mine)

time: 39.2 us -> 39.4 us (level)
  transfers between devices with their start and end apart: 1 -> 1, of which waited for: 1 -> 1; matrix products, arithmetic and copies ran while one was open for 0% -> 0% of each run, Pallas kernels for 10% -> 9%
where the time goes in v7:
time: 39.4 us; the launch traced here: 39.1 us
  waiting for transfers between devices  11.5 us (29%)
  blocking collectives  10.2 us (26%)
  Pallas kernels  8.72 us (22%)
  starting transfers between devices  7.3 us (19%)
  between operations  0.76 us (2%)
  local copies, waits for them, and re-layouts  0.65 us (2%)
    all_to_all x1, waiting for transfers between devices, exchange(): sent = lax.all_to_all(sent, AXES, split_axis=0, concat_axis=0, tiled=True)  11.5 us
    all_to_all x1, blocking collectives, exchange(): sent = lax.all_to_all(sent, AXES, split_axis=0, concat_axis=0, tiled=True)  10.2 us
    all_to_all x1, starting transfers between devices, exchange(): sent = lax.all_to_all(sent, AXES, split_axis=0, concat_axis=0, tiled=True)  7.3 us
    pallas_call x1, Pallas kernels, local(): call(local_kernel, [array(devices * TARGET, LANE), array(2 * SUB, slots),...  3.69 us
    pallas_call x1, Pallas kernels, local(): call(pack_kernel, [array(devices * MSG, LANE)], [vmem(3, blocks, LANE), p...  2.38 us
    pallas_call x1, Pallas kernels, local(): call(functools.partial(remote_kernel, per_frag=per_frag), [array(devices...  1.9 us
  transfers between devices with their start and end apart: 1, of which 1 were waited for; matrix products, arithmetic and copies ran while one was open for 0% of the time, Pallas kernels for 9%

profile of v7, /device:TPU:0, one launch (start us, length us, event | category | flops | bytes accessed | tf_op | source)
XLA Modules:
  0.0 39.1 jit_solution(12179333990572076982)
XLA Ops:
  0.6 2.4 %shard_map.113 = f32[1056,128]{1,0:T(8,128)} custom-call(f32[3,256,128]{2,1,0:T(8,128)} %bitcast.10, f32[6,8]{1,0:T(8,128)} %poses.1, f32[6,2,8]{2,1,0:T(2,128)} %bitcast.15, s32[1,256]{1,0:T(1,128)} %src_h.1, s32[256,128]{1,0:T(8,128)} %bitcast.18, s32[1,32]{1,0:T(1,128)} %counts_h.1), custom_call_target="tpu_custom_call" | custom-call | tf_op jit(solution)/shard_map/pallas_call | solution.py:459
  3.0 0.0 copy-start
  3.0 0.0 copy-start.1
  3.0 0.0 copy-start.2
  3.1 0.0 copy-start.3
  3.1 0.0 copy-start.4
  3.1 0.0 copy-start.6
  3.1 7.3 %all-to-all-start = ((f32[32,1,4224]{2,1,0:T(1,128)}), f32[32,1,4224]{2,1,0:T(1,128)S(1)}, u32[]{:S(2)}, u32[]{:S(2)}) async-start(f32[32,1,4224]{2,1,0:T(1,128)} %bitcast.17), calls=%async_computation | async-start | bytes 1081344 | tf_op jit(solution)/shard_map/all_to_all | solution.py:430
  10.4 0.0 copy-start.5
  10.4 0.0 copy-done
  10.4 0.0 copy-done.1
  10.4 0.0 copy-done.2
  10.4 0.0 copy-done.3
  10.5 0.0 copy-done.4
  10.5 0.0 copy-done.6
  10.5 0.6 %copy-done.5 = s32[1,256]{1,0:T(1,128)S(1)} copy-done((s32[1,256]{1,0:T(1,128)S(1)}, s32[1,256]{1,0:T(1,128)}, u32[]{:S(2)}) %copy-start.5) | copy-done | bytes 1048
  11.1 3.7 %shard_map.114 = (f32[1536,128]{1,0:T(8,128)S(1)}, f32[16,256]{1,0:T(8,128)S(1)}, f32[18,8]{1,0:T(8,128)S(1)}, bf16[128,256]{1,0:T(8,128)(2,1)S(1)}, bf16[16,256...) custom-call(f32[3,256,128]{2,1,0:T(8,128)S(1)} %bitcast.11, ...), custom_call_target="tpu_custom_call" | custom-call | flops 6553600 | bytes 4000000 | tf_op jit(solution)/shard_map/pallas_call | solution.py:482
  14.8 11.5 %all-to-all-done = f32[32,1,4224]{2,1,0:T(1,128)S(1)} async-done(((f32[32,1,4224]{2,1,0:T(1,128)}), f32[32,1,4224]{2,1,0:T(1,128)S(1)}, u32[]{:S(2)}, u32[]{:S(2)}) %all-to-all-start) | async-done | bytes 540704 | tf_op jit(solution)/shard_map/all_to_all | solution.py:430
  26.2 1.9 %shard_map.115 = (f32[64,128]{1,0:T(8,128)S(1)}, f32[18,8]{1,0:T(8,128)S(1)}) custom-call(f32[1056,128]{1,0:T(8,128)S(1)} %bitcast.9, f32[1536,128]{1,0:T(8,128)S(1)} %get-tuple-element.13.staged, f32[16,256]{1,0:T(8,128)S(1)} %get-tuple-element.14.remote_b, f32[18,8]{1,0:T(8,128)S(1)} %get-tuple-element.15.local_totals, s32[1,256]{1,0:T(1,128)S(1)} %copy-done.5, ...), custom_call_target="tpu_custom_call" | custom-call | tf_op jit(solution)/shard_map/pallas_call | solution.py:514
  28.1 10.2 %all_to_all.10 = f32[32,1,256]{2,1,0:T(1,128)S(1)} all-to-all(f32[32,1,256]{2,1,0:T(1,128)S(1)} %bitcast.14), channel_id=1, replica_groups=mesh['tile'=8,'band'=4] {'tile','band'}, dimensions={0} | all-to-all | bytes 65536 | tf_op jit(solution)/shard_map/all_to_all | solution.py:430
  38.4 0.7 %shard_map.116 = (f32[6,8]{1,0:T(8,128)}, f32[6,2,8]{2,1,0:T(2,128)}) custom-call(f32[64,128]{1,0:T(8,128)S(1)} %bitcast.13, f32[18,8]{1,0:T(8,128)S(1)} %get-tuple-element.21.totals), custom_call_target="tpu_custom_call" | custom-call | tf_op jit(solution)/shard_map/pallas_call | solution.py:529
Async XLA Ops:
  3.0 7.4 %copy-start = (f32[256,3,128]{2,0,1:T(8,128)S(1)}, f32[256,3,128]{2,0,1:T(8,128)}, u32[]{:S(2)}) copy-start(f32[256,3,128]{2,0,1:T(8,128)} %param.10) | copy-start | bytes 1179652
  3.0 7.4 %copy-start.1 = (f32[256,3,128]{2,0,1:T(8,128)S(1)}, f32[256,3,128]{2,0,1:T(8,128)}, u32[]{:S(2)}) copy-start(f32[256,3,128]{2,0,1:T(8,128)} %param.11) | copy-start | bytes 1179652
  3.0 7.4 %copy-start.2 = (s32[256,128]{1,0:T(8,128)S(1)}, s32[256,128]{1,0:T(8,128)}, u32[]{:S(2)}) copy-start(s32[256,128]{1,0:T(8,128)} %maps.1) | copy-start | bytes 393220
  3.1 7.4 %copy-start.3 = (f32[2,6,8]{2,0,1:T(2,128)S(1)}, f32[2,6,8]{2,0,1:T(2,128)}, u32[]{:S(2)}) copy-start(f32[2,6,8]{2,0,1:T(2,128)} %param.13) | copy-start | bytes 1156
  3.1 7.4 %copy-start.4 = (f32[6,8]{1,0:T(8,128)S(1)}, f32[6,8]{1,0:T(8,128)}, u32[]{:S(2)}) copy-start(f32[6,8]{1,0:T(8,128)} %poses.1) | copy-start | bytes 580
  3.1 7.4 %copy-start.6 = (s32[2,256]{1,0:T(2,128)S(1)}, s32[2,256]{1,0:T(2,128)}, u32[]{:S(2)}) copy-start(s32[2,256]{1,0:T(2,128)} %pairs_v.1) | copy-start | bytes 6148
  3.1 23.2 %all-to-all-start = ((f32[32,1,4224]{2,1,0:T(1,128)}), f32[32,1,4224]{2,1,0:T(1,128)S(1)}, u32[]{:S(2)}, u32[]{:S(2)}) async-start(f32[32,1,4224]{2,1,0:T(1,128)} %bitcast.17), calls=%async_computation | async-start | bytes 1081344 | tf_op jit(solution)/shard_map/all_to_all | solution.py:430
  10.4 0.7 %copy-start.5 = (s32[1,256]{1,0:T(1,128)S(1)}, s32[1,256]{1,0:T(1,128)}, u32[]{:S(2)}) copy-start(s32[1,256]{1,0:T(1,128)} %dst_v.3) | copy-start | bytes 3076

commit v8 on v7

--- a/solution.py
+++ b/solution.py
@@ -103,19 +103,13 @@
     per_frag = points.shape[1] // poses.shape[1]
     stride = points.shape[1] + SUB
     frags = poses.shape[1]
-    half = points.shape[1] // 2
-    pieces = [slice(i * half, (i + 1) * half) for i in range(2)]
-    pairs = [(poses_h, poses), (directions_h, directions), (src_h, src_v), (counts_h, used)]
-    pairs += [(points_h.at[j, rows], points.at[j, rows]) for rows in pieces for j in range(3)]
-    rows = maps.shape[0] // 2
-    pairs += [(src_h, src_s)]
-    pairs += [(maps_h.at[pl.ds(i, rows)], maps.at[pl.ds(i, rows)]) for i in (0, rows)]
+    pairs = [(directions_h, directions), (src_h, src_v), (counts_h, used), (poses_h, poses)]
+    pairs += [(points_h.at[j], points.at[j]) for j in range(3)]
+    pairs += [(src_h, src_s), (maps_h, maps)]
     copies = [pltpu.make_async_copy(a, b, sems.at[i]) for i, (a, b) in enumerate(pairs)]
-    for i in (0, 4, 5, 6, 7, 8, 9, 10, 11, 12, 1, 2, 3):
-        copies[i].start()
-    copies[0].wait()
-    write_rotations(poses, turns)
-    for copy in copies[1:4]:
+    for copy in copies:
+        copy.start()
+    for copy in copies[0:3]:
         copy.wait()
     write_directions(directions, table)
     limits = jnp.broadcast_to(used[0:1, :], (SUB, devices)).astype(jnp.float32)
@@ -132,11 +126,12 @@
             extras = jnp.where(field == j, pick(table[j : j + 1, :], frag), extras)
         extras = jnp.where(field == 13, frag.astype(jnp.float32), extras)
         out[pl.ds(q * MSG + MSG - 1, SUB, stride=MSG), :] = extras
-    for i in range(2):
-        for copy in copies[4 + 3 * i : 7 + 3 * i]:
-            copy.wait()
-        write_world([points], turns, world, range(i * frags // 2, (i + 1) * frags // 2))
-    for copy in copies[10:]:
+    copies[3].wait()
+    write_rotations(poses, turns)
+    for copy in copies[4:7]:
+        copy.wait()
+    write_world([points], turns, world, range(frags))
+    for copy in copies[7:]:
         copy.wait()
 
     def peer(p):
@@ -189,9 +184,8 @@
 
         turned[k * LANE : (k + 1) * LANE, lanes] = turn(at, same, parts, k, t)
     for k in range(3):
-        turned[(6 + k) * LANE : (7 + k) * LANE, lanes] = turn(
-            lambda u, k=k: source(u, k), same, parts, 6 + k, t
-        )
+        tiles = [source(u, k) for u in range(t // SUB, (t + LANE) // SUB)]
+        turned[(6 + k) * LANE : (7 + k) * LANE, lanes] = jnp.concatenate(tiles, axis=0).T
 
 
 def join_directions(side_a, side_b, joined, lanes, lanes_b):
@@ -356,7 +350,7 @@
             for u in range(t // SUB, (t + LANE) // SUB):
                 row = (first + u) * MSG + 3 * SUB
                 index[u * SUB : (u + 1) * SUB, :] = arrived[pl.ds(row, SUB), :].astype(jnp.int32)
-            side_a[:, lanes] = turn(extras, gather[...], parts, 9, t)
+            side_a[:, lanes] = turn(extras, gather[...], parts, 6, t)
             join_directions(side_a, remote_b, joined, lanes, lanes_b)
             turn_fields(
                 lambda u, k: arrived[pl.ds((first + u) * MSG + SUB * k, SUB), :],
@@ -471,7 +465,7 @@
             vmem(12 * frags * SUB, LANE),
             vmem(2 * SUB, LANE),
             vmem(devices * MSG, LANE),
-            pltpu.SemaphoreType.DMA((13,)),
+            pltpu.SemaphoreType.DMA((9,)),
             pltpu.SemaphoreType.DMA((devices // SUB,)),
         ],
         "hhhhhh",
@@ -499,7 +493,7 @@
             vmem(2 * SUB, pairs),
             vmem(2 * SUB, pairs),
             vmem(3 * SUB, pairs),
-            vmem(pairs, 9 * 2 * LANE, dtype=bf16),
+            vmem(pairs, 6 * 2 * LANE, dtype=bf16),
             vmem(9 * LANE, pairs),
             vmem(pairs // LANE * ROWS * SUB, LANE),
         ],
@@ -519,7 +513,7 @@
             vmem(3 * SUB, part),
             vmem(part, LANE),
             vmem(part, LANE, dtype=i32),
-            vmem(part, 10 * 2 * LANE, dtype=bf16),
+            vmem(part, 7 * 2 * LANE, dtype=bf16),
             vmem(9 * LANE, part),
             vmem(part // LANE * ROWS * SUB, LANE),
         ],

time: 39.4 us -> 39.1 us (level)
  transfers between devices with their start and end apart: 1 -> 1, of which waited for: 1 -> 1; matrix products, arithmetic and copies ran while one was open for 0% -> 0% of each run, Pallas kernels for 9% -> 10%
where the time goes in v8:
time: 39.1 us; the launch traced here: 38.9 us
  waiting for transfers between devices  11.4 us (29%)
  blocking collectives  10.2 us (26%)
  Pallas kernels  8.56 us (22%)
  starting transfers between devices  7.3 us (19%)
  between operations  0.76 us (2%)
  local copies, waits for them, and re-layouts  0.65 us (2%)
    all_to_all x1, waiting for transfers between devices, exchange(): sent = lax.all_to_all(sent, AXES, split_axis=0, concat_axis=0, tiled=True)  11.4 us
    all_to_all x1, blocking collectives, exchange(): sent = lax.all_to_all(sent, AXES, split_axis=0, concat_axis=0, tiled=True)  10.2 us
    all_to_all x1, starting transfers between devices, exchange(): sent = lax.all_to_all(sent, AXES, split_axis=0, concat_axis=0, tiled=True)  7.3 us
    pallas_call x1, Pallas kernels, local(): call(local_kernel, [array(devices * TARGET, LANE), array(2 * SUB, slots),...  3.73 us
    pallas_call x1, Pallas kernels, local(): call(pack_kernel, [array(devices * MSG, LANE)], [vmem(3, blocks, LANE), p...  2.21 us
    pallas_call x1, Pallas kernels, local(): call(functools.partial(remote_kernel, per_frag=per_frag), [array(devices...  1.87 us
  transfers between devices with their start and end apart: 1, of which 1 were waited for; matrix products, arithmetic and copies ran while one was open for 0% of the time, Pallas kernels for 10%

profile of v8, /device:TPU:0, one launch (start us, length us, event | category | flops | bytes accessed | tf_op | source)
XLA Modules:
  0.0 38.9 jit_solution(10391264801881382981)
XLA Ops:
  0.6 2.2 %shard_map.113 = f32[1056,128]{1,0:T(8,128)} custom-call(f32[3,256,128]{2,1,0:T(8,128)} %bitcast.10, f32[6,8]{1,0:T(8,128)} %poses.1, f32[6,2,8]{2,1,0:T(2,128)} %bitcast.15, s32[1,256]{1,0:T(1,128)} %src_h.1, s32[256,128]{1,0:T(8,128)} %bitcast.18, s32[1,32]{1,0:T(1,128)} %counts_h.1), custom_call_target="tpu_custom_call" | custom-call | tf_op jit(solution)/shard_map/pallas_call | solution.py:453
  2.9 0.0 copy-start
  2.9 0.0 copy-start.1
  2.9 0.0 copy-start.2
  2.9 0.0 copy-start.3
  2.9 0.0 copy-start.4
  2.9 0.0 copy-start.6
  2.9 7.3 %all-to-all-start = ((f32[32,1,4224]{2,1,0:T(1,128)}), f32[32,1,4224]{2,1,0:T(1,128)S(1)}, u32[]{:S(2)}, u32[]{:S(2)}) async-start(f32[32,1,4224]{2,1,0:T(1,128)} %bitcast.17), calls=%async_computation | async-start | bytes 1081344 | tf_op jit(solution)/shard_map/all_to_all | solution.py:424
  10.2 0.0 copy-start.5
  10.2 0.0 copy-done
  10.3 0.0 copy-done.1
  10.3 0.0 copy-done.2
  10.3 0.0 copy-done.3
  10.3 0.0 copy-done.4
  10.3 0.0 copy-done.6
  10.3 0.6 %copy-done.5 = s32[1,256]{1,0:T(1,128)S(1)} copy-done((s32[1,256]{1,0:T(1,128)S(1)}, s32[1,256]{1,0:T(1,128)}, u32[]{:S(2)}) %copy-start.5) | copy-done | bytes 1048
  10.9 3.7 %shard_map.114 = (f32[1536,128]{1,0:T(8,128)S(1)}, f32[16,256]{1,0:T(8,128)S(1)}, f32[18,8]{1,0:T(8,128)S(1)}, bf16[128,256]{1,0:T(8,128)(2,1)S(1)}, bf16[16,256...) custom-call(f32[3,256,128]{2,1,0:T(8,128)S(1)} %bitcast.11, ...), custom_call_target="tpu_custom_call" | custom-call | flops 6553600 | bytes 4000000 | tf_op jit(solution)/shard_map/pallas_call | solution.py:476
  14.7 11.4 %all-to-all-done = f32[32,1,4224]{2,1,0:T(1,128)S(1)} async-done(((f32[32,1,4224]{2,1,0:T(1,128)}), f32[32,1,4224]{2,1,0:T(1,128)S(1)}, u32[]{:S(2)}, u32[]{:S(2)}) %all-to-all-start) | async-done | bytes 540704 | tf_op jit(solution)/shard_map/all_to_all | solution.py:424
  26.1 1.9 %shard_map.115 = (f32[64,128]{1,0:T(8,128)S(1)}, f32[18,8]{1,0:T(8,128)S(1)}) custom-call(f32[1056,128]{1,0:T(8,128)S(1)} %bitcast.9, f32[1536,128]{1,0:T(8,128)S(1)} %get-tuple-element.13.staged, f32[16,256]{1,0:T(8,128)S(1)} %get-tuple-element.14.remote_b, f32[18,8]{1,0:T(8,128)S(1)} %get-tuple-element.15.local_totals, s32[1,256]{1,0:T(1,128)S(1)} %copy-done.5, ...), custom_call_target="tpu_custom_call" | custom-call | tf_op jit(solution)/shard_map/pallas_call | solution.py:508
  27.9 10.2 %all_to_all.10 = f32[32,1,256]{2,1,0:T(1,128)S(1)} all-to-all(f32[32,1,256]{2,1,0:T(1,128)S(1)} %bitcast.14), channel_id=1, replica_groups=mesh['tile'=8,'band'=4] {'tile','band'}, dimensions={0} | all-to-all | bytes 65536 | tf_op jit(solution)/shard_map/all_to_all | solution.py:424
  38.1 0.7 %shard_map.116 = (f32[6,8]{1,0:T(8,128)}, f32[6,2,8]{2,1,0:T(2,128)}) custom-call(f32[64,128]{1,0:T(8,128)S(1)} %bitcast.13, f32[18,8]{1,0:T(8,128)S(1)} %get-tuple-element.21.totals), custom_call_target="tpu_custom_call" | custom-call | tf_op jit(solution)/shard_map/pallas_call | solution.py:523
Async XLA Ops:
  2.9 7.4 %copy-start = (f32[256,3,128]{2,0,1:T(8,128)S(1)}, f32[256,3,128]{2,0,1:T(8,128)}, u32[]{:S(2)}) copy-start(f32[256,3,128]{2,0,1:T(8,128)} %param.10) | copy-start | bytes 1179652
  2.9 7.4 %copy-start.1 = (f32[256,3,128]{2,0,1:T(8,128)S(1)}, f32[256,3,128]{2,0,1:T(8,128)}, u32[]{:S(2)}) copy-start(f32[256,3,128]{2,0,1:T(8,128)} %param.11) | copy-start | bytes 1179652
  2.9 7.4 %copy-start.2 = (s32[256,128]{1,0:T(8,128)S(1)}, s32[256,128]{1,0:T(8,128)}, u32[]{:S(2)}) copy-start(s32[256,128]{1,0:T(8,128)} %maps.1) | copy-start | bytes 393220
  2.9 7.4 %copy-start.3 = (f32[2,6,8]{2,0,1:T(2,128)S(1)}, f32[2,6,8]{2,0,1:T(2,128)}, u32[]{:S(2)}) copy-start(f32[2,6,8]{2,0,1:T(2,128)} %param.13) | copy-start | bytes 1156
  2.9 7.4 %copy-start.4 = (f32[6,8]{1,0:T(8,128)S(1)}, f32[6,8]{1,0:T(8,128)}, u32[]{:S(2)}) copy-start(f32[6,8]{1,0:T(8,128)} %poses.1) | copy-start | bytes 580
  2.9 7.4 %copy-start.6 = (s32[2,256]{1,0:T(2,128)S(1)}, s32[2,256]{1,0:T(2,128)}, u32[]{:S(2)}) copy-start(s32[2,256]{1,0:T(2,128)} %pairs_v.1) | copy-start | bytes 6148
  2.9 23.2 %all-to-all-start = ((f32[32,1,4224]{2,1,0:T(1,128)}), f32[32,1,4224]{2,1,0:T(1,128)S(1)}, u32[]{:S(2)}, u32[]{:S(2)}) async-start(f32[32,1,4224]{2,1,0:T(1,128)} %bitcast.17), calls=%async_computation | async-start | bytes 1081344 | tf_op jit(solution)/shard_map/all_to_all | solution.py:424
  10.2 0.7 %copy-start.5 = (s32[1,256]{1,0:T(1,128)S(1)}, s32[1,256]{1,0:T(1,128)}, u32[]{:S(2)}) copy-start(s32[1,256]{1,0:T(1,128)} %dst_v.3) | copy-start | bytes 3076

commit v9 on v8

--- a/solution.py
+++ b/solution.py
@@ -8,6 +8,7 @@
 from jax.sharding import PartitionSpec as P
 
 AXES = ("tile", "band")
+ORDER = ("band", "tile")
 SUB = 8
 LANE = 128
 MSG = 4 * SUB + 1
@@ -90,14 +91,24 @@
             table[6 * v + j : 6 * v + j + 1, 0:frags] = directions[j, v : v + 1, :]
 
 
-def index_tile(row_ref, first, offset):
-    tile = first // LANE * LANE
-    return pick(row_ref[0:1, pl.ds(tile, LANE)], offset + first % LANE)
+def peer_at(place, sizes):
+    n_tile, n_band = sizes
+    tile = lax.bitwise_and(place, n_tile - 1)
+    return tile * n_band + lax.shift_right_logical(place, shift_of(n_tile))
+
+
+def entries(row_ref, index):
+    out = jnp.zeros((SUB, LANE), row_ref.dtype)
+    tile = lax.shift_right_logical(index, shift_of(LANE))
+    for t in range(row_ref.shape[1] // LANE):
+        hit = pick(row_ref[0:1, t * LANE : (t + 1) * LANE], lax.bitwise_and(index, LANE - 1))
+        out = jnp.where(tile == t, hit, out)
+    return out
 
 
 def pack_kernel(
     points_h, poses_h, directions_h, src_h, maps_h, counts_h, out_h,
-    points, poses, directions, src_s, src_v, maps, used, world, turns, table, out, sems, out_sems,
+    points, poses, directions, src_s, src_v, maps, used, world, turns, table, out, sems, out_sems, *, sizes,
 ):
     devices = counts_h.shape[1]
     per_frag = points.shape[1] // poses.shape[1]
@@ -118,9 +129,10 @@
     slot = lax.shift_right_logical(iota(1), shift_of(GROUP))
     field = lax.bitwise_and(iota(1), GROUP - 1)
     for q in range(0, devices, SUB):
-        block = index_tile(src_v, q * SUB, iota(0) * SUB + slot)
+        block = entries(src_v, peer_at(iota(0) + q, sizes) * SUB + slot)
         frag = lax.shift_right_logical(block, shift_of(per_frag))
-        limit = jnp.sum(jnp.where(peers == row + q, limits, 0.0), axis=1, keepdims=True)
+        hit = peers == peer_at(row + q, sizes)
+        limit = jnp.sum(jnp.where(hit, limits, 0.0), axis=1, keepdims=True)
         extras = jnp.where(slot.astype(jnp.float32) < limit, 1.0, 0.0)
         for j in range(12):
             extras = jnp.where(field == j, pick(table[j : j + 1, :], frag), extras)
@@ -134,12 +146,13 @@
     for copy in copies[7:]:
         copy.wait()
 
-    def peer(p):
+    def peer(q):
+        p = peer_at(q, sizes)
         for s in range(SUB):
             block = src_s[0, p * SUB + s]
-            out[pl.ds(p * MSG + s, 3, stride=SUB), :] = world[pl.ds(block, 3, stride=stride), :]
+            out[pl.ds(q * MSG + s, 3, stride=SUB), :] = world[pl.ds(block, 3, stride=stride), :]
         rows = maps[pl.ds(pl.multiple_of(p * SUB, SUB), SUB), :]
-        out[pl.ds(p * MSG + 3 * SUB, SUB), :] = rows.astype(jnp.float32)
+        out[pl.ds(q * MSG + 3 * SUB, SUB), :] = rows.astype(jnp.float32)
 
     def piece(i):
         rows = pl.ds(pl.multiple_of(i * SUB * MSG, SUB), SUB * MSG)
@@ -275,15 +288,20 @@
 
 def local_kernel(
     points, normals, poses, directions, pairs_s, pairs_v, maps, dst_s, dst_v,
-    staged, remote_b, totals, same, gather, place, mine,
-    world, turns, table, sources, targets, side_a, side_b, joined, parts, turned, partial,
+    staged, remote_b, remote_frag, totals, same, gather, place, mine,
+    world, turns, table, sources, targets, side_a, side_b, joined, parts, turned, partial, *, sizes,
 ):
     per_frag = points.shape[1] // poses.shape[1]
     stride = points.shape[1] + SUB
     constants(same, gather, place, mine)
     table[...] = jnp.zeros_like(table)
     write_directions(directions, table)
-    look_up(table, frag_of(dst_v[...], per_frag), remote_b)
+    for at in range(0, dst_v.shape[1], LANE):
+        flat = iota(1) + at
+        peer = peer_at(lax.shift_right_logical(flat, shift_of(SUB)), sizes)
+        block = entries(dst_v, peer * SUB + lax.bitwise_and(flat, SUB - 1))
+        remote_frag[0:1, at : at + LANE] = frag_of(block, per_frag)[0:1, :]
+    look_up(table, remote_frag[...], remote_b)
     frag_a, frag_b = frag_of(pairs_v[0:1, :], per_frag), frag_of(pairs_v[1:2, :], per_frag)
     look_up(table, frag_a, side_a)
     look_up(table, frag_b, side_b)
@@ -294,7 +312,7 @@
 
     def stage_remote(g, carry):
         for s in range(SUB):
-            block = dst_s[0, g * SUB + s]
+            block = dst_s[0, peer_at(g, sizes) * SUB + s]
             staged[pl.ds(g * TARGET + s, 6, stride=SUB), :] = world[pl.ds(block, 6, stride=stride), :]
         return carry
 
@@ -326,8 +344,8 @@
 
 
 def remote_kernel(
-    arrived, staged, remote_b, local_totals, dst_v, same, gather, place, mine,
-    back, totals, side_a, joined, frags, index, parts, turned, partial, *, per_frag,
+    arrived, staged, remote_b, remote_frag, local_totals, same, gather, place, mine,
+    back, totals, side_a, joined, frags, index, parts, turned, partial,
 ):
     f32 = jnp.float32
     pairs = parts.shape[0]
@@ -377,7 +395,7 @@
                     rows[half] = rows[half] + jnp.dot(
                         mine[:, lanes], piece, preferred_element_type=f32
                     )
-            total = total + target_side(by_frag(sums, frag_of(dst_v[0:1, lanes_b], per_frag)))
+            total = total + target_side(by_frag(sums, remote_frag[0:1, lanes_b]))
         for half in range(2):
             back[pl.ds(2 * first + half, peers, stride=2), :] = rows[half]
         return total
@@ -421,7 +439,7 @@
 
 def exchange(rows, devices):
     sent = rows.reshape(devices, 1, -1)
-    sent = lax.all_to_all(sent, AXES, split_axis=0, concat_axis=0, tiled=True)
+    sent = lax.all_to_all(sent, ORDER, split_axis=0, concat_axis=0, tiled=True)
     return sent.reshape(rows.shape)
 
 
@@ -429,7 +447,8 @@
     points, normals, poses, directions, local_pairs, local_maps,
     remote_src, remote_maps, remote_dst, counts,
 ):
-    devices = lax.axis_size("tile") * lax.axis_size("band")
+    sizes = lax.axis_size("tile"), lax.axis_size("band")
+    devices = sizes[0] * sizes[1]
     blocks, _, count = points.shape
     frags = poses.shape[1]
     slots = remote_src.shape[1]
@@ -451,7 +470,7 @@
     i32, bf16 = jnp.int32, jnp.bfloat16
     part = PEERS * SUB
     (message,) = call(
-        pack_kernel,
+        functools.partial(pack_kernel, sizes=sizes),
         [array(devices * MSG, LANE)],
         [
             vmem(3, blocks, LANE),
@@ -473,11 +492,12 @@
         out_space="h",
     )(*[in_hbm(x) for x in (points, poses, directions, remote_src, remote_maps[0], counts)])
     arrived = exchange(message, devices)
-    staged, remote_b, totals, same, gather, place, mine = call(
-        local_kernel,
+    staged, remote_b, remote_frag, totals, same, gather, place, mine = call(
+        functools.partial(local_kernel, sizes=sizes),
         [
             array(devices * TARGET, LANE),
             array(2 * SUB, slots),
+            array(1, slots, dtype=i32),
             array(18, frags),
             array(LANE, 2 * LANE, dtype=bf16),
             array(GROUP, 2 * LANE, dtype=bf16),
@@ -506,7 +526,7 @@
         remote_dst, remote_dst,
     )
     back, totals = call(
-        functools.partial(remote_kernel, per_frag=per_frag),
+        remote_kernel,
         [array(devices * 2, LANE), array(18, frags)],
         [
             vmem(2 * SUB, part),
@@ -518,7 +538,7 @@
             vmem(part // LANE * ROWS * SUB, LANE),
         ],
         "vvvvvvvvv",
-    )(arrived, staged, remote_b, totals, remote_dst, same, gather, place, mine)
+    )(arrived, staged, remote_b, remote_frag, totals, same, gather, place, mine)
     back = exchange(back, devices)
     gradient, hess = call(
         functools.partial(final_kernel, per_frag=per_frag),

time: 39.1 us -> 39.1 us (level)
  blocking collectives: 10.2 us -> 9.28 us
  waiting for transfers between devices: 11.4 us -> 12.2 us
    all_to_all x1, blocking collectives: 10.2 us -> 9.28 us  [exchange(): sent = lax.all_to_all(sent, ORDER, split_axis=0, concat_axis=0, tiled=True)]
    all_to_all x1, waiting for transfers between devices: 11.4 us -> 12.2 us  [exchange(): sent = lax.all_to_all(sent, ORDER, split_axis=0, concat_axis=0, tiled=True)]
where the time goes in v9:
time: 39.1 us; the launch traced here: 38.9 us
  waiting for transfers between devices  12.2 us (31%)
  blocking collectives  9.28 us (24%)
  Pallas kernels  8.68 us (22%)
  starting transfers between devices  7.3 us (19%)
  between operations  0.76 us (2%)
  local copies, waits for them, and re-layouts  0.65 us (2%)
    all_to_all x1, waiting for transfers between devices, exchange(): sent = lax.all_to_all(sent, ORDER, split_axis=0, concat_axis=0, tiled=True)  12.2 us
    all_to_all x1, blocking collectives, exchange(): sent = lax.all_to_all(sent, ORDER, split_axis=0, concat_axis=0, tiled=True)  9.28 us
    all_to_all x1, starting transfers between devices, exchange(): sent = lax.all_to_all(sent, ORDER, split_axis=0, concat_axis=0, tiled=True)  7.3 us
    pallas_call x1, Pallas kernels, local(): call(functools.partial(local_kernel, sizes=sizes), [array(devices * TARGE...  3.81 us
    pallas_call x1, Pallas kernels, local(): call(functools.partial(pack_kernel, sizes=sizes), [array(devices * MSG, L...  2.28 us
    pallas_call x1, Pallas kernels, local(): call(remote_kernel, [array(devices * 2, LANE), array(18, frags)], [vmem(2...  1.85 us
  transfers between devices with their start and end apart: 1, of which 1 were waited for; matrix products, arithmetic and copies ran while one was open for 0% of the time, Pallas kernels for 10%

profile of v9, /device:TPU:0, one launch (start us, length us, event | category | flops | bytes accessed | tf_op | source)
XLA Modules:
  0.0 38.9 jit_solution(7980763941648496374)
XLA Ops:
  0.6 2.3 %shard_map.113 = f32[1056,128]{1,0:T(8,128)} custom-call(f32[3,256,128]{2,1,0:T(8,128)} %bitcast.10, f32[6,8]{1,0:T(8,128)} %poses.1, f32[6,2,8]{2,1,0:T(2,128)} %bitcast.15, s32[1,256]{1,0:T(1,128)} %src_h.1, s32[256,128]{1,0:T(8,128)} %bitcast.18, s32[1,32]{1,0:T(1,128)} %counts_h.1), custom_call_target="tpu_custom_call" | custom-call | tf_op jit(solution)/shard_map/pallas_call | solution.py:472
  2.9 0.0 copy-start
  2.9 0.0 copy-start.1
  2.9 0.0 copy-start.2
  3.0 0.0 copy-start.3
  3.0 0.0 copy-start.4
  3.0 0.0 copy-start.5
  3.0 7.3 %all-to-all-start = ((f32[32,1,4224]{2,1,0:T(1,128)}), f32[32,1,4224]{2,1,0:T(1,128)S(1)}, u32[]{:S(2)}, u32[]{:S(2)}) async-start(f32[32,1,4224]{2,1,0:T(1,128)} %bitcast.17), calls=%async_computation | async-start | bytes 1081344 | tf_op jit(solution)/shard_map/all_to_all | solution.py:442
  10.3 0.0 copy-start.6
  10.3 0.0 copy-done
  10.3 0.0 copy-done.1
  10.3 0.0 copy-done.2
  10.3 0.0 copy-done.3
  10.4 0.0 copy-done.4
  10.4 0.0 copy-done.5
  10.4 0.6 %copy-done.6 = s32[1,256]{1,0:T(1,128)S(1)} copy-done((s32[1,256]{1,0:T(1,128)S(1)}, s32[1,256]{1,0:T(1,128)}, u32[]{:S(2)}) %copy-start.6) | copy-done | bytes 1048
  11.0 3.8 %shard_map.114 = (f32[1536,128]{1,0:T(8,128)S(1)}, f32[16,256]{1,0:T(8,128)S(1)}, s32[1,256]{1,0:T(1,128)S(1)}, f32[18,8]{1,0:T(8,128)S(1)}, bf16[128,256]{1,0:T...) custom-call(f32[3,256,128]{2,1,0:T(8,128)S(1)} %bitcast.11, ...), custom_call_target="tpu_custom_call" | custom-call | flops 6553600 | bytes 4000000 | tf_op jit(solution)/shard_map/pallas_call | solution.py:495
  14.8 12.2 %all-to-all-done = f32[32,1,4224]{2,1,0:T(1,128)S(1)} async-done(((f32[32,1,4224]{2,1,0:T(1,128)}), f32[32,1,4224]{2,1,0:T(1,128)S(1)}, u32[]{:S(2)}, u32[]{:S(2)}) %all-to-all-start) | async-done | bytes 540704 | tf_op jit(solution)/shard_map/all_to_all | solution.py:442
  27.0 1.8 %shard_map.115 = (f32[64,128]{1,0:T(8,128)S(1)}, f32[18,8]{1,0:T(8,128)S(1)}) custom-call(f32[1056,128]{1,0:T(8,128)S(1)} %bitcast.9, f32[1536,128]{1,0:T(8,128)S(1)} %get-tuple-element.14.staged, f32[16,256]{1,0:T(8,128)S(1)} %get-tuple-element.15.remote_b, s32[1,256]{1,0:T(1,128)S(1)} %get-tuple-element.16.remote_frag, ...), custom_call_target="tpu_custom_call" | custom-call | tf_op jit(solution)/shard_map/pallas_call | solution.py:528
  28.9 9.3 %all_to_all.10 = f32[32,1,256]{2,1,0:T(1,128)S(1)} all-to-all(f32[32,1,256]{2,1,0:T(1,128)S(1)} %bitcast.14), channel_id=1, replica_groups=mesh['tile'=8,'band'=4] {'band','tile'}, dimensions={0} | all-to-all | bytes 65536 | tf_op jit(solution)/shard_map/all_to_all | solution.py:442
  38.1 0.7 %shard_map.116 = (f32[6,8]{1,0:T(8,128)}, f32[6,2,8]{2,1,0:T(2,128)}) custom-call(f32[64,128]{1,0:T(8,128)S(1)} %bitcast.13, f32[18,8]{1,0:T(8,128)S(1)} %get-tuple-element.23.totals), custom_call_target="tpu_custom_call" | custom-call | tf_op jit(solution)/shard_map/pallas_call | solution.py:543
Async XLA Ops:
  2.9 7.4 %copy-start = (f32[256,3,128]{2,0,1:T(8,128)S(1)}, f32[256,3,128]{2,0,1:T(8,128)}, u32[]{:S(2)}) copy-start(f32[256,3,128]{2,0,1:T(8,128)} %param.10) | copy-start | bytes 1179652
  2.9 7.4 %copy-start.1 = (f32[256,3,128]{2,0,1:T(8,128)S(1)}, f32[256,3,128]{2,0,1:T(8,128)}, u32[]{:S(2)}) copy-start(f32[256,3,128]{2,0,1:T(8,128)} %param.11) | copy-start | bytes 1179652
  2.9 7.4 %copy-start.2 = (s32[256,128]{1,0:T(8,128)S(1)}, s32[256,128]{1,0:T(8,128)}, u32[]{:S(2)}) copy-start(s32[256,128]{1,0:T(8,128)} %maps.1) | copy-start | bytes 393220
  3.0 7.4 %copy-start.3 = (f32[2,6,8]{2,0,1:T(2,128)S(1)}, f32[2,6,8]{2,0,1:T(2,128)}, u32[]{:S(2)}) copy-start(f32[2,6,8]{2,0,1:T(2,128)} %param.13) | copy-start | bytes 1156
  3.0 7.4 %copy-start.4 = (f32[6,8]{1,0:T(8,128)S(1)}, f32[6,8]{1,0:T(8,128)}, u32[]{:S(2)}) copy-start(f32[6,8]{1,0:T(8,128)} %poses.1) | copy-start | bytes 580
  3.0 7.4 %copy-start.5 = (s32[2,256]{1,0:T(2,128)S(1)}, s32[2,256]{1,0:T(2,128)}, u32[]{:S(2)}) copy-start(s32[2,256]{1,0:T(2,128)} %pairs_v.1) | copy-start | bytes 6148
  3.0 24.0 %all-to-all-start = ((f32[32,1,4224]{2,1,0:T(1,128)}), f32[32,1,4224]{2,1,0:T(1,128)S(1)}, u32[]{:S(2)}, u32[]{:S(2)}) async-start(f32[32,1,4224]{2,1,0:T(1,128)} %bitcast.17), calls=%async_computation | async-start | bytes 1081344 | tf_op jit(solution)/shard_map/all_to_all | solution.py:442
  10.3 0.7 %copy-start.6 = (s32[1,256]{1,0:T(1,128)S(1)}, s32[1,256]{1,0:T(1,128)}, u32[]{:S(2)}) copy-start(s32[1,256]{1,0:T(1,128)} %dst_v.1) | copy-start | bytes 3076

commit v10 on v9

--- a/solution.py
+++ b/solution.py
@@ -174,31 +174,49 @@
     return high, (values - high.astype(jnp.float32)).astype(jnp.bfloat16)
 
 
-def turn(at, left, parts, i, t):
-    columns = slice(i * 2 * LANE, i * 2 * LANE + LANE), slice(i * 2 * LANE + LANE, (i + 1) * 2 * LANE)
-    for u in range(t // SUB, (t + LANE) // SUB, 2):
+def turn_steps(at, left, parts, i, t, put):
+    first, second = i * 2 * LANE, i * 2 * LANE + LANE
+
+    def split(u):
         high, low = halves_of(jnp.concatenate([at(u), at(u + 1)], axis=0))
-        parts[u * SUB : (u + 2) * SUB, columns[0]] = high
-        parts[u * SUB : (u + 2) * SUB, columns[1]] = low
-    return lax.dot_general(
-        left,
-        parts[t : t + LANE, i * 2 * LANE : (i + 1) * 2 * LANE],
-        (((1,), (1,)), ((), ())),
-        preferred_element_type=jnp.float32,
-    )
-
-
-def turn_fields(source, target, index, same, parts, turned, t):
-    lanes = slice(t, t + LANE)
+        parts[u * SUB : (u + 2) * SUB, first : first + LANE] = high
+        parts[u * SUB : (u + 2) * SUB, second : second + LANE] = low
+
+    def multiply():
+        put(
+            lax.dot_general(
+                left,
+                parts[t : t + LANE, first : second + LANE],
+                (((1,), (1,)), ((), ())),
+                preferred_element_type=jnp.float32,
+            )
+        )
+
+    tiles = range(t // SUB, (t + LANE) // SUB, 2)
+    return [functools.partial(split, u) for u in tiles] + [multiply]
+
+
+def field_steps(source, target, index, same, parts, turned, t):
+    def put(k, value):
+        turned[k * LANE : (k + 1) * LANE, t : t + LANE] = value
+
+    def turn_source(k):
+        tiles = [source(u, k) for u in range(t // SUB, (t + LANE) // SUB)]
+        put(6 + k, jnp.concatenate(tiles, axis=0).T)
+
+    steps = []
     for k in range(6):
 
         def at(u, k=k):
             return pick(target(u, k), index(u))
 
-        turned[k * LANE : (k + 1) * LANE, lanes] = turn(at, same, parts, k, t)
-    for k in range(3):
-        tiles = [source(u, k) for u in range(t // SUB, (t + LANE) // SUB)]
-        turned[(6 + k) * LANE : (7 + k) * LANE, lanes] = jnp.concatenate(tiles, axis=0).T
+        steps += turn_steps(at, same, parts, k, t, functools.partial(put, k))
+    return steps + [functools.partial(turn_source, k) for k in range(3)]
+
+
+def run(steps):
+    for step in steps:
+        step()
 
 
 def join_directions(side_a, side_b, joined, lanes, lanes_b):
@@ -209,13 +227,14 @@
         joined[12 + 3 * v : 15 + 3 * v, lanes] = side_b[turn_rows, lanes_b]
 
 
-def point_sums(turned, joined, partial, t):
+def point_sums(turned, joined, partial, t, between=()):
     lanes = slice(t, t + LANE)
     first = t // LANE * ROWS * SUB
-
-    def add(i, totals):
-        start = pl.multiple_of(i * SUB, SUB)
-        field = [turned[pl.ds(start + k * LANE, SUB), lanes] for k in range(9)]
+    zero = jnp.zeros((SUB, LANE), jnp.float32)
+    totals = [zero] * 27
+    rounds = LANE // SUB
+    for i in range(rounds):
+        field = [turned[i * SUB + k * LANE : (i + 1) * SUB + k * LANE, lanes] for k in range(9)]
         way = [joined[j : j + 1, lanes] for j in range(18)]
         y, n, x = field[0:3], field[3:6], field[6:9]
         p, q = cross(x, n), cross(y, n)
@@ -228,10 +247,8 @@
             terms += [s * value for value in p + n]
         for s in scalars:
             terms += [s * value for value in q]
-        return tuple(total + term for total, term in zip(totals, terms))
-
-    zero = jnp.zeros((SUB, LANE), jnp.float32)
-    totals = lax.fori_loop(0, LANE // SUB, add, (zero,) * 27, unroll=LANE // SUB)
+        totals = [total + term for total, term in zip(totals, terms)]
+        run(between[i * len(between) // rounds : (i + 1) * len(between) // rounds])
     for j in range(ROWS):
         partial[first + j * SUB : first + (j + 1) * SUB, :] = totals[j] if j < 27 else zero
     total = partial[pl.ds(first, ROWS, stride=SUB), :]
@@ -327,8 +344,9 @@
 
     lax.fori_loop(0, pairs_s.shape[1] // SUB, stage_local, 0, unroll=4)
     total = jnp.zeros(totals.shape, jnp.float32)
-    for t in range(0, pairs_s.shape[1], LANE):
-        turn_fields(
+    tiles = range(0, pairs_s.shape[1], LANE)
+    steps = [
+        field_steps(
             lambda u, k: sources[u * SOURCE + k * SUB : u * SOURCE + (k + 1) * SUB, :],
             lambda u, k: targets[u * TARGET + k * SUB : u * TARGET + (k + 1) * SUB, :],
             lambda u: maps[u * SUB : (u + 1) * SUB, :],
@@ -337,7 +355,12 @@
             turned,
             t,
         )
-        sums = point_sums(turned, joined, partial, t)
+        for t in tiles
+    ]
+    run(steps[0])
+    for i, t in enumerate(tiles):
+        between = steps[i + 1] if i + 1 < len(steps) else ()
+        sums = point_sums(turned, joined, partial, t, between)
         total = total + by_frag(sums, frag_a[:, t : t + LANE])[0:18, :]
         total = total + target_side(by_frag(sums, frag_b[:, t : t + LANE]))
     totals[...] = total
@@ -355,52 +378,91 @@
 
     def block(c, total):
         first = c * peers
+        start = c * pairs if isinstance(c, int) else pl.multiple_of(c * pairs, LANE)
+
+        def row_at(u, size, row):
+            at = (first + u) * size + row
+            return at if isinstance(c, int) or size == MSG else pl.multiple_of(at, SUB)
 
         def extras(u):
-            row = arrived[pl.ds((first + u) * MSG + 4 * SUB, 1), :]
+            row = arrived[pl.ds(row_at(u, MSG, 4 * SUB), 1), :]
             frags[u * SUB : (u + 1) * SUB, :] = pick(row, iota(0) * GROUP + 13)
             return jnp.where(own, jnp.broadcast_to(row, (SUB, LANE)), 0.0)
 
+        def front(t):
+            lanes = slice(t, t + LANE)
+
+            def indices():
+                for u in range(t // SUB, (t + LANE) // SUB):
+                    rows = arrived[pl.ds(row_at(u, MSG, 3 * SUB), SUB), :]
+                    index[u * SUB : (u + 1) * SUB, :] = rows.astype(jnp.int32)
+
+            def put(value):
+                side_a[:, lanes] = value
+                join_directions(side_a, remote_b, joined, lanes, pl.ds(start + t, LANE))
+
+            return (
+                [indices]
+                + turn_steps(extras, gather[...], parts, 6, t, put)
+                + field_steps(
+                    lambda u, k: arrived[pl.ds(row_at(u, MSG, SUB * k), SUB), :],
+                    lambda u, k: staged[pl.ds(row_at(u, TARGET, SUB * k), SUB), :],
+                    lambda u: index[u * SUB : (u + 1) * SUB, :],
+                    same[...],
+                    parts,
+                    turned,
+                    t,
+                )
+            )
+
         rows = [jnp.zeros((peers, LANE), f32) for half in range(2)]
-        for t in range(0, pairs, LANE):
+
+        def back_steps(sums, t):
             lanes = slice(t, t + LANE)
-            lanes_b = pl.ds(pl.multiple_of(c * pairs, LANE) + t, LANE)
-            for u in range(t // SUB, (t + LANE) // SUB):
-                row = (first + u) * MSG + 3 * SUB
-                index[u * SUB : (u + 1) * SUB, :] = arrived[pl.ds(row, SUB), :].astype(jnp.int32)
-            side_a[:, lanes] = turn(extras, gather[...], parts, 6, t)
-            join_directions(side_a, remote_b, joined, lanes, lanes_b)
-            turn_fields(
-                lambda u, k: arrived[pl.ds((first + u) * MSG + SUB * k, SUB), :],
-                lambda u, k: staged[
-                    pl.ds(pl.multiple_of((first + u) * TARGET, SUB) + SUB * k, SUB), :
-                ],
-                lambda u: index[u * SUB : (u + 1) * SUB, :],
-                same[...],
-                parts,
-                turned,
-                t,
-            )
-            sums = point_sums(turned, joined, partial, t) * side_a[12:13, lanes]
-            placed = lax.dot_general(
-                jnp.concatenate(halves_of(sums), axis=0),
-                place[...],
-                (((0,), (0,)), ((), ())),
-                preferred_element_type=f32,
-            )
-            hit = frags[lanes, :] == jnp.broadcast_to(slot, (LANE, LANE))
-            for half in range(2):
-                part = jnp.where(hit, placed[:, half * LANE : (half + 1) * LANE], 0.0)
+            held = {}
+
+            def scatter():
+                held["placed"] = lax.dot_general(
+                    jnp.concatenate(halves_of(sums), axis=0),
+                    place[...],
+                    (((0,), (0,)), ((), ())),
+                    preferred_element_type=f32,
+                )
+
+            def add(half):
+                hit = frags[lanes, :] == jnp.broadcast_to(slot, (LANE, LANE))
+                part = jnp.where(hit, held["placed"][:, half * LANE : (half + 1) * LANE], 0.0)
                 for piece in halves_of(part):
                     rows[half] = rows[half] + jnp.dot(
                         mine[:, lanes], piece, preferred_element_type=f32
                     )
-            total = total + target_side(by_frag(sums, remote_frag[0:1, lanes_b]))
+
+            def own_side():
+                frag = remote_frag[0:1, pl.ds(start + t, LANE)]
+                held["total"] = target_side(by_frag(sums, frag))
+
+            return [scatter, functools.partial(add, 0), functools.partial(add, 1), own_side], held
+
+        tiles = range(0, pairs, LANE)
+        steps = front(tiles[0])
+        run(steps)
+        behind, held = [], []
+        for t in tiles:
+            between = behind + (front(t + LANE) if t + LANE < pairs else [])
+            sums = point_sums(turned, joined, partial, t, between)
+            sums = sums * side_a[12:13, t : t + LANE]
+            behind, kept = back_steps(sums, t)
+            held.append(kept)
+        run(behind)
+        for kept in held:
+            total = total + kept["total"]
         for half in range(2):
             back[pl.ds(2 * first + half, peers, stride=2), :] = rows[half]
         return total
 
-    totals[...] = lax.fori_loop(0, back.shape[0] // (2 * peers), block, local_totals[...])
+    blocks = back.shape[0] // (2 * peers)
+    total = local_totals[...]
+    totals[...] = block(0, total) if blocks == 1 else lax.fori_loop(0, blocks, block, total)
 
 
 def final_kernel(back, totals, gradient, hess, *, per_frag):

time: 39.1 us -> 38.9 us (level)
  no operation moved by 1% of the time
where the time goes in v10:
time: 38.9 us; the launch traced here: 38.6 us
  waiting for transfers between devices  12.3 us (32%)
  blocking collectives  9.28 us (24%)
  Pallas kernels  8.32 us (21%)
  starting transfers between devices  7.3 us (19%)
  between operations  0.76 us (2%)
  local copies, waits for them, and re-layouts  0.65 us (2%)
    all_to_all x1, waiting for transfers between devices, exchange(): sent = lax.all_to_all(sent, ORDER, split_axis=0, concat_axis=0, tiled=True)  12.3 us
    all_to_all x1, blocking collectives, exchange(): sent = lax.all_to_all(sent, ORDER, split_axis=0, concat_axis=0, tiled=True)  9.28 us
    all_to_all x1, starting transfers between devices, exchange(): sent = lax.all_to_all(sent, ORDER, split_axis=0, concat_axis=0, tiled=True)  7.3 us
    pallas_call x1, Pallas kernels, local(): call(functools.partial(local_kernel, sizes=sizes), [array(devices * TARGE...  3.7 us
    pallas_call x1, Pallas kernels, local(): call(functools.partial(pack_kernel, sizes=sizes), [array(devices * MSG, L...  2.28 us
    pallas_call x1, Pallas kernels, local(): call(remote_kernel, [array(devices * 2, LANE), array(18, frags)], [vmem(2...  1.59 us
  transfers between devices with their start and end apart: 1, of which 1 were waited for; matrix products, arithmetic and copies ran while one was open for 0% of the time, Pallas kernels for 10%

profile of v10, /device:TPU:0, one launch (start us, length us, event | category | flops | bytes accessed | tf_op | source)
XLA Modules:
  0.0 38.6 jit_solution(4622258927976455237)
XLA Ops:
  0.6 2.3 %shard_map.113 = f32[1056,128]{1,0:T(8,128)} custom-call(f32[3,256,128]{2,1,0:T(8,128)} %bitcast.10, f32[6,8]{1,0:T(8,128)} %poses.1, f32[6,2,8]{2,1,0:T(2,128)} %bitcast.15, s32[1,256]{1,0:T(1,128)} %src_h.1, s32[256,128]{1,0:T(8,128)} %bitcast.18, s32[1,32]{1,0:T(1,128)} %counts_h.1), custom_call_target="tpu_custom_call" | custom-call | tf_op jit(solution)/shard_map/pallas_call | solution.py:534
  2.9 0.0 copy-start
  2.9 0.0 copy-start.1
  2.9 0.0 copy-start.2
  3.0 0.0 copy-start.3
  3.0 0.0 copy-start.4
  3.0 0.0 copy-start.5
  3.0 7.3 %all-to-all-start = ((f32[32,1,4224]{2,1,0:T(1,128)}), f32[32,1,4224]{2,1,0:T(1,128)S(1)}, u32[]{:S(2)}, u32[]{:S(2)}) async-start(f32[32,1,4224]{2,1,0:T(1,128)} %bitcast.17), calls=%async_computation | async-start | bytes 1081344 | tf_op jit(solution)/shard_map/all_to_all | solution.py:504
  10.3 0.0 copy-start.6
  10.3 0.0 copy-done
  10.3 0.0 copy-done.1
  10.3 0.0 copy-done.2
  10.3 0.0 copy-done.3
  10.4 0.0 copy-done.4
  10.4 0.0 copy-done.5
  10.4 0.6 %copy-done.6 = s32[1,256]{1,0:T(1,128)S(1)} copy-done((s32[1,256]{1,0:T(1,128)S(1)}, s32[1,256]{1,0:T(1,128)}, u32[]{:S(2)}) %copy-start.6) | copy-done | bytes 1048
  11.0 3.7 %shard_map.114 = (f32[1536,128]{1,0:T(8,128)S(1)}, f32[16,256]{1,0:T(8,128)S(1)}, s32[1,256]{1,0:T(1,128)S(1)}, f32[18,8]{1,0:T(8,128)S(1)}, bf16[128,256]{1,0:T...) custom-call(f32[3,256,128]{2,1,0:T(8,128)S(1)} %bitcast.11, ...), custom_call_target="tpu_custom_call" | custom-call | flops 6553600 | bytes 4000000 | tf_op jit(solution)/shard_map/pallas_call | solution.py:557
  14.7 12.3 %all-to-all-done = f32[32,1,4224]{2,1,0:T(1,128)S(1)} async-done(((f32[32,1,4224]{2,1,0:T(1,128)}), f32[32,1,4224]{2,1,0:T(1,128)S(1)}, u32[]{:S(2)}, u32[]{:S(2)}) %all-to-all-start) | async-done | bytes 540704 | tf_op jit(solution)/shard_map/all_to_all | solution.py:504
  27.0 1.6 %shard_map.115 = (f32[64,128]{1,0:T(8,128)S(1)}, f32[18,8]{1,0:T(8,128)S(1)}) custom-call(f32[1056,128]{1,0:T(8,128)S(1)} %bitcast.9, f32[1536,128]{1,0:T(8,128)S(1)} %get-tuple-element.14.staged, f32[16,256]{1,0:T(8,128)S(1)} %get-tuple-element.15.remote_b, s32[1,256]{1,0:T(1,128)S(1)} %get-tuple-element.16.remote_frag, ...), custom_call_target="tpu_custom_call" | custom-call | tf_op jit(solution)/shard_map/pallas_call | solution.py:590
  28.6 9.3 %all_to_all.10 = f32[32,1,256]{2,1,0:T(1,128)S(1)} all-to-all(f32[32,1,256]{2,1,0:T(1,128)S(1)} %bitcast.14), channel_id=1, replica_groups=mesh['tile'=8,'band'=4] {'band','tile'}, dimensions={0} | all-to-all | bytes 65536 | tf_op jit(solution)/shard_map/all_to_all | solution.py:504
  37.9 0.7 %shard_map.116 = (f32[6,8]{1,0:T(8,128)}, f32[6,2,8]{2,1,0:T(2,128)}) custom-call(f32[64,128]{1,0:T(8,128)S(1)} %bitcast.13, f32[18,8]{1,0:T(8,128)S(1)} %get-tuple-element.23.totals), custom_call_target="tpu_custom_call" | custom-call | tf_op jit(solution)/shard_map/pallas_call | solution.py:605
Async XLA Ops:
  2.9 7.4 %copy-start = (f32[256,3,128]{2,0,1:T(8,128)S(1)}, f32[256,3,128]{2,0,1:T(8,128)}, u32[]{:S(2)}) copy-start(f32[256,3,128]{2,0,1:T(8,128)} %param.10) | copy-start | bytes 1179652
  2.9 7.4 %copy-start.1 = (f32[256,3,128]{2,0,1:T(8,128)S(1)}, f32[256,3,128]{2,0,1:T(8,128)}, u32[]{:S(2)}) copy-start(f32[256,3,128]{2,0,1:T(8,128)} %param.11) | copy-start | bytes 1179652
  2.9 7.4 %copy-start.2 = (s32[256,128]{1,0:T(8,128)S(1)}, s32[256,128]{1,0:T(8,128)}, u32[]{:S(2)}) copy-start(s32[256,128]{1,0:T(8,128)} %maps.1) | copy-start | bytes 393220
  3.0 7.4 %copy-start.3 = (f32[2,6,8]{2,0,1:T(2,128)S(1)}, f32[2,6,8]{2,0,1:T(2,128)}, u32[]{:S(2)}) copy-start(f32[2,6,8]{2,0,1:T(2,128)} %param.13) | copy-start | bytes 1156
  3.0 7.4 %copy-start.4 = (f32[6,8]{1,0:T(8,128)S(1)}, f32[6,8]{1,0:T(8,128)}, u32[]{:S(2)}) copy-start(f32[6,8]{1,0:T(8,128)} %poses.1) | copy-start | bytes 580
  3.0 7.4 %copy-start.5 = (s32[2,256]{1,0:T(2,128)S(1)}, s32[2,256]{1,0:T(2,128)}, u32[]{:S(2)}) copy-start(s32[2,256]{1,0:T(2,128)} %pairs_v.1) | copy-start | bytes 6148
  3.0 24.0 %all-to-all-start = ((f32[32,1,4224]{2,1,0:T(1,128)}), f32[32,1,4224]{2,1,0:T(1,128)S(1)}, u32[]{:S(2)}, u32[]{:S(2)}) async-start(f32[32,1,4224]{2,1,0:T(1,128)} %bitcast.17), calls=%async_computation | async-start | bytes 1081344 | tf_op jit(solution)/shard_map/all_to_all | solution.py:504
  10.3 0.7 %copy-start.6 = (s32[1,256]{1,0:T(1,128)S(1)}, s32[1,256]{1,0:T(1,128)}, u32[]{:S(2)}) copy-start(s32[1,256]{1,0:T(1,128)} %dst_v.1) | copy-start | bytes 3076

commit v11 on v10

--- a/solution.py
+++ b/solution.py
@@ -93,6 +93,8 @@
 
 def peer_at(place, sizes):
     n_tile, n_band = sizes
+    if isinstance(place, int):
+        return place % n_tile * n_band + place // n_tile
     tile = lax.bitwise_and(place, n_tile - 1)
     return tile * n_band + lax.shift_right_logical(place, shift_of(n_tile))
 
@@ -151,20 +153,17 @@
         for s in range(SUB):
             block = src_s[0, p * SUB + s]
             out[pl.ds(q * MSG + s, 3, stride=SUB), :] = world[pl.ds(block, 3, stride=stride), :]
-        rows = maps[pl.ds(pl.multiple_of(p * SUB, SUB), SUB), :]
+        rows = maps[p * SUB : (p + 1) * SUB, :]
         out[pl.ds(q * MSG + 3 * SUB, SUB), :] = rows.astype(jnp.float32)
 
     def piece(i):
-        rows = pl.ds(pl.multiple_of(i * SUB * MSG, SUB), SUB * MSG)
+        rows = pl.ds(i * SUB * MSG, SUB * MSG)
         return pltpu.make_async_copy(out.at[rows], out_h.at[rows], out_sems.at[i])
 
-    def pack(i, carry):
+    for i in range(devices // SUB):
         for u in range(SUB):
             peer(i * SUB + u)
         piece(i).start()
-        return carry
-
-    lax.fori_loop(0, devices // SUB, pack, 0)
     for i in range(devices // SUB):
         piece(i).wait()
 
@@ -193,7 +192,7 @@
         )
 
     tiles = range(t // SUB, (t + LANE) // SUB, 2)
-    return [functools.partial(split, u) for u in tiles] + [multiply]
+    return [functools.partial(split, u) for u in tiles], multiply
 
 
 def field_steps(source, target, index, same, parts, turned, t):
@@ -204,14 +203,17 @@
         tiles = [source(u, k) for u in range(t // SUB, (t + LANE) // SUB)]
         put(6 + k, jnp.concatenate(tiles, axis=0).T)
 
-    steps = []
+    splits, products = [], []
     for k in range(6):
 
         def at(u, k=k):
             return pick(target(u, k), index(u))
 
-        steps += turn_steps(at, same, parts, k, t, functools.partial(put, k))
-    return steps + [functools.partial(turn_source, k) for k in range(3)]
+        split, product = turn_steps(at, same, parts, k, t, functools.partial(put, k))
+        splits.append(split)
+        products.append(product)
+    steps = [split[u] for u in range(len(splits[0])) for split in splits]
+    return steps + products + [functools.partial(turn_source, k) for k in range(3)]
 
 
 def run(steps):
@@ -401,9 +403,11 @@
                 side_a[:, lanes] = value
                 join_directions(side_a, remote_b, joined, lanes, pl.ds(start + t, LANE))
 
+            split, product = turn_steps(extras, gather[...], parts, 6, t, put)
             return (
                 [indices]
-                + turn_steps(extras, gather[...], parts, 6, t, put)
+                + split
+                + [product]
                 + field_steps(
                     lambda u, k: arrived[pl.ds(row_at(u, MSG, SUB * k), SUB), :],
                     lambda u, k: staged[pl.ds(row_at(u, TARGET, SUB * k), SUB), :],

time: 38.9 us -> 38.8 us (level)
  no operation moved by 1% of the time
where the time goes in v11:
time: 38.8 us; the launch traced here: 38.5 us
  waiting for transfers between devices  12.3 us (32%)
  blocking collectives  9.28 us (24%)
  Pallas kernels  8.22 us (21%)
  starting transfers between devices  7.3 us (19%)
  between operations  0.76 us (2%)
  local copies, waits for them, and re-layouts  0.65 us (2%)
    all_to_all x1, waiting for transfers between devices, exchange(): sent = lax.all_to_all(sent, ORDER, split_axis=0, concat_axis=0, tiled=True)  12.3 us
    all_to_all x1, blocking collectives, exchange(): sent = lax.all_to_all(sent, ORDER, split_axis=0, concat_axis=0, tiled=True)  9.28 us
    all_to_all x1, starting transfers between devices, exchange(): sent = lax.all_to_all(sent, ORDER, split_axis=0, concat_axis=0, tiled=True)  7.3 us
    pallas_call x1, Pallas kernels, local(): call(functools.partial(local_kernel, sizes=sizes), [array(devices * TARGE...  3.7 us
    pallas_call x1, Pallas kernels, local(): call(functools.partial(pack_kernel, sizes=sizes), [array(devices * MSG, L...  2.18 us
    pallas_call x1, Pallas kernels, local(): call(remote_kernel, [array(devices * 2, LANE), array(18, frags)], [vmem(2...  1.59 us
  transfers between devices with their start and end apart: 1, of which 1 were waited for; matrix products, arithmetic and copies ran while one was open for 0% of the time, Pallas kernels for 10%

profile of v11, /device:TPU:0, one launch (start us, length us, event | category | flops | bytes accessed | tf_op | source)
XLA Modules:
  0.0 38.5 jit_solution(5609893298331357159)
XLA Ops:
  0.6 2.2 %shard_map.113 = f32[1056,128]{1,0:T(8,128)} custom-call(f32[3,256,128]{2,1,0:T(8,128)} %bitcast.10, f32[6,8]{1,0:T(8,128)} %poses.1, f32[6,2,8]{2,1,0:T(2,128)} %bitcast.15, s32[1,256]{1,0:T(1,128)} %src_h.1, s32[256,128]{1,0:T(8,128)} %bitcast.18, s32[1,32]{1,0:T(1,128)} %counts_h.1), custom_call_target="tpu_custom_call" | custom-call | tf_op jit(solution)/shard_map/pallas_call | solution.py:538
  2.8 0.0 copy-start
  2.8 0.0 copy-start.1
  2.8 0.0 copy-start.2
  2.9 0.0 copy-start.3
  2.9 0.0 copy-start.4
  2.9 0.0 copy-start.5
  2.9 7.3 %all-to-all-start = ((f32[32,1,4224]{2,1,0:T(1,128)}), f32[32,1,4224]{2,1,0:T(1,128)S(1)}, u32[]{:S(2)}, u32[]{:S(2)}) async-start(f32[32,1,4224]{2,1,0:T(1,128)} %bitcast.17), calls=%async_computation | async-start | bytes 1081344 | tf_op jit(solution)/shard_map/all_to_all | solution.py:508
  10.2 0.0 copy-start.6
  10.2 0.0 copy-done
  10.2 0.0 copy-done.1
  10.2 0.0 copy-done.2
  10.2 0.0 copy-done.3
  10.3 0.0 copy-done.4
  10.3 0.0 copy-done.5
  10.3 0.6 %copy-done.6 = s32[1,256]{1,0:T(1,128)S(1)} copy-done((s32[1,256]{1,0:T(1,128)S(1)}, s32[1,256]{1,0:T(1,128)}, u32[]{:S(2)}) %copy-start.6) | copy-done | bytes 1048
  10.9 3.7 %shard_map.114 = (f32[1536,128]{1,0:T(8,128)S(1)}, f32[16,256]{1,0:T(8,128)S(1)}, s32[1,256]{1,0:T(1,128)S(1)}, f32[18,8]{1,0:T(8,128)S(1)}, bf16[128,256]{1,0:T...) custom-call(f32[3,256,128]{2,1,0:T(8,128)S(1)} %bitcast.11, ...), custom_call_target="tpu_custom_call" | custom-call | flops 6553600 | bytes 4000000 | tf_op jit(solution)/shard_map/pallas_call | solution.py:561
  14.6 12.3 %all-to-all-done = f32[32,1,4224]{2,1,0:T(1,128)S(1)} async-done(((f32[32,1,4224]{2,1,0:T(1,128)}), f32[32,1,4224]{2,1,0:T(1,128)S(1)}, u32[]{:S(2)}, u32[]{:S(2)}) %all-to-all-start) | async-done | bytes 540704 | tf_op jit(solution)/shard_map/all_to_all | solution.py:508
  26.9 1.6 %shard_map.115 = (f32[64,128]{1,0:T(8,128)S(1)}, f32[18,8]{1,0:T(8,128)S(1)}) custom-call(f32[1056,128]{1,0:T(8,128)S(1)} %bitcast.9, f32[1536,128]{1,0:T(8,128)S(1)} %get-tuple-element.14.staged, f32[16,256]{1,0:T(8,128)S(1)} %get-tuple-element.15.remote_b, s32[1,256]{1,0:T(1,128)S(1)} %get-tuple-element.16.remote_frag, ...), custom_call_target="tpu_custom_call" | custom-call | tf_op jit(solution)/shard_map/pallas_call | solution.py:594
  28.5 9.3 %all_to_all.10 = f32[32,1,256]{2,1,0:T(1,128)S(1)} all-to-all(f32[32,1,256]{2,1,0:T(1,128)S(1)} %bitcast.14), channel_id=1, replica_groups=mesh['tile'=8,'band'=4] {'band','tile'}, dimensions={0} | all-to-all | bytes 65536 | tf_op jit(solution)/shard_map/all_to_all | solution.py:508
  37.8 0.7 %shard_map.116 = (f32[6,8]{1,0:T(8,128)}, f32[6,2,8]{2,1,0:T(2,128)}) custom-call(f32[64,128]{1,0:T(8,128)S(1)} %bitcast.13, f32[18,8]{1,0:T(8,128)S(1)} %get-tuple-element.23.totals), custom_call_target="tpu_custom_call" | custom-call | tf_op jit(solution)/shard_map/pallas_call | solution.py:609
Async XLA Ops:
  2.8 7.4 %copy-start = (f32[256,3,128]{2,0,1:T(8,128)S(1)}, f32[256,3,128]{2,0,1:T(8,128)}, u32[]{:S(2)}) copy-start(f32[256,3,128]{2,0,1:T(8,128)} %param.10) | copy-start | bytes 1179652
  2.8 7.4 %copy-start.1 = (f32[256,3,128]{2,0,1:T(8,128)S(1)}, f32[256,3,128]{2,0,1:T(8,128)}, u32[]{:S(2)}) copy-start(f32[256,3,128]{2,0,1:T(8,128)} %param.11) | copy-start | bytes 1179652
  2.8 7.4 %copy-start.2 = (s32[256,128]{1,0:T(8,128)S(1)}, s32[256,128]{1,0:T(8,128)}, u32[]{:S(2)}) copy-start(s32[256,128]{1,0:T(8,128)} %maps.1) | copy-start | bytes 393220
  2.9 7.4 %copy-start.3 = (f32[2,6,8]{2,0,1:T(2,128)S(1)}, f32[2,6,8]{2,0,1:T(2,128)}, u32[]{:S(2)}) copy-start(f32[2,6,8]{2,0,1:T(2,128)} %param.13) | copy-start | bytes 1156
  2.9 7.4 %copy-start.4 = (f32[6,8]{1,0:T(8,128)S(1)}, f32[6,8]{1,0:T(8,128)}, u32[]{:S(2)}) copy-start(f32[6,8]{1,0:T(8,128)} %poses.1) | copy-start | bytes 580
  2.9 7.4 %copy-start.5 = (s32[2,256]{1,0:T(2,128)S(1)}, s32[2,256]{1,0:T(2,128)}, u32[]{:S(2)}) copy-start(s32[2,256]{1,0:T(2,128)} %pairs_v.1) | copy-start | bytes 6148
  2.9 24.0 %all-to-all-start = ((f32[32,1,4224]{2,1,0:T(1,128)}), f32[32,1,4224]{2,1,0:T(1,128)S(1)}, u32[]{:S(2)}, u32[]{:S(2)}) async-start(f32[32,1,4224]{2,1,0:T(1,128)} %bitcast.17), calls=%async_computation | async-start | bytes 1081344 | tf_op jit(solution)/shard_map/all_to_all | solution.py:508
  10.2 0.7 %copy-start.6 = (s32[1,256]{1,0:T(1,128)S(1)}, s32[1,256]{1,0:T(1,128)}, u32[]{:S(2)}) copy-start(s32[1,256]{1,0:T(1,128)} %dst_v.1) | copy-start | bytes 3076

commit v12 on v11

--- a/solution.py
+++ b/solution.py
@@ -117,8 +117,8 @@
     stride = points.shape[1] + SUB
     frags = poses.shape[1]
     pairs = [(directions_h, directions), (src_h, src_v), (counts_h, used), (poses_h, poses)]
+    pairs += [(src_h, src_s), (maps_h, maps)]
     pairs += [(points_h.at[j], points.at[j]) for j in range(3)]
-    pairs += [(src_h, src_s), (maps_h, maps)]
     copies = [pltpu.make_async_copy(a, b, sems.at[i]) for i, (a, b) in enumerate(pairs)]
     for copy in copies:
         copy.start()
@@ -142,19 +142,21 @@
         out[pl.ds(q * MSG + MSG - 1, SUB, stride=MSG), :] = extras
     copies[3].wait()
     write_rotations(poses, turns)
-    for copy in copies[4:7]:
+    copies[5].wait()
+    for q in range(devices):
+        p = peer_at(q, sizes)
+        rows = maps[p * SUB : (p + 1) * SUB, :]
+        out[pl.ds(q * MSG + 3 * SUB, SUB), :] = rows.astype(jnp.float32)
+    for copy in copies[6:]:
         copy.wait()
     write_world([points], turns, world, range(frags))
-    for copy in copies[7:]:
-        copy.wait()
+    copies[4].wait()
 
     def peer(q):
         p = peer_at(q, sizes)
         for s in range(SUB):
             block = src_s[0, p * SUB + s]
             out[pl.ds(q * MSG + s, 3, stride=SUB), :] = world[pl.ds(block, 3, stride=stride), :]
-        rows = maps[p * SUB : (p + 1) * SUB, :]
-        out[pl.ds(q * MSG + 3 * SUB, SUB), :] = rows.astype(jnp.float32)
 
     def piece(i):
         rows = pl.ds(i * SUB * MSG, SUB * MSG)
@@ -471,14 +473,16 @@
 
 def final_kernel(back, totals, gradient, hess, *, per_frag):
     devices = back.shape[0] // 2
-    index = iota(0) * GROUP + lax.bitwise_and(iota(1), GROUP - 1)
+    frags = gradient.shape[1]
+    index = lax.bitwise_and(iota(1), frags - 1) * GROUP + iota(0)
     halves = []
     for half in range(2):
         tile = back[pl.ds(half, SUB, stride=2), :]
         for q in range(SUB, devices, SUB):
             tile = tile + back[pl.ds(2 * q + half, SUB, stride=2), :]
-        halves.append(pick(jnp.sum(tile, axis=0, keepdims=True), index))
-    total = jnp.where(iota(1) < GROUP, halves[0], halves[1]).T[0:18, :] + totals[...]
+        halves.append(jnp.sum(tile, axis=0, keepdims=True))
+    parts = [pick(halves[0], index), pick(halves[0], index + SUB), pick(halves[1], index)]
+    total = jnp.concatenate(parts, axis=0)[0:18, 0:frags] + totals[...]
     gradient[...] = total[0:6, :] * (1.0 / LANE)
     for v in range(2):
         part = total[6 + 6 * v : 12 + 6 * v, :] * (1.0 / (LANE * per_frag))

time: 38.8 us -> 38.8 us (level)
  no operation moved by 1% of the time
where the time goes in v12:
time: 38.8 us; the launch traced here: 38.5 us
  waiting for transfers between devices  12.3 us (32%)
  blocking collectives  9.28 us (24%)
  Pallas kernels  8.22 us (21%)
  starting transfers between devices  7.3 us (19%)
  between operations  0.76 us (2%)
  local copies, waits for them, and re-layouts  0.65 us (2%)
    all_to_all x1, waiting for transfers between devices, exchange(): sent = lax.all_to_all(sent, ORDER, split_axis=0, concat_axis=0, tiled=True)  12.3 us
    all_to_all x1, blocking collectives, exchange(): sent = lax.all_to_all(sent, ORDER, split_axis=0, concat_axis=0, tiled=True)  9.28 us
    all_to_all x1, starting transfers between devices, exchange(): sent = lax.all_to_all(sent, ORDER, split_axis=0, concat_axis=0, tiled=True)  7.3 us
    pallas_call x1, Pallas kernels, local(): call(functools.partial(local_kernel, sizes=sizes), [array(devices * TARGE...  3.7 us
    pallas_call x1, Pallas kernels, local(): call(functools.partial(pack_kernel, sizes=sizes), [array(devices * MSG, L...  2.24 us
    pallas_call x1, Pallas kernels, local(): call(remote_kernel, [array(devices * 2, LANE), array(18, frags)], [vmem(2...  1.59 us
  transfers between devices with their start and end apart: 1, of which 1 were waited for; matrix products, arithmetic and copies ran while one was open for 0% of the time, Pallas kernels for 10%

profile of v12, /device:TPU:0, one launch (start us, length us, event | category | flops | bytes accessed | tf_op | source)
XLA Modules:
  0.0 38.5 jit_solution(16341509691406146081)
XLA Ops:
  0.6 2.2 %shard_map.113 = f32[1056,128]{1,0:T(8,128)} custom-call(f32[3,256,128]{2,1,0:T(8,128)} %bitcast.10, f32[6,8]{1,0:T(8,128)} %poses.1, f32[6,2,8]{2,1,0:T(2,128)} %bitcast.15, s32[1,256]{1,0:T(1,128)} %src_h.1, s32[256,128]{1,0:T(8,128)} %bitcast.18, s32[1,32]{1,0:T(1,128)} %counts_h.1), custom_call_target="tpu_custom_call" | custom-call | tf_op jit(solution)/shard_map/pallas_call | solution.py:542
  2.9 0.0 copy-start
  2.9 0.0 copy-start.1
  2.9 0.0 copy-start.2
  2.9 0.0 copy-start.3
  2.9 0.0 copy-start.4
  2.9 0.0 copy-start.5
  3.0 7.3 %all-to-all-start = ((f32[32,1,4224]{2,1,0:T(1,128)}), f32[32,1,4224]{2,1,0:T(1,128)S(1)}, u32[]{:S(2)}, u32[]{:S(2)}) async-start(f32[32,1,4224]{2,1,0:T(1,128)} %bitcast.17), calls=%async_computation | async-start | bytes 1081344 | tf_op jit(solution)/shard_map/all_to_all | solution.py:512
  10.3 0.0 copy-start.6
  10.3 0.0 copy-done
  10.3 0.0 copy-done.1
  10.3 0.0 copy-done.2
  10.3 0.0 copy-done.3
  10.3 0.0 copy-done.4
  10.3 0.0 copy-done.5
  10.3 0.6 %copy-done.6 = s32[1,256]{1,0:T(1,128)S(1)} copy-done((s32[1,256]{1,0:T(1,128)S(1)}, s32[1,256]{1,0:T(1,128)}, u32[]{:S(2)}) %copy-start.6) | copy-done | bytes 1048
  10.9 3.7 %shard_map.114 = (f32[1536,128]{1,0:T(8,128)S(1)}, f32[16,256]{1,0:T(8,128)S(1)}, s32[1,256]{1,0:T(1,128)S(1)}, f32[18,8]{1,0:T(8,128)S(1)}, bf16[128,256]{1,0:T...) custom-call(f32[3,256,128]{2,1,0:T(8,128)S(1)} %bitcast.11, ...), custom_call_target="tpu_custom_call" | custom-call | flops 6553600 | bytes 4000000 | tf_op jit(solution)/shard_map/pallas_call | solution.py:565
  14.7 12.3 %all-to-all-done = f32[32,1,4224]{2,1,0:T(1,128)S(1)} async-done(((f32[32,1,4224]{2,1,0:T(1,128)}), f32[32,1,4224]{2,1,0:T(1,128)S(1)}, u32[]{:S(2)}, u32[]{:S(2)}) %all-to-all-start) | async-done | bytes 540704 | tf_op jit(solution)/shard_map/all_to_all | solution.py:512
  27.0 1.6 %shard_map.115 = (f32[64,128]{1,0:T(8,128)S(1)}, f32[18,8]{1,0:T(8,128)S(1)}) custom-call(f32[1056,128]{1,0:T(8,128)S(1)} %bitcast.9, f32[1536,128]{1,0:T(8,128)S(1)} %get-tuple-element.14.staged, f32[16,256]{1,0:T(8,128)S(1)} %get-tuple-element.15.remote_b, s32[1,256]{1,0:T(1,128)S(1)} %get-tuple-element.16.remote_frag, ...), custom_call_target="tpu_custom_call" | custom-call | tf_op jit(solution)/shard_map/pallas_call | solution.py:598
  28.6 9.3 %all_to_all.10 = f32[32,1,256]{2,1,0:T(1,128)S(1)} all-to-all(f32[32,1,256]{2,1,0:T(1,128)S(1)} %bitcast.14), channel_id=1, replica_groups=mesh['tile'=8,'band'=4] {'band','tile'}, dimensions={0} | all-to-all | bytes 65536 | tf_op jit(solution)/shard_map/all_to_all | solution.py:512
  37.8 0.7 %shard_map.116 = (f32[6,8]{1,0:T(8,128)}, f32[6,2,8]{2,1,0:T(2,128)}) custom-call(f32[64,128]{1,0:T(8,128)S(1)} %bitcast.13, f32[18,8]{1,0:T(8,128)S(1)} %get-tuple-element.23.totals), custom_call_target="tpu_custom_call" | custom-call | tf_op jit(solution)/shard_map/pallas_call | solution.py:613
Async XLA Ops:
  2.9 7.4 %copy-start = (f32[256,3,128]{2,0,1:T(8,128)S(1)}, f32[256,3,128]{2,0,1:T(8,128)}, u32[]{:S(2)}) copy-start(f32[256,3,128]{2,0,1:T(8,128)} %param.10) | copy-start | bytes 1179652
  2.9 7.4 %copy-start.1 = (f32[256,3,128]{2,0,1:T(8,128)S(1)}, f32[256,3,128]{2,0,1:T(8,128)}, u32[]{:S(2)}) copy-start(f32[256,3,128]{2,0,1:T(8,128)} %param.11) | copy-start | bytes 1179652
  2.9 7.4 %copy-start.2 = (s32[256,128]{1,0:T(8,128)S(1)}, s32[256,128]{1,0:T(8,128)}, u32[]{:S(2)}) copy-start(s32[256,128]{1,0:T(8,128)} %maps.1) | copy-start | bytes 393220
  2.9 7.4 %copy-start.3 = (f32[2,6,8]{2,0,1:T(2,128)S(1)}, f32[2,6,8]{2,0,1:T(2,128)}, u32[]{:S(2)}) copy-start(f32[2,6,8]{2,0,1:T(2,128)} %param.13) | copy-start | bytes 1156
  2.9 7.4 %copy-start.4 = (f32[6,8]{1,0:T(8,128)S(1)}, f32[6,8]{1,0:T(8,128)}, u32[]{:S(2)}) copy-start(f32[6,8]{1,0:T(8,128)} %poses.1) | copy-start | bytes 580
  2.9 7.4 %copy-start.5 = (s32[2,256]{1,0:T(2,128)S(1)}, s32[2,256]{1,0:T(2,128)}, u32[]{:S(2)}) copy-start(s32[2,256]{1,0:T(2,128)} %pairs_v.1) | copy-start | bytes 6148
  3.0 24.0 %all-to-all-start = ((f32[32,1,4224]{2,1,0:T(1,128)}), f32[32,1,4224]{2,1,0:T(1,128)S(1)}, u32[]{:S(2)}, u32[]{:S(2)}) async-start(f32[32,1,4224]{2,1,0:T(1,128)} %bitcast.17), calls=%async_computation | async-start | bytes 1081344 | tf_op jit(solution)/shard_map/all_to_all | solution.py:512
  10.3 0.7 %copy-start.6 = (s32[1,256]{1,0:T(1,128)S(1)}, s32[1,256]{1,0:T(1,128)}, u32[]{:S(2)}) copy-start(s32[1,256]{1,0:T(1,128)} %dst_v.1) | copy-start | bytes 3076

commit v13 on v11

--- a/solution.py
+++ b/solution.py
@@ -424,10 +424,11 @@
         def back_steps(sums, t):
             lanes = slice(t, t + LANE)
             held = {}
+            both = jnp.concatenate(halves_of(sums), axis=0)
 
             def scatter():
                 held["placed"] = lax.dot_general(
-                    jnp.concatenate(halves_of(sums), axis=0),
+                    both,
                     place[...],
                     (((0,), (0,)), ((), ())),
                     preferred_element_type=f32,
@@ -443,7 +444,14 @@
 
             def own_side():
                 frag = remote_frag[0:1, pl.ds(start + t, LANE)]
-                held["total"] = target_side(by_frag(sums, frag))
+                hot = jnp.broadcast_to(frag, (SUB, LANE)) == iota(0)
+                added = lax.dot_general(
+                    both,
+                    hot.astype(f32).astype(jnp.bfloat16),
+                    (((1,), (1,)), ((), ())),
+                    preferred_element_type=f32,
+                )
+                held["total"] = target_side(added[0:ROWS, :] + added[ROWS:, :])
 
             return [scatter, functools.partial(add, 0), functools.partial(add, 1), own_side], held
 
@@ -471,14 +479,16 @@
 
 def final_kernel(back, totals, gradient, hess, *, per_frag):
     devices = back.shape[0] // 2
-    index = iota(0) * GROUP + lax.bitwise_and(iota(1), GROUP - 1)
+    frags = gradient.shape[1]
+    index = lax.bitwise_and(iota(1), frags - 1) * GROUP + iota(0)
     halves = []
     for half in range(2):
         tile = back[pl.ds(half, SUB, stride=2), :]
         for q in range(SUB, devices, SUB):
             tile = tile + back[pl.ds(2 * q + half, SUB, stride=2), :]
-        halves.append(pick(jnp.sum(tile, axis=0, keepdims=True), index))
-    total = jnp.where(iota(1) < GROUP, halves[0], halves[1]).T[0:18, :] + totals[...]
+        halves.append(jnp.sum(tile, axis=0, keepdims=True))
+    parts = [pick(halves[0], index), pick(halves[0], index + SUB), pick(halves[1], index)]
+    total = jnp.concatenate(parts, axis=0)[0:18, 0:frags] + totals[...]
     gradient[...] = total[0:6, :] * (1.0 / LANE)
     for v in range(2):
         part = total[6 + 6 * v : 12 + 6 * v, :] * (1.0 / (LANE * per_frag))

time: 38.8 us -> 38.7 us (level)
  no operation moved by 1% of the time
where the time goes in v13:
time: 38.7 us; the launch traced here: 38.4 us
  waiting for transfers between devices  12.3 us (32%)
  blocking collectives  9.27 us (24%)
  Pallas kernels  8.12 us (21%)
  starting transfers between devices  7.3 us (19%)
  between operations  0.76 us (2%)
  local copies, waits for them, and re-layouts  0.65 us (2%)
    all_to_all x1, waiting for transfers between devices, exchange(): sent = lax.all_to_all(sent, ORDER, split_axis=0, concat_axis=0, tiled=True)  12.3 us
    all_to_all x1, blocking collectives, exchange(): sent = lax.all_to_all(sent, ORDER, split_axis=0, concat_axis=0, tiled=True)  9.27 us
    all_to_all x1, starting transfers between devices, exchange(): sent = lax.all_to_all(sent, ORDER, split_axis=0, concat_axis=0, tiled=True)  7.3 us
    pallas_call x1, Pallas kernels, local(): call(functools.partial(local_kernel, sizes=sizes), [array(devices * TARGE...  3.7 us
    pallas_call x1, Pallas kernels, local(): call(functools.partial(pack_kernel, sizes=sizes), [array(devices * MSG, L...  2.18 us
    pallas_call x1, Pallas kernels, local(): call(remote_kernel, [array(devices * 2, LANE), array(18, frags)], [vmem(2...  1.56 us
  transfers between devices with their start and end apart: 1, of which 1 were waited for; matrix products, arithmetic and copies ran while one was open for 0% of the time, Pallas kernels for 10%

profile of v13, /device:TPU:0, one launch (start us, length us, event | category | flops | bytes accessed | tf_op | source)
XLA Modules:
  0.0 38.4 jit_solution(10782498745159947160)
XLA Ops:
  0.6 2.2 %shard_map.113 = f32[1056,128]{1,0:T(8,128)} custom-call(f32[3,256,128]{2,1,0:T(8,128)} %bitcast.10, f32[6,8]{1,0:T(8,128)} %poses.1, f32[6,2,8]{2,1,0:T(2,128)} %bitcast.15, s32[1,256]{1,0:T(1,128)} %src_h.1, s32[256,128]{1,0:T(8,128)} %bitcast.18, s32[1,32]{1,0:T(1,128)} %counts_h.1), custom_call_target="tpu_custom_call" | custom-call | tf_op jit(solution)/shard_map/pallas_call | solution.py:548
  2.8 0.0 copy-start
  2.8 0.0 copy-start.1
  2.8 0.0 copy-start.2
  2.9 0.0 copy-start.3
  2.9 0.0 copy-start.4
  2.9 0.0 copy-start.5
  2.9 7.3 %all-to-all-start = ((f32[32,1,4224]{2,1,0:T(1,128)}), f32[32,1,4224]{2,1,0:T(1,128)S(1)}, u32[]{:S(2)}, u32[]{:S(2)}) async-start(f32[32,1,4224]{2,1,0:T(1,128)} %bitcast.17), calls=%async_computation | async-start | bytes 1081344 | tf_op jit(solution)/shard_map/all_to_all | solution.py:518
  10.2 0.0 copy-start.6
  10.2 0.0 copy-done
  10.2 0.0 copy-done.1
  10.2 0.0 copy-done.2
  10.2 0.0 copy-done.3
  10.3 0.0 copy-done.4
  10.3 0.0 copy-done.5
  10.3 0.6 %copy-done.6 = s32[1,256]{1,0:T(1,128)S(1)} copy-done((s32[1,256]{1,0:T(1,128)S(1)}, s32[1,256]{1,0:T(1,128)}, u32[]{:S(2)}) %copy-start.6) | copy-done | bytes 1048
  10.9 3.7 %shard_map.114 = (f32[1536,128]{1,0:T(8,128)S(1)}, f32[16,256]{1,0:T(8,128)S(1)}, s32[1,256]{1,0:T(1,128)S(1)}, f32[18,8]{1,0:T(8,128)S(1)}, bf16[128,256]{1,0:T...) custom-call(f32[3,256,128]{2,1,0:T(8,128)S(1)} %bitcast.11, ...), custom_call_target="tpu_custom_call" | custom-call | flops 6553600 | bytes 4000000 | tf_op jit(solution)/shard_map/pallas_call | solution.py:571
  14.6 12.3 %all-to-all-done = f32[32,1,4224]{2,1,0:T(1,128)S(1)} async-done(((f32[32,1,4224]{2,1,0:T(1,128)}), f32[32,1,4224]{2,1,0:T(1,128)S(1)}, u32[]{:S(2)}, u32[]{:S(2)}) %all-to-all-start) | async-done | bytes 540704 | tf_op jit(solution)/shard_map/all_to_all | solution.py:518
  26.9 1.6 %shard_map.115 = (f32[64,128]{1,0:T(8,128)S(1)}, f32[18,8]{1,0:T(8,128)S(1)}) custom-call(f32[1056,128]{1,0:T(8,128)S(1)} %bitcast.9, f32[1536,128]{1,0:T(8,128)S(1)} %get-tuple-element.14.staged, f32[16,256]{1,0:T(8,128)S(1)} %get-tuple-element.15.remote_b, s32[1,256]{1,0:T(1,128)S(1)} %get-tuple-element.16.remote_frag, ...), custom_call_target="tpu_custom_call" | custom-call | tf_op jit(solution)/shard_map/pallas_call | solution.py:604
  28.5 9.3 %all_to_all.10 = f32[32,1,256]{2,1,0:T(1,128)S(1)} all-to-all(f32[32,1,256]{2,1,0:T(1,128)S(1)} %bitcast.14), channel_id=1, replica_groups=mesh['tile'=8,'band'=4] {'band','tile'}, dimensions={0} | all-to-all | bytes 65536 | tf_op jit(solution)/shard_map/all_to_all | solution.py:518
  37.7 0.7 %shard_map.116 = (f32[6,8]{1,0:T(8,128)}, f32[6,2,8]{2,1,0:T(2,128)}) custom-call(f32[64,128]{1,0:T(8,128)S(1)} %bitcast.13, f32[18,8]{1,0:T(8,128)S(1)} %get-tuple-element.23.totals), custom_call_target="tpu_custom_call" | custom-call | tf_op jit(solution)/shard_map/pallas_call | solution.py:619
Async XLA Ops:
  2.8 7.4 %copy-start = (f32[256,3,128]{2,0,1:T(8,128)S(1)}, f32[256,3,128]{2,0,1:T(8,128)}, u32[]{:S(2)}) copy-start(f32[256,3,128]{2,0,1:T(8,128)} %param.10) | copy-start | bytes 1179652
  2.8 7.4 %copy-start.1 = (f32[256,3,128]{2,0,1:T(8,128)S(1)}, f32[256,3,128]{2,0,1:T(8,128)}, u32[]{:S(2)}) copy-start(f32[256,3,128]{2,0,1:T(8,128)} %param.11) | copy-start | bytes 1179652
  2.8 7.4 %copy-start.2 = (s32[256,128]{1,0:T(8,128)S(1)}, s32[256,128]{1,0:T(8,128)}, u32[]{:S(2)}) copy-start(s32[256,128]{1,0:T(8,128)} %maps.1) | copy-start | bytes 393220
  2.9 7.4 %copy-start.3 = (f32[2,6,8]{2,0,1:T(2,128)S(1)}, f32[2,6,8]{2,0,1:T(2,128)}, u32[]{:S(2)}) copy-start(f32[2,6,8]{2,0,1:T(2,128)} %param.13) | copy-start | bytes 1156
  2.9 7.4 %copy-start.4 = (f32[6,8]{1,0:T(8,128)S(1)}, f32[6,8]{1,0:T(8,128)}, u32[]{:S(2)}) copy-start(f32[6,8]{1,0:T(8,128)} %poses.1) | copy-start | bytes 580
  2.9 7.4 %copy-start.5 = (s32[2,256]{1,0:T(2,128)S(1)}, s32[2,256]{1,0:T(2,128)}, u32[]{:S(2)}) copy-start(s32[2,256]{1,0:T(2,128)} %pairs_v.1) | copy-start | bytes 6148
  2.9 24.0 %all-to-all-start = ((f32[32,1,4224]{2,1,0:T(1,128)}), f32[32,1,4224]{2,1,0:T(1,128)S(1)}, u32[]{:S(2)}, u32[]{:S(2)}) async-start(f32[32,1,4224]{2,1,0:T(1,128)} %bitcast.17), calls=%async_computation | async-start | bytes 1081344 | tf_op jit(solution)/shard_map/all_to_all | solution.py:518
  10.2 0.7 %copy-start.6 = (s32[1,256]{1,0:T(1,128)S(1)}, s32[1,256]{1,0:T(1,128)}, u32[]{:S(2)}) copy-start(s32[1,256]{1,0:T(1,128)} %dst_v.1) | copy-start | bytes 3076

commit v14 on v13

--- a/solution.py
+++ b/solution.py
@@ -368,6 +368,17 @@
     totals[...] = total
 
 
+def fetch_local(*refs, inputs, outputs, sizes):
+    far, outs, rest = refs[:inputs], refs[inputs : inputs + outputs], refs[inputs + outputs :]
+    near, scratch, sems = rest[:inputs], rest[inputs:-1], rest[-1]
+    copies = [pltpu.make_async_copy(a, b, sems.at[i]) for i, (a, b) in enumerate(zip(far, near))]
+    for copy in copies:
+        copy.start()
+    for copy in copies:
+        copy.wait()
+    local_kernel(*near, *outs, *scratch, sizes=sizes)
+
+
 def remote_kernel(
     arrived, staged, remote_b, remote_frag, local_totals, same, gather, place, mine,
     back, totals, side_a, joined, frags, index, parts, turned, partial,
@@ -569,7 +580,7 @@
     )(*[in_hbm(x) for x in (points, poses, directions, remote_src, remote_maps[0], counts)])
     arrived = exchange(message, devices)
     staged, remote_b, remote_frag, totals, same, gather, place, mine = call(
-        functools.partial(local_kernel, sizes=sizes),
+        functools.partial(fetch_local, inputs=9, outputs=8, sizes=sizes),
         [
             array(devices * TARGET, LANE),
             array(2 * SUB, slots),
@@ -581,6 +592,15 @@
             array(PEERS, part, dtype=bf16),
         ],
         [
+            vmem(3, blocks, LANE),
+            vmem(3, blocks, LANE),
+            pltpu.SMEM((6, frags), f32),
+            vmem(6, 2, frags),
+            pltpu.SMEM((2, pairs), i32),
+            vmem(2, pairs, dtype=i32),
+            vmem(pairs, LANE, dtype=i32),
+            pltpu.SMEM((1, slots), i32),
+            vmem(1, slots, dtype=i32),
             vmem(6 * stride, LANE),
             vmem(12 * frags * SUB, LANE),
             vmem(2 * SUB, LANE),
@@ -592,14 +612,20 @@
             vmem(pairs, 6 * 2 * LANE, dtype=bf16),
             vmem(9 * LANE, pairs),
             vmem(pairs // LANE * ROWS * SUB, LANE),
+            pltpu.SemaphoreType.DMA((9,)),
         ],
-        "vvsvsvvsv",
+        "hhhhhhhhh",
         cost_estimate=pl.CostEstimate(
             flops=200 * pairs * LANE, bytes_accessed=4_000_000, transcendentals=0
         ),
     )(
-        points, normals, poses, directions, local_pairs, local_pairs, local_maps,
-        remote_dst, remote_dst,
+        *[
+            in_hbm(x)
+            for x in (
+                points, normals, poses, directions, local_pairs, local_pairs, local_maps,
+                remote_dst, remote_dst,
+            )
+        ]
     )
     back, totals = call(
         remote_kernel,

time: 38.7 us -> 38.6 us (level)
  Pallas kernels: 8.12 us -> 8.86 us
  local copies, waits for them, and re-layouts: 0.65 us -> 0 us
    pallas_call x1, Pallas kernels: 3.7 us -> 4.43 us  [local(): call(functools.partial(fetch_local, inputs=9, outputs=8, sizes=sizes), [a...]
    unnamed x14 -> x0, local copies, waits for them, and re-layouts: 0.65 us -> none
  transfers between devices with their start and end apart: 1 -> 1, of which waited for: 1 -> 1; matrix products, arithmetic and copies ran while one was open for 0% -> 0% of each run, Pallas kernels for 10% -> 12%
where the time goes in v14:
time: 38.6 us; the launch traced here: 38.3 us
  waiting for transfers between devices  12.3 us (32%)
  blocking collectives  9.27 us (24%)
  Pallas kernels  8.86 us (23%)
  starting transfers between devices  7.3 us (19%)
  between operations  0.66 us (2%)
    all_to_all x1, waiting for transfers between devices, exchange(): sent = lax.all_to_all(sent, ORDER, split_axis=0, concat_axis=0, tiled=True)  12.3 us
    all_to_all x1, blocking collectives, exchange(): sent = lax.all_to_all(sent, ORDER, split_axis=0, concat_axis=0, tiled=True)  9.27 us
    all_to_all x1, starting transfers between devices, exchange(): sent = lax.all_to_all(sent, ORDER, split_axis=0, concat_axis=0, tiled=True)  7.3 us
    pallas_call x1, Pallas kernels, local(): call(functools.partial(fetch_local, inputs=9, outputs=8, sizes=sizes), [a...  4.43 us
    pallas_call x1, Pallas kernels, local(): call(functools.partial(pack_kernel, sizes=sizes), [array(devices * MSG, L...  2.19 us
    pallas_call x1, Pallas kernels, local(): call(remote_kernel, [array(devices * 2, LANE), array(18, frags)], [vmem(2...  1.56 us
  transfers between devices with their start and end apart: 1, of which 1 were waited for; matrix products, arithmetic and copies ran while one was open for 0% of the time, Pallas kernels for 12%

profile of v14, /device:TPU:0, one launch (start us, length us, event | category | flops | bytes accessed | tf_op | source)
XLA Modules:
  0.0 38.3 jit_solution(2094130100992828475)
XLA Ops:
  0.6 2.2 %shard_map.113 = f32[1056,128]{1,0:T(8,128)} custom-call(f32[3,256,128]{2,1,0:T(8,128)} %bitcast.13, f32[6,8]{1,0:T(8,128)} %refs_2_.1, f32[6,2,8]{2,1,0:T(2,128)} %bitcast.17, s32[1,256]{1,0:T(1,128)} %src_h.1, s32[256,128]{1,0:T(8,128)} %bitcast.16, s32[1,32]{1,0:T(1,128)} %counts_h.1), custom_call_target="tpu_custom_call" | custom-call | tf_op jit(solution)/shard_map/pallas_call | solution.py:559
  2.8 7.3 %all-to-all-start = ((f32[32,1,4224]{2,1,0:T(1,128)}), f32[32,1,4224]{2,1,0:T(1,128)S(1)}, u32[]{:S(2)}, u32[]{:S(2)}) async-start(f32[32,1,4224]{2,1,0:T(1,128)} %bitcast.12), calls=%async_computation | async-start | bytes 1081344 | tf_op jit(solution)/shard_map/all_to_all | solution.py:529
  10.1 4.4 %shard_map.114 = (f32[1536,128]{1,0:T(8,128)S(1)}, f32[16,256]{1,0:T(8,128)S(1)}, s32[1,256]{1,0:T(1,128)S(1)}, f32[18,8]{1,0:T(8,128)S(1)}, bf16[128,256]{1,0:T...) custom-call(f32[3,256,128]{2,1,0:T(8,128)} %bitcast.14, ...), custom_call_target="tpu_custom_call" | custom-call | flops 6553600 | bytes 4000000 | tf_op jit(solution)/shard_map/pallas_call | solution.py:582
  14.6 12.3 %all-to-all-done = f32[32,1,4224]{2,1,0:T(1,128)S(1)} async-done(((f32[32,1,4224]{2,1,0:T(1,128)}), f32[32,1,4224]{2,1,0:T(1,128)S(1)}, u32[]{:S(2)}, u32[]{:S(2)}) %all-to-all-start) | async-done | bytes 540704 | tf_op jit(solution)/shard_map/all_to_all | solution.py:529
  26.8 1.6 %shard_map.115 = (f32[64,128]{1,0:T(8,128)S(1)}, f32[18,8]{1,0:T(8,128)S(1)}) custom-call(f32[1056,128]{1,0:T(8,128)S(1)} %bitcast.9, f32[1536,128]{1,0:T(8,128)S(1)} %get-tuple-element.14.staged, f32[16,256]{1,0:T(8,128)S(1)} %get-tuple-element.15.remote_b, s32[1,256]{1,0:T(1,128)S(1)} %get-tuple-element.16.remote_frag, ...), custom_call_target="tpu_custom_call" | custom-call | tf_op jit(solution)/shard_map/pallas_call | solution.py:630
  28.4 9.3 %all_to_all.10 = f32[32,1,256]{2,1,0:T(1,128)S(1)} all-to-all(f32[32,1,256]{2,1,0:T(1,128)S(1)} %bitcast.11), channel_id=1, replica_groups=mesh['tile'=8,'band'=4] {'band','tile'}, dimensions={0} | all-to-all | bytes 65536 | tf_op jit(solution)/shard_map/all_to_all | solution.py:529
  37.7 0.7 %shard_map.116 = (f32[6,8]{1,0:T(8,128)}, f32[6,2,8]{2,1,0:T(2,128)}) custom-call(f32[64,128]{1,0:T(8,128)S(1)} %bitcast.10, f32[18,8]{1,0:T(8,128)S(1)} %get-tuple-element.23.totals), custom_call_target="tpu_custom_call" | custom-call | tf_op jit(solution)/shard_map/pallas_call | solution.py:645
Async XLA Ops:
  2.8 24.0 %all-to-all-start = ((f32[32,1,4224]{2,1,0:T(1,128)}), f32[32,1,4224]{2,1,0:T(1,128)S(1)}, u32[]{:S(2)}, u32[]{:S(2)}) async-start(f32[32,1,4224]{2,1,0:T(1,128)} %bitcast.12), calls=%async_computation | async-start | bytes 1081344 | tf_op jit(solution)/shard_map/all_to_all | solution.py:529

commit v15 on v14

--- a/solution.py
+++ b/solution.py
@@ -445,13 +445,17 @@
                     preferred_element_type=f32,
                 )
 
-            def add(half):
+            def add():
                 hit = frags[lanes, :] == jnp.broadcast_to(slot, (LANE, LANE))
-                part = jnp.where(hit, held["placed"][:, half * LANE : (half + 1) * LANE], 0.0)
-                for piece in halves_of(part):
-                    rows[half] = rows[half] + jnp.dot(
-                        mine[:, lanes], piece, preferred_element_type=f32
-                    )
+                part = [
+                    jnp.where(hit, held["placed"][:, half * LANE : (half + 1) * LANE], 0.0)
+                    for half in range(2)
+                ]
+                pieces = jnp.concatenate(halves_of(jnp.concatenate(part, axis=1)), axis=0)
+                twice = jnp.concatenate([mine[:, lanes]] * 2, axis=1)
+                sent = jnp.dot(twice, pieces, preferred_element_type=f32)
+                for half in range(2):
+                    rows[half] = rows[half] + sent[:, half * LANE : (half + 1) * LANE]
 
             def own_side():
                 frag = remote_frag[0:1, pl.ds(start + t, LANE)]
@@ -464,7 +468,7 @@
                 )
                 held["total"] = target_side(added[0:ROWS, :] + added[ROWS:, :])
 
-            return [scatter, functools.partial(add, 0), functools.partial(add, 1), own_side], held
+            return [scatter, add, own_side], held
 
         tiles = range(0, pairs, LANE)
         steps = front(tiles[0])

time: 38.6 us -> 38.5 us (level)
  no operation moved by 1% of the time
where the time goes in v15:
time: 38.5 us; the launch traced here: 38.3 us
  waiting for transfers between devices  12.3 us (32%)
  blocking collectives  9.28 us (24%)
  Pallas kernels  8.79 us (23%)
  starting transfers between devices  7.3 us (19%)
  between operations  0.66 us (2%)
    all_to_all x1, waiting for transfers between devices, exchange(): sent = lax.all_to_all(sent, ORDER, split_axis=0, concat_axis=0, tiled=True)  12.3 us
    all_to_all x1, blocking collectives, exchange(): sent = lax.all_to_all(sent, ORDER, split_axis=0, concat_axis=0, tiled=True)  9.28 us
    all_to_all x1, starting transfers between devices, exchange(): sent = lax.all_to_all(sent, ORDER, split_axis=0, concat_axis=0, tiled=True)  7.3 us
    pallas_call x1, Pallas kernels, local(): call(functools.partial(fetch_local, inputs=9, outputs=8, sizes=sizes), [a...  4.43 us
    pallas_call x1, Pallas kernels, local(): call(functools.partial(pack_kernel, sizes=sizes), [array(devices * MSG, L...  2.19 us
    pallas_call x1, Pallas kernels, local(): call(remote_kernel, [array(devices * 2, LANE), array(18, frags)], [vmem(2...  1.49 us
  transfers between devices with their start and end apart: 1, of which 1 were waited for; matrix products, arithmetic and copies ran while one was open for 0% of the time, Pallas kernels for 12%

profile of v15, /device:TPU:0, one launch (start us, length us, event | category | flops | bytes accessed | tf_op | source)
XLA Modules:
  0.0 38.3 jit_solution(5115277576288122388)
XLA Ops:
  0.6 2.2 %shard_map.113 = f32[1056,128]{1,0:T(8,128)} custom-call(f32[3,256,128]{2,1,0:T(8,128)} %bitcast.13, f32[6,8]{1,0:T(8,128)} %refs_2_.1, f32[6,2,8]{2,1,0:T(2,128)} %bitcast.17, s32[1,256]{1,0:T(1,128)} %src_h.1, s32[256,128]{1,0:T(8,128)} %bitcast.16, s32[1,32]{1,0:T(1,128)} %counts_h.1), custom_call_target="tpu_custom_call" | custom-call | tf_op jit(solution)/shard_map/pallas_call | solution.py:563
  2.8 7.3 %all-to-all-start = ((f32[32,1,4224]{2,1,0:T(1,128)}), f32[32,1,4224]{2,1,0:T(1,128)S(1)}, u32[]{:S(2)}, u32[]{:S(2)}) async-start(f32[32,1,4224]{2,1,0:T(1,128)} %bitcast.12), calls=%async_computation | async-start | bytes 1081344 | tf_op jit(solution)/shard_map/all_to_all | solution.py:533
  10.1 4.4 %shard_map.114 = (f32[1536,128]{1,0:T(8,128)S(1)}, f32[16,256]{1,0:T(8,128)S(1)}, s32[1,256]{1,0:T(1,128)S(1)}, f32[18,8]{1,0:T(8,128)S(1)}, bf16[128,256]{1,0:T...) custom-call(f32[3,256,128]{2,1,0:T(8,128)} %bitcast.14, ...), custom_call_target="tpu_custom_call" | custom-call | flops 6553600 | bytes 4000000 | tf_op jit(solution)/shard_map/pallas_call | solution.py:586
  14.6 12.3 %all-to-all-done = f32[32,1,4224]{2,1,0:T(1,128)S(1)} async-done(((f32[32,1,4224]{2,1,0:T(1,128)}), f32[32,1,4224]{2,1,0:T(1,128)S(1)}, u32[]{:S(2)}, u32[]{:S(2)}) %all-to-all-start) | async-done | bytes 540704 | tf_op jit(solution)/shard_map/all_to_all | solution.py:533
  26.8 1.5 %shard_map.115 = (f32[64,128]{1,0:T(8,128)S(1)}, f32[18,8]{1,0:T(8,128)S(1)}) custom-call(f32[1056,128]{1,0:T(8,128)S(1)} %bitcast.9, f32[1536,128]{1,0:T(8,128)S(1)} %get-tuple-element.14.staged, f32[16,256]{1,0:T(8,128)S(1)} %get-tuple-element.15.remote_b, s32[1,256]{1,0:T(1,128)S(1)} %get-tuple-element.16.remote_frag, ...), custom_call_target="tpu_custom_call" | custom-call | tf_op jit(solution)/shard_map/pallas_call | solution.py:634
  28.3 9.3 %all_to_all.10 = f32[32,1,256]{2,1,0:T(1,128)S(1)} all-to-all(f32[32,1,256]{2,1,0:T(1,128)S(1)} %bitcast.11), channel_id=1, replica_groups=mesh['tile'=8,'band'=4] {'band','tile'}, dimensions={0} | all-to-all | bytes 65536 | tf_op jit(solution)/shard_map/all_to_all | solution.py:533
  37.6 0.7 %shard_map.116 = (f32[6,8]{1,0:T(8,128)}, f32[6,2,8]{2,1,0:T(2,128)}) custom-call(f32[64,128]{1,0:T(8,128)S(1)} %bitcast.10, f32[18,8]{1,0:T(8,128)S(1)} %get-tuple-element.23.totals), custom_call_target="tpu_custom_call" | custom-call | tf_op jit(solution)/shard_map/pallas_call | solution.py:649
Async XLA Ops:
  2.8 24.0 %all-to-all-start = ((f32[32,1,4224]{2,1,0:T(1,128)}), f32[32,1,4224]{2,1,0:T(1,128)S(1)}, u32[]{:S(2)}, u32[]{:S(2)}) async-start(f32[32,1,4224]{2,1,0:T(1,128)} %bitcast.12), calls=%async_computation | async-start | bytes 1081344 | tf_op jit(solution)/shard_map/all_to_all | solution.py:533
